TPU v7x, 128 devices: a whole 4x4x4 slice. The times are simulated.
128 devices in a mesh: seq: 32 (over z, x, core), section: 4 (over y).
Axes of the slice: x: 4, y: 4, z: 4, core: 2. Of those that a mesh axis runs over, the one named last changes fastest.
Arguments:
- layer_in: bfloat16 [4, 8192, 3072], P('section', 'seq'), may hold values from -6 to 6
- norm_gain: float32 [4, 3072], P('section'), may hold values from 0.1 to 1.9
- conv_weight: float32 [4, 3, 3072], P('section'), may hold values from -3.5 to 3.5
- query_weight: bfloat16 [4, 3072, 384], P('section'), may hold values from -0.109375 to 0.109375
- key_weight: bfloat16 [4, 3072, 384], P('section'), may hold values from -0.109375 to 0.109375
- out_gain: float32 [4, 3072], P('section'), may hold values from 0.1 to 1.9
- layer_grad: bfloat16 [4, 8192, 3072], P('section', 'seq'), may hold values from -6 to 6
Outputs:
- next_input: bfloat16 [4, 8192, 3072], P('section', 'seq')
- prev_grad: bfloat16 [4, 8192, 3072], P('section', 'seq')
All inputs are finite; a program needn't handle non-finite values.
Results may differ from a plain program's by a relative error of at most 0.03.
Values may be sent and summed in bfloat16 or wider, within the bound.
No kernel may reach another device: no remote copies, remote signals or barrier semaphores. Data moves between devices by JAX's collectives and lax.ppermute only.
A program may use at most 192 MiB of HBM per device.

v0:
```python
import math

import jax
import jax.numpy as jnp
import numpy as np
from jax import lax
from jax.sharding import PartitionSpec as P

HEADS = 24
FEAT = 16
VDIM = 128


EPSILON = 1e-06


def carried_in(part, axis, combine, identity, reverse):
    count = lax.axis_size(axis)
    place = lax.axis_index(axis)
    ahead = count - 1 - place if reverse else place
    gathered = lax.all_gather(part, axis)
    state = jnp.zeros_like(part) + jnp.asarray(identity, part.dtype)

    def one(lap, state):
        source = count - 1 - lap if reverse else lap
        return combine(state, lax.dynamic_index_in_dim(gathered, source, 0, False))

    return lax.fori_loop(0, ahead, one, state)


def passed_along(block, axis, distance):
    devices = range(lax.axis_size(axis))
    route = [(i - distance, i) for i in devices if i - distance in devices]
    return lax.ppermute(block, axis, route)


def shifted(block, axis, distance):
    devices = range(lax.axis_size(axis))
    route = [((i - distance) % len(devices), i) for i in devices]
    return lax.ppermute(block, axis, route)


def taylor_map(columns):
    feat_count = columns.shape[1]
    products = columns[:, :, None, :] * columns[:, None, :, :]
    products = products.reshape(columns.shape[0], feat_count * feat_count, columns.shape[2])
    constant = jnp.ones((columns.shape[0], 1, columns.shape[2]), jnp.float32)
    pieces = [
        constant,
        columns * feat_count ** (-0.25),
        products * (1.0 / math.sqrt(2.0 * feat_count)),
    ]
    return jnp.concatenate(pieces, axis=1).astype(jnp.bfloat16)


def taylor_back(columns, grad_feat):
    feat_count = columns.shape[1]
    linear_part = grad_feat[:, 1 : 1 + feat_count, :]
    square_part = grad_feat[:, 1 + feat_count :, :].reshape(
        grad_feat.shape[0], feat_count, feat_count, grad_feat.shape[2]
    )
    symmetric = square_part + jnp.swapaxes(square_part, 1, 2)
    mixed_term = jnp.einsum("habk,hbk->hak", symmetric, columns, precision=lax.Precision.HIGHEST)
    return linear_part * feat_count ** (-0.25) + mixed_term * (1.0 / math.sqrt(2.0 * feat_count))


def pack_tables(feat_count):
    kept_rows = list(range(1 + feat_count))
    where_pair = {}
    for row_a in range(feat_count):
        for row_b in range(row_a, feat_count):
            where_pair[row_a, row_b] = len(kept_rows)
            kept_rows.append(1 + feat_count + row_a * feat_count + row_b)
    spread_rows = list(range(1 + feat_count))
    for row_a in range(feat_count):
        for row_b in range(feat_count):
            spread_rows.append(where_pair[min(row_a, row_b), max(row_a, row_b)])
    return (np.array(kept_rows, np.int32), np.array(spread_rows, np.int32))


def add_states(earlier_term, later_term):
    return (earlier_term.astype(jnp.float32) + later_term.astype(jnp.float32)).astype(jnp.bfloat16)


def scan_states(state_half, reverse):
    kept_rows, spread_rows = pack_tables(FEAT)
    packed = jnp.take(state_half, kept_rows, axis=1)
    packed = carried_in(packed, "seq", add_states, jnp.zeros_like(packed), reverse)
    return jnp.take(packed, spread_rows, axis=1)


def neighbour_rows(edge_vals, offset):
    return passed_along(edge_vals, "seq", offset)


def section_pass(tensor_half, offset):
    return shifted(tensor_half, "section", offset)


def attention_weights(query_r, key_r, mask_rows):
    scores = jnp.einsum("bhf,chf->hbc", query_r, key_r, preferred_element_type=jnp.float32) * (
        1.0 / math.sqrt(FEAT)
    )
    weights = jnp.where(mask_rows, 1.0 + scores + 0.5 * scores * scores, 0.0).astype(jnp.bfloat16)
    return (scores, weights)


def forward_layer(hidden, norm_scale, conv_taps, query_proj, key_proj, out_scale, mask_rows):
    rows_here = hidden.shape[0]
    width_all = hidden.shape[1]
    hidden_f = hidden.astype(jnp.float32)
    inv_rms = lax.rsqrt(jnp.mean(hidden_f * hidden_f, axis=1, keepdims=True) + EPSILON)
    normed = (hidden_f * inv_rms * norm_scale).astype(jnp.bfloat16)
    before = neighbour_rows(normed[-2:].astype(jnp.float32), 1)
    padded = jnp.concatenate([before, normed.astype(jnp.float32)], axis=0)
    values = (
        conv_taps[0] * padded[:-2] + conv_taps[1] * padded[1:-1] + conv_taps[2] * padded[2:]
    ).astype(jnp.bfloat16)
    queries = jnp.dot(normed, query_proj, preferred_element_type=jnp.float32).astype(jnp.bfloat16)
    keys_half = jnp.dot(normed, key_proj, preferred_element_type=jnp.float32).astype(jnp.bfloat16)
    query_r = queries.reshape(rows_here, HEADS, FEAT)
    key_r = keys_half.reshape(rows_here, HEADS, FEAT)
    value_r = values.reshape(rows_here, HEADS, VDIM)
    query_feat = taylor_map(jnp.transpose(query_r.astype(jnp.float32), (1, 2, 0)))
    key_feat = taylor_map(jnp.transpose(key_r.astype(jnp.float32), (1, 2, 0)))
    scores, weights = attention_weights(query_r, key_r, mask_rows)
    inside = jnp.einsum("hbc,chv->bhv", weights, value_r, preferred_element_type=jnp.float32)
    key_state = jnp.einsum(
        "htb,bhv->htv", key_feat, value_r, preferred_element_type=jnp.float32
    ).astype(jnp.bfloat16)
    prefix = scan_states(key_state, False)
    across = jnp.einsum("htb,htv->bhv", query_feat, prefix, preferred_element_type=jnp.float32)
    numerator = inside + across
    head_rms = lax.rsqrt(jnp.mean(numerator * numerator, axis=2, keepdims=True) + EPSILON)
    output = (hidden_f + out_scale * (numerator * head_rms).reshape(rows_here, width_all)).astype(
        jnp.bfloat16
    )
    kept_scores = (scores, weights)
    stored = (
        hidden_f,
        inv_rms,
        normed,
        query_r,
        key_r,
        value_r,
        query_feat,
        key_feat,
        kept_scores,
        prefix,
        numerator,
        head_rms,
    )
    return (output, stored)


def backward_layer(
    grad_in, stored, norm_scale, conv_taps, query_proj, key_proj, out_scale, mask_rows
):
    (
        hidden_f,
        inv_rms,
        normed,
        query_r,
        key_r,
        value_r,
        query_feat,
        key_feat,
        kept_scores,
        prefix,
        numerator,
        head_rms,
    ) = stored
    scores, weights = kept_scores
    rows_here = hidden_f.shape[0]
    width_all = hidden_f.shape[1]
    score_scale = 1.0 / math.sqrt(FEAT)
    grad_f = grad_in.astype(jnp.float32)
    grad_head = (grad_f * out_scale).reshape(rows_here, HEADS, VDIM)
    grad_numer = head_rms * grad_head - numerator * (head_rms * head_rms * head_rms) * jnp.mean(
        grad_head * numerator, axis=2, keepdims=True
    )
    grad_numer_half = grad_numer.astype(jnp.bfloat16)
    grad_weights = jnp.einsum(
        "bhv,chv->hbc", grad_numer_half, value_r, preferred_element_type=jnp.float32
    )
    grad_scores = jnp.where(mask_rows, grad_weights * (1.0 + scores), 0.0).astype(jnp.bfloat16)
    grad_query_in = (
        jnp.einsum("hbc,chf->bhf", grad_scores, key_r, preferred_element_type=jnp.float32)
        * score_scale
    )
    grad_key_in = (
        jnp.einsum("hbc,bhf->chf", grad_scores, query_r, preferred_element_type=jnp.float32)
        * score_scale
    )
    grad_value_in = jnp.einsum(
        "hbc,bhv->chv", weights, grad_numer_half, preferred_element_type=jnp.float32
    )
    query_cols = jnp.transpose(query_r.astype(jnp.float32), (1, 2, 0))
    key_cols = jnp.transpose(key_r.astype(jnp.float32), (1, 2, 0))
    grad_query_feat = jnp.einsum(
        "bhv,htv->htb", grad_numer_half, prefix, preferred_element_type=jnp.float32
    )
    grad_prefix = jnp.einsum(
        "htb,bhv->htv", query_feat, grad_numer_half, preferred_element_type=jnp.float32
    ).astype(jnp.bfloat16)
    grad_state = scan_states(grad_prefix, True)
    grad_key_feat = jnp.einsum(
        "bhv,htv->htb", value_r, grad_state, preferred_element_type=jnp.float32
    )
    grad_value_out = jnp.einsum(
        "htb,htv->bhv", key_feat, grad_state, preferred_element_type=jnp.float32
    )
    grad_values = (grad_value_in + grad_value_out).reshape(rows_here, width_all)
    grad_query = grad_query_in + jnp.transpose(taylor_back(query_cols, grad_query_feat), (2, 0, 1))
    grad_key = grad_key_in + jnp.transpose(taylor_back(key_cols, grad_key_feat), (2, 0, 1))
    grad_query_half = grad_query.reshape(rows_here, HEADS * FEAT).astype(jnp.bfloat16)
    grad_key_half = grad_key.reshape(rows_here, HEADS * FEAT).astype(jnp.bfloat16)
    contract_rows = (((1,), (1,)), ((), ()))
    grad_normed = lax.dot_general(
        grad_query_half, query_proj, contract_rows, preferred_element_type=jnp.float32
    )
    grad_normed = grad_normed + lax.dot_general(
        grad_key_half, key_proj, contract_rows, preferred_element_type=jnp.float32
    )
    after_rows = neighbour_rows(grad_values[:2], -1)
    padded = jnp.concatenate([grad_values, after_rows], axis=0)
    grad_normed = grad_normed + (
        conv_taps[2] * padded[:-2] + conv_taps[1] * padded[1:-1] + conv_taps[0] * padded[2:]
    )
    grad_scaled = grad_normed * norm_scale
    grad_hidden = inv_rms * grad_scaled - hidden_f * (inv_rms * inv_rms * inv_rms) * jnp.mean(
        hidden_f * grad_scaled, axis=1, keepdims=True
    )
    return (grad_f + grad_hidden).astype(jnp.bfloat16)


def local(layer_in, norm_gain, conv_weight, query_weight, key_weight, out_gain, layer_grad):
    norm_scale = norm_gain[0]
    conv_taps = conv_weight[0]
    query_proj = query_weight[0]
    key_proj = key_weight[0]
    out_scale = out_gain[0]
    hidden = layer_in[0]
    rows_here = hidden.shape[0]
    position = jnp.arange(rows_here)
    mask_rows = position[:, None] >= position[None, :]
    output, stored = forward_layer(
        hidden, norm_scale, conv_taps, query_proj, key_proj, out_scale, mask_rows
    )
    sent_forward = section_pass(output, 1)
    grad_out = backward_layer(
        layer_grad[0], stored, norm_scale, conv_taps, query_proj, key_proj, out_scale, mask_rows
    )
    sent_backward = section_pass(grad_out, -1)
    return (sent_forward[None], sent_backward[None])


def solution(mesh):
    return jax.shard_map(
        local,
        mesh=mesh,
        in_specs=(
            P("section", "seq", None),
            P("section", None),
            P("section", None, None),
            P("section", None, None),
            P("section", None, None),
            P("section", None),
            P("section", "seq", None),
        ),
        out_specs=(P("section", "seq", None), P("section", "seq", None)),
        check_vma=False,
    )
```

profile of v0, /device:TPU:1, one launch (start us, length us, event | category | flops | bytes accessed | tf_op | source)
XLA Modules:
  0.0 490.4 jit_solution(15663873519284924083)
XLA Ops:
  9.8 3.8 fusion.95
  13.6 4.5 collective-permute-start
  25.5 3.2 gather_fusion
  28.8 3.2 fusion.77
  39.2 3.7 fusion.98
  42.9 104.4 %all-gather.5.cloned.1.call-done = bf16[768,153,128]{2,0,1:T(8,128)(2,1)} async-done(((bf16[24,153,128]{2,0,1:T(8,128)(2,1)}), bf16[768,153,128]{2,0,1:T(8,128)(2,1)}) %all-gather.5.cloned.1.call-update) | async-done | bytes 30081040 | tf_op jit(solution)/shard_map/all_gather | solution.py:21
  150.7 3.5 gather_fusion.1
  154.3 4.2 fusion.52
  158.5 4.2 fusion.41
  168.2 3.4 gather_fusion.2
  175.5 3.8 slice.74
  180.2 4.0 copy.40
  184.2 11.6 %fusion.7 = f32[24,256,16]{1,2,0:T(8,128)S(1)} fusion(f32[24,16,16,256]{3,2,1,0:T(8,128)} %bitcast.187, f32[24,256,16]{1,2,0:T(8,128)S(1)} %convert.29), kind=kLoop, calls=%fused_computation.19 | loop fusion | flops 4620288 | bytes 7077888 | tf_op jit(solution)/shard_map/habk,hbk->hak/dot_general | solution.py:63
  195.9 4.4 select_convert_fusion
  206.8 132.9 %all-gather.7.cloned.1.call-done = bf16[768,153,128]{2,0,1:T(8,128)(2,1)} async-done(((bf16[24,153,128]{2,0,1:T(8,128)(2,1)}), bf16[768,153,128]{2,0,1:T(8,128)(2,1)}) %all-gather.7.cloned.1.call-update) | async-done | bytes 30081040 | tf_op jit(solution)/shard_map/all_gather | solution.py:21
  339.8 52.3 %while.23 = (s32[]{:T(128)}, bf16[24,153,128]{2,1,0:T(8,128)(2,1)S(1)}, s32[]{:T(128)}, bf16[32,24,153,128]{3,1,0,2:T(8,128)(2,1)}, s32[]{:T(128)}, /*index=5*/s32[]{:T(128)}, s32[]{:T(128)}, s32[]{:T(128)}) while((s32[]{:T(128)}, bf16[24,153,128]{2,1,0:T(8,128)(2,1)S(1)}, s32[]{:T(128)}, bf16[32,24,153,128]{3,1,0,2:T(8,128)(2,1)}, s32[]{:T(128)}, ...), condition=%wide.region_6.9_spmd, body=%wide.region_5.8_spmd.sunk | while | flops 1880070 | bytes 4700295 | solution.py:28
  393.5 3.5 gather_fusion.3
  397.0 3.2 fusion.63
  403.8 3.5 slice.76
  414.2 3.9 collective-permute-start.2
  418.2 11.7 %fusion.4 = f32[24,256,16]{1,2,0:T(8,128)S(1)} fusion(f32[24,16,16,256]{3,2,1,0:T(8,128)} %bitcast.186, f32[24,256,16]{1,2,0:T(8,128)S(1)} %copy-done.25), kind=kLoop, calls=%fused_computation.15 | loop fusion | flops 4620288 | bytes 7077888 | tf_op jit(solution)/shard_map/habk,hbk->hak/dot_general | solution.py:63
  431.5 3.5 copy.76
  435.2 6.5 %fusion.32 = (f32[256]{0:T(256)S(1)}, f32[256,3072]{1,0:T(8,128)S(1)}) fusion(bf16[1,256,3072]{2,1,0:T(8,128)(2,1)} %param.19, f32[3072]{0:T(1024)S(1)} %bitcast.232, f32[2,3072]{1,0:T(2,128)S(1)} %collective-permute-done.2, f32[256,3072]{1,0:T(8,128)} %copy.76, f32[3072]{0:T(1024)S(1)} %bitcast.224, f32[3072]{0:T(1024)S(1)} %bitcast.228, ...), kind=kOutput, calls=%fused_computation.57 | convolution fusion | flops 614203136 | bytes 13640704 | tf_op jit(solution)/shard_map/dot_general | solution.py:222
  446.3 34.6 %collective-permute-done.1 = bf16[256,3072]{1,0:T(8,128)(2,1)S(1)} collective-permute-done((bf16[256,3072]{1,0:T(8,128)(2,1)S(1)}, bf16[256,3072]{1,0:T(8,128)(2,1)S(1)}, u32[]{:S(2)}, u32[]{:S(2)}) %collective-permute-start.1) | collective-permute-done | bytes 1572896 | tf_op jit(solution)/shard_map/ppermute | solution.py:40
  (222 shorter events, 111.0 us)
Async XLA Ops:
  7.2 10.9 %copy-start = (bf16[1,3072,384]{2,1,0:T(8,128)(2,1)S(1)}, bf16[1,3072,384]{2,1,0:T(8,128)(2,1)}, u32[]{:S(2)}) copy-start(bf16[1,3072,384]{2,1,0:T(8,128)(2,1)} %param.23) | copy-start | bytes 7077892
  7.2 140.2 %all-gather.5.cloned.1.call-start = ((), (), s32[]{:S(2)}) async-start(), calls=%async_computation | async-start | bytes 31021056 | tf_op jit(solution)/shard_map/all_gather | solution.py:21
  9.8 19.0 %copy-start.43 = (f32[256]{0:T(256)}, f32[256]{0:T(256)S(1)}, u32[]{:S(2)}) copy-start(f32[256]{0:T(256)S(1)} %get-tuple-element.123) | copy-start | bytes 3076
  9.8 8.3 %copy-start.12 = (bf16[1,256,3072]{2,1,0:T(8,128)(2,1)S(1)}, bf16[1,256,3072]{2,1,0:T(8,128)(2,1)}, u32[]{:S(2)}) copy-start(bf16[1,256,3072]{2,1,0:T(8,128)(2,1)} %param.19) | copy-start | bytes 4718596
  9.8 8.3 %copy-start.40 = (f32[1,3072]{1,0:T(1,128)S(1)}, f32[1,3072]{1,0:T(1,128)}, u32[]{:S(2)}) copy-start(f32[1,3072]{1,0:T(1,128)} %param.20) | copy-start | bytes 36868
  13.6 5.9 %copy-start.39 = (f32[1,3,3072]{2,0,1:T(1,128)S(1)}, f32[1,3,3072]{2,0,1:T(1,128)}, u32[]{:S(2)}) copy-start(f32[1,3,3072]{2,0,1:T(1,128)} %param.21) | copy-start | bytes 110596
  13.6 6.9 %collective-permute-start = (f32[2,3072]{1,0:T(2,128)S(1)}, f32[2,3072]{1,0:T(2,128)S(1)}, u32[]{:S(2)}, u32[]{:S(2)}) collective-permute-start(f32[2,3072]{1,0:T(2,128)S(1)} %slice_convert_fusion), channel_id=1, source_target_pairs={{0,4},{4,8},{8,12},{12,16},{16,20},{20,24},{24,28},{28,32},{32,36}... | collective-permute-start | bytes 73736 | tf_op jit(solution)/shard_map/ppermute | solution.py:34
  19.4 19.9 %copy-start.17 = (bf16[256,384]{0,1:T(8,128)(2,1)}, bf16[256,384]{0,1:T(8,128)(2,1)S(1)}, u32[]{:S(2)}) copy-start(bf16[256,384]{0,1:T(8,128)(2,1)S(1)} %copy.33) | copy-start | bytes 589828
  20.5 5.0 %copy-start.42 = (s32[1024]{0:T(1024)}, s32[1024]{0:T(1024)S(1)}, u32[]{:S(2)}) copy-start(s32[1024]{0:T(1024)S(1)} %pad_clamp_fusion.1) | copy-start | bytes 12292
  28.7 310.9 %all-gather.7.cloned.1.call-start = ((), (), s32[]{:S(2)}) async-start(), calls=%async_computation.1 | async-start | bytes 31021056 | tf_op jit(solution)/shard_map/all_gather | solution.py:21
  184.2 11.7 %copy-start.6 = (bf16[256,24,128]{0,2,1:T(8,128)(2,1)S(1)}, bf16[256,24,128]{0,2,1:T(8,128)(2,1)}, u32[]{:S(2)}) copy-start(bf16[256,24,128]{0,2,1:T(8,128)(2,1)} %copy-done.5) | copy-start | bytes 4718596
  184.2 11.7 %copy-start.11 = (bf16[32,24,8,128]{3,2,1,0:T(8,128)(2,1)S(1)}, bf16[32,24,8,128]{3,2,1,0:T(8,128)(2,1)}, u32[]{:S(2)}) copy-start(bf16[32,24,8,128]{3,2,1,0:T(8,128)(2,1)} %copy-done.9) | copy-start | bytes 4718596
  184.2 11.7 %copy-start.27 = (pred[256,256]{1,0:T(8,128)(4,1)S(1)}, pred[256,256]{1,0:T(8,128)(4,1)}, u32[]{:S(2)}) copy-start(pred[256,256]{1,0:T(8,128)(4,1)} %iota_compare_fusion) | copy-start | bytes 196612
  400.3 7.0 %slice-start = ((s8[6291456]{0:T(1024)(128)(4,1)}), s8[4194304]{0:T(1024)(128)(4,1)S(1)}, s32[]{:S(2)}) async-start(s8[6291456]{0:T(1024)(128)(4,1)} %bitcast.184), calls=%async_computation.2 | async-start | bytes 8388608
  409.5 8.7 %copy-start.25 = (f32[24,256,16]{1,2,0:T(8,128)S(1)}, f32[24,256,16]{1,2,0:T(8,128)}, u32[]{:S(2)}) copy-start(f32[24,256,16]{1,2,0:T(8,128)} %convert.30) | copy-start | bytes 1179652
  414.2 20.8 %collective-permute-start.2 = (f32[2,3072]{1,0:T(2,128)S(1)}, f32[2,3072]{1,0:T(2,128)S(1)}, u32[]{:S(2)}, u32[]{:S(2)}) collective-permute-start(f32[2,3072]{1,0:T(2,128)S(1)} %copy.77), channel_id=1, source_target_pairs={{4,0},{8,4},{12,8},{16,12},{20,16},{24,20},{28,24},{32,28},{36,32}... | collective-permute-start | bytes 73736 | tf_op jit(solution)/shard_map/ppermute | solution.py:34
  418.2 11.7 %copy-start.2 = (bf16[24,256,256]{2,1,0:T(8,128)(2,1)S(1)}, bf16[24,256,256]{2,1,0:T(8,128)(2,1)}, u32[]{:S(2)}) copy-start(bf16[24,256,256]{2,1,0:T(8,128)(2,1)} %copy-done.1) | copy-start | bytes 9437188
  435.1 6.6 %copy-start.13 = (bf16[1,256,3072]{2,1,0:T(8,128)(2,1)S(1)}, bf16[1,256,3072]{2,1,0:T(8,128)(2,1)}, u32[]{:S(2)}) copy-start(bf16[1,256,3072]{2,1,0:T(8,128)(2,1)} %param.19) | copy-start | bytes 4718596
  435.1 6.6 %copy-start.14 = (f32[256,3072]{1,0:T(8,128)S(1)}, f32[256,3072]{1,0:T(8,128)}, u32[]{:S(2)}) copy-start(f32[256,3072]{1,0:T(8,128)} %copy.40) | copy-start | bytes 9437188
  435.1 6.9 %copy-start.20 = (bf16[1,256,3072]{2,1,0:T(8,128)(2,1)S(1)}, bf16[1,256,3072]{2,1,0:T(8,128)(2,1)}, u32[]{:S(2)}) copy-start(bf16[1,256,3072]{2,1,0:T(8,128)(2,1)} %param.25) | copy-start | bytes 4718596
  435.1 6.9 %copy-start.44 = (f32[256]{0:T(256)S(1)}, f32[256]{0:T(256)}, u32[]{:S(2)}) copy-start(f32[256]{0:T(256)} %copy-done.43) | copy-start | bytes 3076
  435.1 6.9 %copy-start.45 = (f32[256]{0:T(256)S(1)}, f32[256]{0:T(256)}, u32[]{:S(2)}) copy-start(f32[256]{0:T(256)} %get-tuple-element.122) | copy-start | bytes 3076
  443.6 37.4 %collective-permute-start.1 = (bf16[256,3072]{1,0:T(8,128)(2,1)S(1)}, bf16[256,3072]{1,0:T(8,128)(2,1)S(1)}, u32[]{:S(2)}, u32[]{:S(2)}) collective-permute-start(bf16[256,3072]{1,0:T(8,128)(2,1)S(1)} %get-tuple-element.116), channel_id=1, source_target_pairs={{3,0},{0,1},{1,2},{2,3},{7,4},{4,5},{5,6},{6,7},{11,8},{8,9},{9,10... | collective-permute-start | bytes 4718600 | tf_op jit(solution)/shard_map/ppermute | solution.py:40
  444.8 36.3 %collective-permute-start.3 = (bf16[256,3072]{1,0:T(8,128)(2,1)S(1)}, bf16[256,3072]{1,0:T(8,128)(2,1)S(1)}, u32[]{:S(2)}, u32[]{:S(2)}) collective-permute-start(bf16[256,3072]{1,0:T(8,128)(2,1)S(1)} %get-tuple-element.115), channel_id=1, source_target_pairs={{1,0},{2,1},{3,2},{0,3},{5,4},{6,5},{7,6},{4,7},{9,8},{10,9},{11,1... | collective-permute-start | bytes 4718600 | tf_op jit(solution)/shard_map/ppermute | solution.py:40
  (35 other events, 112.8 us)
Sparse Core Ops, SparseCore 0:
  28.8 118.4 all-gather.4
  171.8 167.8 all-gather.6
where the time goes:
time: 500 us; the launch traced here: 490 us
  waiting for transfers between devices  272 us (54%)
  local copies, waits for them, and re-layouts  94.3 us (19%)
  other arithmetic  50.6 us (10%)
  matrix products  45.9 us (9%)
  between operations  15 us (3%)
  starting transfers between devices  11.2 us (2%)
    all_gather x2, waiting for transfers between devices, carried_in(): gathered = lax.all_gather(part, axis)  237 us
    dynamic_slice x31, local copies, waits for them, and re-layouts, one(): return combine(state, lax.dynamic_index_in_dim(gathered, source, 0, False))  42.7 us
    ppermute x2, waiting for transfers between devices, shifted(): return lax.ppermute(block, axis, route)  34.8 us
    dot_general x2, other arithmetic, taylor_back(): jnp.einsum('habk,hbk->hak', symmetric, columns, precision=lax.Precision.H...  23.3 us
    unnamed x108, local copies, waits for them, and re-layouts  10.9 us
    convert_element_type x31, other arithmetic, add_states(): (earlier_term.astype(jnp.float32) + later_term.astype(jnp.float32)).astyp...  10.3 us
  transfers between devices with their start and end apart: 6, of which 4 were waited for; matrix products, arithmetic and copies ran while one was open for 13% of the time, Pallas kernels for 0%

commit v1 on v0

v1 whole, which is shorter than its diff:
```python
import functools
import math

import jax
import jax.numpy as jnp
from jax import lax
from jax.experimental import pallas as pl
from jax.experimental.pallas import tpu as pltpu
from jax.sharding import PartitionSpec as P

HEADS = 24
FEAT = 16
VDIM = 128
PACKED = 160
GROUPS = 3
GROUP_HEADS = HEADS // GROUPS
STEP_HEADS = 4
STEPS = GROUP_HEADS // STEP_HEADS
CHIPS = 16

EPSILON = 1e-06
SCORE_SCALE = 1.0 / math.sqrt(FEAT)
LINEAR_SCALE = FEAT ** (-0.25)
PAIR_SCALE = 1.0 / math.sqrt(2.0 * FEAT)

f32 = jnp.float32
bf16 = jnp.bfloat16


def dot(a, b, contract):
    return lax.dot_general(a, b, (contract, ((), ())), preferred_element_type=f32)


def kernel_params(limit_mib=40):
    return pltpu.CompilerParams(vmem_limit_bytes=limit_mib << 20)


def cost(flops, moved):
    return pl.CostEstimate(flops=flops, bytes_accessed=moved, transcendentals=0)


def rolled(block, distance):
    return pltpu.roll(block, distance % block.shape[0], 0)


def taylor_rows(cols, pair_weight):
    pieces = []
    for distance in range(FEAT // 2 + 1):
        if distance == 0:
            product = cols * cols * PAIR_SCALE
        else:
            product = cols * rolled(cols, -distance) * (PAIR_SCALE * pair_weight)
        pieces.append(product if distance < FEAT // 2 else product[: FEAT // 2])
    row = lax.broadcasted_iota(jnp.int32, (FEAT // 2, cols.shape[1]), 0)
    pieces.append(jnp.where(row == 0, 1.0, 0.0).astype(f32))
    pieces.append(cols * LINEAR_SCALE)
    return jnp.concatenate(pieces, axis=0).astype(bf16)


def taylor_back(cols, grad_rows, pair_weight):
    mixed = 2.0 * grad_rows[:FEAT] * cols
    for distance in range(1, FEAT // 2):
        part = grad_rows[FEAT * distance : FEAT * (distance + 1)]
        term = part * rolled(cols, -distance) + rolled(part * cols, distance)
        mixed = mixed + (term if pair_weight == 1.0 else pair_weight * term)
    half = FEAT // 2
    last = grad_rows[FEAT * half : FEAT * half + half]
    term = jnp.concatenate([last * cols[half:], last * cols[:half]], axis=0)
    mixed = mixed + (term if pair_weight == 1.0 else pair_weight * term)
    return grad_rows[PACKED - FEAT :] * LINEAR_SCALE + mixed * PAIR_SCALE


def project_kernel(x_ref, gain_ref, query_ref, key_ref, normed_ref, query_cols_ref, key_cols_ref):
    @pl.when(pl.program_id(0) == 0)
    def _():
        x = x_ref[...].astype(f32)
        inv_rms = lax.rsqrt(jnp.mean(x * x, axis=1, keepdims=True) + EPSILON)
        normed_ref[...] = (x * inv_rms * gain_ref[...]).astype(bf16)

    normed = normed_ref[...]
    query = dot(normed, query_ref[...], ((1,), (0,)))
    key = dot(normed, key_ref[...], ((1,), (0,)))
    query_cols_ref[...] = query.T.astype(bf16)
    key_cols_ref[...] = key.T.astype(bf16)


def project(x, gain, query_proj, key_proj):
    rows, width = x.shape
    cols = query_proj.shape[1]
    whole = lambda j: (0, 0)
    return pl.pallas_call(
        project_kernel,
        grid=(cols // 128,),
        in_specs=[
            pl.BlockSpec((rows, width), whole),
            pl.BlockSpec((1, width), whole),
            pl.BlockSpec((width, 128), lambda j: (0, j)),
            pl.BlockSpec((width, 128), lambda j: (0, j)),
        ],
        out_specs=[
            pl.BlockSpec((rows, width), whole),
            pl.BlockSpec((128, rows), lambda j: (j, 0)),
            pl.BlockSpec((128, rows), lambda j: (j, 0)),
        ],
        out_shape=[
            jax.ShapeDtypeStruct((rows, width), bf16),
            jax.ShapeDtypeStruct((cols, rows), bf16),
            jax.ShapeDtypeStruct((cols, rows), bf16),
        ],
        compiler_params=kernel_params(),
        cost_estimate=cost(4 * rows * width * cols, 8 << 20),
        name="project",
    )(x, gain, query_proj, key_proj)


def head_of(index, size):
    return slice(index * size, (index + 1) * size)


def state_kernel(normed_ref, before_ref, taps_ref, key_ref, values_ref, state_ref):
    normed = normed_ref[...].astype(f32)
    before = before_ref[...].astype(f32)
    row = lax.broadcasted_iota(jnp.int32, normed.shape, 0)
    one_back = jnp.where(row == 0, before[1:2], rolled(normed, 1))
    two_back = jnp.where(row == 0, before[0:1], rolled(one_back, 1))
    values = (taps_ref[0:1] * two_back + taps_ref[1:2] * one_back + taps_ref[2:3] * normed).astype(bf16)
    values_ref[...] = values
    for head in range(STEP_HEADS):
        feat = taylor_rows(key_ref[head_of(head, FEAT)].astype(f32), 1.0)
        state = dot(feat, values[:, head_of(head, VDIM)], ((1,), (0,)))
        state_ref[head_of(head, PACKED)] = state.astype(bf16)


def inside_kernel(query_ref, key_ref, values_ref, inside_ref):
    rows = query_ref.shape[1]
    token = lax.broadcasted_iota(jnp.int32, (rows, rows), 0)
    other = lax.broadcasted_iota(jnp.int32, (rows, rows), 1)
    for head in range(STEP_HEADS):
        query = query_ref[head_of(head, FEAT)]
        key = key_ref[head_of(head, FEAT)]
        scores = dot(query, key, ((0,), (0,))) * SCORE_SCALE
        weights = jnp.where(token >= other, 1.0 + scores + 0.5 * scores * scores, 0.0).astype(bf16)
        lanes = head_of(head, VDIM)
        inside_ref[:, lanes] = dot(weights, values_ref[:, lanes], ((1,), (0,)))


def output_kernel(query_ref, inside_ref, prefix_ref, x_ref, grad_ref, scale_ref, out_ref, numer_ref, grad_state_ref):
    for head in range(STEP_HEADS):
        lanes = head_of(head, VDIM)
        feat = taylor_rows(query_ref[head_of(head, FEAT)].astype(f32), 2.0)
        across = dot(feat, prefix_ref[head_of(head, PACKED)], ((0,), (0,)))
        numer = inside_ref[:, lanes] + across
        inv = lax.rsqrt(jnp.mean(numer * numer, axis=1, keepdims=True) + EPSILON)
        scale = scale_ref[:, lanes]
        out_ref[:, lanes] = (x_ref[:, lanes].astype(f32) + scale * (numer * inv)).astype(bf16)
        grad = grad_ref[:, lanes].astype(f32) * scale
        mean = jnp.mean(grad * numer, axis=1, keepdims=True)
        grad_numer = (inv * grad - numer * (inv * inv * inv * mean)).astype(bf16)
        numer_ref[:, lanes] = grad_numer
        grad_state_ref[head_of(head, PACKED)] = dot(feat, grad_numer, ((1,), (0,))).astype(bf16)


def inside_back_kernel(
    query_ref, key_ref, values_ref, numer_ref, prefix_ref, grad_query_ref, grad_key_ref, grad_values_ref
):
    rows = query_ref.shape[1]
    token = lax.broadcasted_iota(jnp.int32, (rows, rows), 0)
    other = lax.broadcasted_iota(jnp.int32, (rows, rows), 1)
    for head in range(STEP_HEADS):
        lanes = head_of(head, VDIM)
        query = query_ref[head_of(head, FEAT)]
        key = key_ref[head_of(head, FEAT)]
        grad_numer = numer_ref[:, lanes]
        values = values_ref[:, lanes]
        scores = dot(query, key, ((0,), (0,))) * SCORE_SCALE
        turned = dot(key, query, ((0,), (0,))) * SCORE_SCALE
        weights = jnp.where(other >= token, 1.0 + turned + 0.5 * turned * turned, 0.0).astype(bf16)
        grad_values_ref[:, lanes] = dot(weights, grad_numer, ((1,), (0,)))
        grad_weights = dot(grad_numer, values, ((1,), (1,)))
        grad_scores = jnp.where(token >= other, grad_weights * (1.0 + scores), 0.0).astype(bf16)
        grad_query = dot(key, grad_scores, ((1,), (1,))) * SCORE_SCALE
        grad_key_ref[head_of(head, FEAT)] = dot(query, grad_scores, ((1,), (0,))) * SCORE_SCALE
        grad_feat = dot(prefix_ref[head_of(head, PACKED)], grad_numer, ((1,), (1,)))
        grad_query = grad_query + taylor_back(query.astype(f32), grad_feat, 2.0)
        grad_query_ref[head_of(head, FEAT)] = grad_query.astype(bf16)


def late_kernel(key_ref, values_ref, state_ref, early_key_ref, early_values_ref, grad_key_ref, grad_values_ref):
    for head in range(STEP_HEADS):
        lanes = head_of(head, VDIM)
        key = key_ref[head_of(head, FEAT)].astype(f32)
        state = state_ref[head_of(head, PACKED)]
        grad_feat = dot(state, values_ref[:, lanes], ((1,), (1,)))
        grad_key = early_key_ref[head_of(head, FEAT)] + taylor_back(key, grad_feat, 1.0)
        grad_key_ref[head_of(head, FEAT)] = grad_key.astype(bf16)
        feat = taylor_rows(key, 1.0)
        grad_values_ref[:, lanes] = early_values_ref[:, lanes] + dot(feat, state, ((0,), (0,)))


def finish_kernel(
    grad_query_ref,
    grad_key_ref,
    query_ref,
    key_ref,
    grad_values_ref,
    after_ref,
    taps_ref,
    gain_ref,
    x_ref,
    grad_ref,
    out_ref,
):
    grad_values = grad_values_ref[...]
    after = after_ref[...]
    rows = grad_values.shape[0]
    row = lax.broadcasted_iota(jnp.int32, grad_values.shape, 0)
    one_on = jnp.where(row == rows - 1, after[0:1], rolled(grad_values, -1))
    two_on = jnp.where(row == rows - 1, after[1:2], rolled(one_on, -1))
    grad_normed = dot(grad_query_ref[...], query_ref[...], ((0,), (1,)))
    grad_normed = grad_normed + dot(grad_key_ref[...], key_ref[...], ((0,), (1,)))
    grad_normed = grad_normed + (taps_ref[2:3] * grad_values + taps_ref[1:2] * one_on + taps_ref[0:1] * two_on)
    scaled = grad_normed * gain_ref[...]
    x = x_ref[...].astype(f32)
    inv = lax.rsqrt(jnp.mean(x * x, axis=1, keepdims=True) + EPSILON)
    mean = jnp.mean(x * scaled, axis=1, keepdims=True)
    out_ref[...] = (grad_ref[...].astype(f32) + inv * scaled - x * (inv * inv * inv * mean)).astype(bf16)


def group_specs(group):
    def tokens(rows, whole):
        return pl.BlockSpec((rows, STEP_HEADS * VDIM), lambda i: (0, i + (group * STEPS if whole else 0)))

    def heads(rows, cols, whole):
        return pl.BlockSpec((STEP_HEADS * rows, cols), lambda i: (i + (group * STEPS if whole else 0), 0))

    return tokens, heads


def per_group(kernel, in_specs, out_specs, out_shape, name, flops=1 << 28):
    return pl.pallas_call(
        kernel,
        grid=(STEPS,),
        in_specs=in_specs,
        out_specs=out_specs,
        out_shape=out_shape,
        compiler_params=kernel_params(),
        cost_estimate=cost(flops, 4 << 20),
        name=name,
    )


def chip_sums_kernel(reverse, got_ref, out_ref):
    total = jnp.zeros(got_ref.shape[1:], f32)
    order = range(CHIPS - 1, -1, -1) if reverse else range(CHIPS)
    for chip in order:
        out_ref[chip] = total.astype(bf16)
        total = total + got_ref[chip].astype(f32)


def chip_sums(got, reverse):
    return pl.pallas_call(
        functools.partial(chip_sums_kernel, reverse),
        out_shape=jax.ShapeDtypeStruct(got.shape, bf16),
        compiler_params=kernel_params(16),
        cost_estimate=cost(1 << 20, 1 << 19),
        name="chip_sums",
    )(got)


def core_swap(block):
    count = lax.axis_size("seq")
    return lax.ppermute(block, "seq", [(i, i ^ 1) for i in range(count)])


def over_chips(block):
    count = lax.axis_size("seq")
    groups = [list(range(core, count, 2)) for core in range(2)]
    return lax.all_to_all(block, "seq", 0, 0, tiled=True, axis_index_groups=groups)


def add_states(one, other):
    return (one.astype(f32) + other.astype(f32)).astype(bf16)


def scan_states(state, reverse):
    core = lax.axis_index("seq") % 2
    half_rows = state.shape[0] // 2
    halves = state.reshape(2, half_rows, VDIM)
    own = lax.dynamic_index_in_dim(halves, core, 0, False)
    away = lax.dynamic_index_in_dim(halves, 1 - core, 0, False)
    other = core_swap(away)
    total = add_states(own, other)
    got = over_chips(total.reshape(CHIPS, half_rows // CHIPS, VDIM))
    before = over_chips(chip_sums(got, reverse)).reshape(half_rows, VDIM)
    behind = core == (0 if reverse else 1)
    mine = jnp.where(behind, add_states(before, other), before)
    theirs = core_swap(jnp.where(behind, before, add_states(before, own)))
    first = jnp.where(core == 0, mine, theirs)
    second = jnp.where(core == 0, theirs, mine)
    return jnp.concatenate([first, second], axis=0)


def neighbour_rows(edge, distance):
    devices = range(lax.axis_size("seq"))
    route = [(i - distance, i) for i in devices if i - distance in devices]
    return lax.ppermute(edge, "seq", route)


def section_pass(block, distance):
    count = lax.axis_size("section")
    return lax.ppermute(block, "section", [((i - distance) % count, i) for i in range(count)])


def section_pass_cut(block, distance, pieces):
    rows = block.shape[0] // pieces
    return jnp.concatenate(
        [section_pass(block[k * rows : (k + 1) * rows], distance) for k in range(pieces)], axis=0
    )


def local(layer_in, norm_gain, conv_weight, query_weight, key_weight, out_gain, layer_grad):
    x, grad = layer_in[0], layer_grad[0]
    taps, query_proj, key_proj = conv_weight[0], query_weight[0], key_weight[0]
    rows, width = x.shape
    group_width = GROUP_HEADS * VDIM
    shape = jax.ShapeDtypeStruct

    normed, query, key = project(x, norm_gain, query_proj, key_proj)
    before = neighbour_rows(normed[-2:], 1)

    values, prefixes = [], []
    for group in range(GROUPS):
        tokens, heads = group_specs(group)
        value, state = per_group(
            state_kernel,
            [tokens(rows, True), tokens(2, True), tokens(3, True), heads(FEAT, rows, True)],
            [tokens(rows, False), heads(PACKED, VDIM, False)],
            [shape((rows, group_width), bf16), shape((GROUP_HEADS * PACKED, VDIM), bf16)],
            "state",
        )(normed, before, taps, key)
        values.append(value)
        prefixes.append(scan_states(state, False))

    insides = []
    for group in range(GROUPS):
        tokens, heads = group_specs(group)
        insides.append(
            per_group(
                inside_kernel,
                [heads(FEAT, rows, True), heads(FEAT, rows, True), tokens(rows, False)],
                tokens(rows, False),
                shape((rows, group_width), f32),
                "inside",
            )(query, key, values[group])
        )

    outputs, grad_numers, grad_states = [], [], []
    for group in range(GROUPS):
        tokens, heads = group_specs(group)
        output, grad_numer, grad_prefix = per_group(
            output_kernel,
            [
                heads(FEAT, rows, True),
                tokens(rows, False),
                heads(PACKED, VDIM, False),
                tokens(rows, True),
                tokens(rows, True),
                tokens(1, True),
            ],
            [tokens(rows, False), tokens(rows, False), heads(PACKED, VDIM, False)],
            [
                shape((rows, group_width), bf16),
                shape((rows, group_width), bf16),
                shape((GROUP_HEADS * PACKED, VDIM), bf16),
            ],
            "output",
        )(query, insides[group], prefixes[group], x, grad, out_gain)
        outputs.append(output)
        grad_numers.append(grad_numer)
        grad_states.append(scan_states(grad_prefix, True))
    sent_forward = section_pass(jnp.concatenate(outputs, axis=1), 1)

    grad_queries, grad_keys, grad_values = [], [], []
    for group in range(GROUPS):
        tokens, heads = group_specs(group)
        grad_query, grad_key, grad_value = per_group(
            inside_back_kernel,
            [
                heads(FEAT, rows, True),
                heads(FEAT, rows, True),
                tokens(rows, False),
                tokens(rows, False),
                heads(PACKED, VDIM, False),
            ],
            [heads(FEAT, rows, False), heads(FEAT, rows, False), tokens(rows, False)],
            [
                shape((GROUP_HEADS * FEAT, rows), bf16),
                shape((GROUP_HEADS * FEAT, rows), f32),
                shape((rows, group_width), f32),
            ],
            "inside_back",
        )(query, key, values[group], grad_numers[group], prefixes[group])
        grad_queries.append(grad_query)
        grad_keys.append(grad_key)
        grad_values.append(grad_value)

    for group in range(GROUPS):
        tokens, heads = group_specs(group)
        grad_keys[group], grad_values[group] = per_group(
            late_kernel,
            [
                heads(FEAT, rows, True),
                tokens(rows, False),
                heads(PACKED, VDIM, False),
                heads(FEAT, rows, False),
                tokens(rows, False),
            ],
            [heads(FEAT, rows, False), tokens(rows, False)],
            [shape((GROUP_HEADS * FEAT, rows), bf16), shape((rows, group_width), f32)],
            "late",
        )(key, values[group], grad_states[group], grad_keys[group], grad_values[group])
    grad_query = jnp.concatenate(grad_queries, axis=0)
    grad_key = jnp.concatenate(grad_keys, axis=0)
    grad_value = jnp.concatenate(grad_values, axis=1)
    after = neighbour_rows(grad_value[:2], -1)
    in_grad = pl.pallas_call(
        finish_kernel,
        out_shape=shape((rows, width), bf16),
        compiler_params=kernel_params(),
        cost_estimate=cost(4 * rows * width * query_proj.shape[1], 16 << 20),
        name="finish",
    )(grad_query, grad_key, query_proj, key_proj, grad_value, after, taps, norm_gain, x, grad)
    sent_backward = section_pass_cut(in_grad, -1, 4)
    return (sent_forward[None], sent_backward[None])


def solution(mesh):
    return jax.shard_map(
        local,
        mesh=mesh,
        in_specs=(
            P("section", "seq", None),
            P("section", None),
            P("section", None, None),
            P("section", None, None),
            P("section", None, None),
            P("section", None),
            P("section", "seq", None),
        ),
        out_specs=(P("section", "seq", None), P("section", "seq", None)),
        check_vma=False,
    )
```

time: 500 us -> 274 us (0.55); the launches traced: 490 us -> 272 us
  waiting for transfers between devices: 272 us -> 75 us
  starting transfers between devices: 11.2 us -> 100 us
  local copies, waits for them, and re-layouts: 94.3 us -> 27.6 us
  matrix products: 45.9 us -> 0 us
  Pallas kernels: 0 us -> 39.9 us
  other arithmetic: 50.6 us -> 27.7 us
  between operations: 15 us -> 1.92 us
    all_gather x2 -> x0, waiting for transfers between devices: 237 us -> none  [carried_in(): gathered = lax.all_gather(part, axis)]
    all_to_all x0 -> x12, starting transfers between devices: none -> 61.4 us  [over_chips(): lax.all_to_all(block, 'seq', 0, 0, tiled=True, axis_index_groups=groups)]
    dot_general x16 -> x0, matrix products: 45.9 us -> none  [the longest x1 6.5 us: backward_layer(): lax.dot_general(grad_key_half, key_proj, contract_rows, preferred_element...]
    dynamic_slice x31 -> x0, local copies, waits for them, and re-layouts: 42.7 us -> none  [one(): return combine(state, lax.dynamic_index_in_dim(gathered, source, 0, False))]
    all_to_all x0 -> x12, waiting for transfers between devices: none -> 40.1 us  [over_chips(): lax.all_to_all(block, 'seq', 0, 0, tiled=True, axis_index_groups=groups)]
    pallas_call x0 -> x23, Pallas kernels: none -> 39.9 us  [the longest x3 9.51 us: local(): per_group(inside_back_kernel, [heads(FEAT, rows, True), heads(FEAT, rows,...]
    ppermute x4 -> x19, starting transfers between devices: 11.2 us -> 38.9 us  [the longest x12 27.4 us: core_swap(): return lax.ppermute(block, 'seq', [(i, i ^ 1) for i in range(count)])]
    dot_general x2 -> x0, other arithmetic: 23.3 us -> none  [taylor_back(): jnp.einsum('habk,hbk->hak', symmetric, columns, precision=lax.Precision.H...]
  transfers between devices with their start and end apart: 6 -> 31, of which waited for: 4 -> 16; matrix products, arithmetic and copies ran while one was open for 13% -> 11% of each run, Pallas kernels for 0% -> 13%
where the time goes in v1:
time: 274 us; the launch traced here: 272 us
  starting transfers between devices  100 us (36%)
  waiting for transfers between devices  75 us (27%)
  Pallas kernels  39.9 us (15%)
  other arithmetic  27.7 us (10%)
  local copies, waits for them, and re-layouts  27.6 us (10%)
    all_to_all x12, starting transfers between devices, over_chips(): lax.all_to_all(block, 'seq', 0, 0, tiled=True, axis_index_groups=groups)  61.4 us
    all_to_all x12, waiting for transfers between devices, over_chips(): lax.all_to_all(block, 'seq', 0, 0, tiled=True, axis_index_groups=groups)  40.1 us
    ppermute x5, waiting for transfers between devices, section_pass(): lax.ppermute(block, 'section', [((i - distance) % count, i) for i in rang...  31 us
    ppermute x12, starting transfers between devices, core_swap(): return lax.ppermute(block, 'seq', [(i, i ^ 1) for i in range(count)])  27.4 us
    unnamed x166, local copies, waits for them, and re-layouts  25.2 us
    pallas_call x3, Pallas kernels, local(): per_group(inside_back_kernel, [heads(FEAT, rows, True), heads(FEAT, rows,...  9.51 us
    select_n x6, other arithmetic, scan_states(): theirs = core_swap(jnp.where(behind, before, add_states(before, own)))  9.12 us
    pallas_call x3, Pallas kernels, local(): per_group(output_kernel, [heads(FEAT, rows, True), tokens(rows, False), h...  8.12 us
  transfers between devices with their start and end apart: 31, of which 16 were waited for; matrix products, arithmetic and copies ran while one was open for 11% of the time, Pallas kernels for 13%

profile of v1, /device:TPU:1, one launch (start us, length us, event | category | flops | bytes accessed | tf_op | source)
XLA Modules:
  0.0 272.5 jit_solution(18065782988192405237)
XLA Ops:
  6.1 4.9 %project.1 = (bf16[256,3072]{1,0:T(8,128)(2,1)S(1)}, bf16[384,256]{1,0:T(8,128)(2,1)S(1)}, bf16[384,256]{1,0:T(8,128)(2,1)S(1)}) custom-call(bf16[256,3072]{1,0:T(8,128)(2,1)S(1)} %bitcast.100, f32[1,3072]{1,0:T(1,128)S(1)} %copy-done.74, bf16[3072,384]{1,0:T(8,128)(2,1)S(1)} %bitcast.109, bf16[3072,384]{1,0:T(8,128)(2,1)S(1)} %bitcast.111), custom_call_target="tpu_custom_call" | custom-call | flops 1207959552 | bytes 8388608 | tf_op jit(solution)/shard_map/project/pallas_call | solution.py:91
  11.0 4.5 %collective-permute-start = (bf16[2,3072]{1,0:T(2,128)(2,1)S(1)}, bf16[2,3072]{1,0:T(2,128)(2,1)S(1)}, u32[]{:S(2)}, u32[]{:S(2)}) collective-permute-start(bf16[2,3072]{1,0:T(2,128)(2,1)S(1)} %slice.18), channel_id=1, source_target_pairs={{0,4},{4,8},{8,12},{12,16},{16,20},{20,24},{24,28},{28,32},{32,36}... | collective-permute-start | bytes 36872 | tf_op jit(solution)/shard_map/ppermute | solution.py:306
  22.3 8.7 %all-to-all-start.4 = ((bf16[16,40,128]{2,1,0:T(8,128)(2,1)}), bf16[16,40,128]{2,1,0:T(8,128)(2,1)S(1)}, u32[]{:S(2)}, u32[]{:S(2)}) async-start(bf16[16,40,128]{2,1,0:T(8,128)(2,1)} %bitcast.19), calls=%async_computation.4 | async-start | bytes 327680 | tf_op jit(solution)/shard_map/all_to_all | solution.py:278
  32.6 5.6 %all-to-all-done.4.got_ref = bf16[16,40,128]{2,1,0:T(8,128)(2,1)S(1)} async-done(((bf16[16,40,128]{2,1,0:T(8,128)(2,1)}), bf16[16,40,128]{2,1,0:T(8,128)(2,1)S(1)}, u32[]{:S(2)}, u32[]{:S(2)}) %all-to-all-start.4) | async-done | bytes 163872 | tf_op jit(solution)/shard_map/all_to_all | solution.py:278
  42.5 6.2 %all-to-all-done.got_ref = bf16[16,40,128]{2,1,0:T(8,128)(2,1)S(1)} async-done(((bf16[16,40,128]{2,1,0:T(8,128)(2,1)}), bf16[16,40,128]{2,1,0:T(8,128)(2,1)S(1)}, u32[]{:S(2)}, u32[]{:S(2)}) %all-to-all-start) | async-done | bytes 163872 | tf_op jit(solution)/shard_map/all_to_all | solution.py:278
  53.0 6.3 %all-to-all-done.2.got_ref = bf16[16,40,128]{2,1,0:T(8,128)(2,1)S(1)} async-done(((bf16[16,40,128]{2,1,0:T(8,128)(2,1)}), bf16[16,40,128]{2,1,0:T(8,128)(2,1)S(1)}, u32[]{:S(2)}, u32[]{:S(2)}) %all-to-all-start.2) | async-done | bytes 163872 | tf_op jit(solution)/shard_map/all_to_all | solution.py:278
  59.3 4.2 %all-to-all-start.5 = ((bf16[16,40,128]{2,1,0:T(8,128)(2,1)}), bf16[16,40,128]{2,1,0:T(8,128)(2,1)}, u32[]{:S(2)}, u32[]{:S(2)}) async-start(bf16[16,40,128]{2,1,0:T(8,128)(2,1)} %chip_sums.8), calls=%async_computation.5 | async-start | bytes 327680 | tf_op jit(solution)/shard_map/all_to_all | solution.py:278
  74.3 6.6 %all-to-all-start.3 = ((bf16[16,40,128]{2,1,0:T(8,128)(2,1)}), bf16[16,40,128]{2,1,0:T(8,128)(2,1)}, u32[]{:S(2)}, u32[]{:S(2)}) async-start(bf16[16,40,128]{2,1,0:T(8,128)(2,1)} %copy-done.51), calls=%async_computation.3 | async-start | bytes 327680 | tf_op jit(solution)/shard_map/all_to_all | solution.py:278
  87.9 5.7 %all-to-all-start.1 = ((bf16[16,40,128]{2,1,0:T(8,128)(2,1)}), bf16[16,40,128]{2,1,0:T(8,128)(2,1)}, u32[]{:S(2)}, u32[]{:S(2)}) async-start(bf16[16,40,128]{2,1,0:T(8,128)(2,1)} %copy-done.46), calls=%async_computation.1 | async-start | bytes 327680 | tf_op jit(solution)/shard_map/all_to_all | solution.py:278
  101.8 4.9 %collective-permute-start.2 = (bf16[640,128]{1,0:T(8,128)(2,1)S(1)}, bf16[640,128]{1,0:T(8,128)(2,1)S(1)}, u32[]{:S(2)}, u32[]{:S(2)}) collective-permute-start(bf16[640,128]{1,0:T(8,128)(2,1)S(1)} %fusion.23), channel_id=1, source_target_pairs={{0,4},{4,0},{8,12},{12,8},{16,20},{20,16},{24,28},{28,24},{32,36},... | collective-permute-start | bytes 491528 | tf_op jit(solution)/shard_map/ppermute | solution.py:272
  126.1 4.2 %all-to-all-start.8 = ((bf16[16,40,128]{2,1,0:T(8,128)(2,1)}), bf16[16,40,128]{2,1,0:T(8,128)(2,1)}, u32[]{:S(2)}, u32[]{:S(2)}) async-start(bf16[16,40,128]{2,1,0:T(8,128)(2,1)} %bitcast.137), calls=%async_computation.8 | async-start | bytes 327680 | tf_op jit(solution)/shard_map/all_to_all | solution.py:278
  132.0 5.6 %all-to-all-done.8.got_ref = bf16[16,40,128]{2,1,0:T(8,128)(2,1)} async-done(((bf16[16,40,128]{2,1,0:T(8,128)(2,1)}), bf16[16,40,128]{2,1,0:T(8,128)(2,1)}, u32[]{:S(2)}, u32[]{:S(2)}) %all-to-all-start.8) | async-done | bytes 163872 | tf_op jit(solution)/shard_map/all_to_all | solution.py:278
  143.5 5.3 %all-to-all-done.6.got_ref = bf16[16,40,128]{2,1,0:T(8,128)(2,1)} async-done(((bf16[16,40,128]{2,1,0:T(8,128)(2,1)}), bf16[16,40,128]{2,1,0:T(8,128)(2,1)}, u32[]{:S(2)}, u32[]{:S(2)}) %all-to-all-start.6) | async-done | bytes 163872 | tf_op jit(solution)/shard_map/all_to_all | solution.py:278
  148.8 4.2 %all-to-all-start.10 = ((bf16[16,40,128]{2,1,0:T(8,128)(2,1)}), bf16[16,40,128]{2,1,0:T(8,128)(2,1)}, u32[]{:S(2)}, u32[]{:S(2)}) async-start(bf16[16,40,128]{2,1,0:T(8,128)(2,1)} %bitcast.136), calls=%async_computation.10 | async-start | bytes 327680 | tf_op jit(solution)/shard_map/all_to_all | solution.py:278
  154.6 5.5 %all-to-all-done.10.got_ref = bf16[16,40,128]{2,1,0:T(8,128)(2,1)} async-done(((bf16[16,40,128]{2,1,0:T(8,128)(2,1)}), bf16[16,40,128]{2,1,0:T(8,128)(2,1)}, u32[]{:S(2)}, u32[]{:S(2)}) %all-to-all-start.10) | async-done | bytes 163872 | tf_op jit(solution)/shard_map/all_to_all | solution.py:278
  160.1 4.2 %all-to-all-start.9 = ((bf16[16,40,128]{2,1,0:T(8,128)(2,1)}), bf16[16,40,128]{2,1,0:T(8,128)(2,1)}, u32[]{:S(2)}, u32[]{:S(2)}) async-start(bf16[16,40,128]{2,1,0:T(8,128)(2,1)} %copy-done.43), calls=%async_computation.9 | async-start | bytes 327680 | tf_op jit(solution)/shard_map/all_to_all | solution.py:278
  184.4 6.7 %all-to-all-start.7 = ((bf16[16,40,128]{2,1,0:T(8,128)(2,1)}), bf16[16,40,128]{2,1,0:T(8,128)(2,1)}, u32[]{:S(2)}, u32[]{:S(2)}) async-start(bf16[16,40,128]{2,1,0:T(8,128)(2,1)} %copy-done.50), calls=%async_computation.7 | async-start | bytes 327680 | tf_op jit(solution)/shard_map/all_to_all | solution.py:278
  192.9 4.3 %collective-permute-start.11 = (bf16[640,128]{1,0:T(8,128)(2,1)}, bf16[640,128]{1,0:T(8,128)(2,1)}, u32[]{:S(2)}, u32[]{:S(2)}) collective-permute-start(bf16[640,128]{1,0:T(8,128)(2,1)} %fusion.19), channel_id=1, source_target_pairs={{0,4},{4,0},{8,12},{12,8},{16,20},{20,16},{24,28},{28,24},{32,36},... | collective-permute-start | bytes 491528 | tf_op jit(solution)/shard_map/ppermute | solution.py:272
  198.2 5.9 %all-to-all-start.11 = ((bf16[16,40,128]{2,1,0:T(8,128)(2,1)}), bf16[16,40,128]{2,1,0:T(8,128)(2,1)}, u32[]{:S(2)}, u32[]{:S(2)}) async-start(bf16[16,40,128]{2,1,0:T(8,128)(2,1)} %copy-done.47), calls=%async_computation.11 | async-start | bytes 327680 | tf_op jit(solution)/shard_map/all_to_all | solution.py:278
  212.4 5.1 %collective-permute-start.13 = (bf16[640,128]{1,0:T(8,128)(2,1)S(1)}, bf16[640,128]{1,0:T(8,128)(2,1)S(1)}, u32[]{:S(2)}, u32[]{:S(2)}) collective-permute-start(bf16[640,128]{1,0:T(8,128)(2,1)S(1)} %fusion.18), channel_id=1, source_target_pairs={{0,4},{4,0},{8,12},{12,8},{16,20},{20,16},{24,28},{28,24},{32,36},... | collective-permute-start | bytes 491528 | tf_op jit(solution)/shard_map/ppermute | solution.py:272
  237.6 7.7 %collective-permute-done.15 = bf16[64,3072]{1,0:T(8,128)(2,1)S(1)} collective-permute-done((bf16[64,3072]{1,0:T(8,128)(2,1)S(1)}, bf16[64,3072]{1,0:T(8,128)(2,1)S(1)}, u32[]{:S(2)}, u32[]{:S(2)}) %collective-permute-start.15) | collective-permute-done | bytes 393248 | tf_op jit(solution)/shard_map/ppermute | solution.py:311
  245.2 8.4 %collective-permute-done.18 = bf16[64,3072]{1,0:T(8,128)(2,1)S(1)} collective-permute-done((bf16[64,3072]{1,0:T(8,128)(2,1)S(1)}, bf16[64,3072]{1,0:T(8,128)(2,1)S(1)}, u32[]{:S(2)}, u32[]{:S(2)}) %collective-permute-start.18) | collective-permute-done | bytes 393248 | tf_op jit(solution)/shard_map/ppermute | solution.py:311
  253.6 8.4 %collective-permute-done.17 = bf16[64,3072]{1,0:T(8,128)(2,1)S(1)} collective-permute-done((bf16[64,3072]{1,0:T(8,128)(2,1)S(1)}, bf16[64,3072]{1,0:T(8,128)(2,1)S(1)}, u32[]{:S(2)}, u32[]{:S(2)}) %collective-permute-start.17) | collective-permute-done | bytes 393248 | tf_op jit(solution)/shard_map/ppermute | solution.py:311
  262.1 6.5 %collective-permute-done.16 = bf16[64,3072]{1,0:T(8,128)(2,1)S(1)} collective-permute-done((bf16[64,3072]{1,0:T(8,128)(2,1)S(1)}, bf16[64,3072]{1,0:T(8,128)(2,1)S(1)}, u32[]{:S(2)}, u32[]{:S(2)}) %collective-permute-start.16) | collective-permute-done | bytes 393248 | tf_op jit(solution)/shard_map/ppermute | solution.py:311
  (264 shorter events, 131.1 us)
Async XLA Ops:
  21.3 20.4 %collective-permute-start.3 = (bf16[640,128]{1,0:T(8,128)(2,1)S(1)}, bf16[640,128]{1,0:T(8,128)(2,1)S(1)}, u32[]{:S(2)}, u32[]{:S(2)}) collective-permute-start(bf16[640,128]{1,0:T(8,128)(2,1)S(1)} %dynamic-slice_bitcast_fusion.4), channel_id=1, source_target_pairs={{0,4},{4,0},{8,12},{12,8},{16,20},{20,16},{24,28},{28,24},{32,36},... | collective-permute-start | bytes 491528 | tf_op jit(solution)/shard_map/ppermute | solution.py:272
  22.3 16.0 %all-to-all-start.4 = ((bf16[16,40,128]{2,1,0:T(8,128)(2,1)}), bf16[16,40,128]{2,1,0:T(8,128)(2,1)S(1)}, u32[]{:S(2)}, u32[]{:S(2)}) async-start(bf16[16,40,128]{2,1,0:T(8,128)(2,1)} %bitcast.19), calls=%async_computation.4 | async-start | bytes 327680 | tf_op jit(solution)/shard_map/all_to_all | solution.py:278
  59.3 15.0 %all-to-all-start.5 = ((bf16[16,40,128]{2,1,0:T(8,128)(2,1)}), bf16[16,40,128]{2,1,0:T(8,128)(2,1)}, u32[]{:S(2)}, u32[]{:S(2)}) async-start(bf16[16,40,128]{2,1,0:T(8,128)(2,1)} %chip_sums.8), calls=%async_computation.5 | async-start | bytes 327680 | tf_op jit(solution)/shard_map/all_to_all | solution.py:278
  74.3 13.7 %all-to-all-start.3 = ((bf16[16,40,128]{2,1,0:T(8,128)(2,1)}), bf16[16,40,128]{2,1,0:T(8,128)(2,1)}, u32[]{:S(2)}, u32[]{:S(2)}) async-start(bf16[16,40,128]{2,1,0:T(8,128)(2,1)} %copy-done.51), calls=%async_computation.3 | async-start | bytes 327680 | tf_op jit(solution)/shard_map/all_to_all | solution.py:278
  82.6 36.4 %collective-permute-start.6 = (bf16[640,128]{1,0:T(8,128)(2,1)}, bf16[640,128]{1,0:T(8,128)(2,1)}, u32[]{:S(2)}, u32[]{:S(2)}) collective-permute-start(bf16[640,128]{1,0:T(8,128)(2,1)} %fusion.21), channel_id=1, source_target_pairs={{0,4},{4,0},{8,12},{12,8},{16,20},{20,16},{24,28},{28,24},{32,36},... | collective-permute-start | bytes 491528 | tf_op jit(solution)/shard_map/ppermute | solution.py:272
  87.9 12.8 %all-to-all-start.1 = ((bf16[16,40,128]{2,1,0:T(8,128)(2,1)}), bf16[16,40,128]{2,1,0:T(8,128)(2,1)}, u32[]{:S(2)}, u32[]{:S(2)}) async-start(bf16[16,40,128]{2,1,0:T(8,128)(2,1)} %copy-done.46), calls=%async_computation.1 | async-start | bytes 327680 | tf_op jit(solution)/shard_map/all_to_all | solution.py:278
  95.4 11.3 %collective-permute-start.4 = (bf16[640,128]{1,0:T(8,128)(2,1)}, bf16[640,128]{1,0:T(8,128)(2,1)}, u32[]{:S(2)}, u32[]{:S(2)}) collective-permute-start(bf16[640,128]{1,0:T(8,128)(2,1)} %fusion.22), channel_id=1, source_target_pairs={{0,4},{4,0},{8,12},{12,8},{16,20},{20,16},{24,28},{28,24},{32,36},... | collective-permute-start | bytes 491528 | tf_op jit(solution)/shard_map/ppermute | solution.py:272
  101.8 11.3 %collective-permute-start.2 = (bf16[640,128]{1,0:T(8,128)(2,1)S(1)}, bf16[640,128]{1,0:T(8,128)(2,1)S(1)}, u32[]{:S(2)}, u32[]{:S(2)}) collective-permute-start(bf16[640,128]{1,0:T(8,128)(2,1)S(1)} %fusion.23), channel_id=1, source_target_pairs={{0,4},{4,0},{8,12},{12,8},{16,20},{20,16},{24,28},{28,24},{32,36},... | collective-permute-start | bytes 491528 | tf_op jit(solution)/shard_map/ppermute | solution.py:272
  112.8 12.5 %collective-permute-start.10 = (bf16[640,128]{1,0:T(8,128)(2,1)S(1)}, bf16[640,128]{1,0:T(8,128)(2,1)S(1)}, u32[]{:S(2)}, u32[]{:S(2)}) collective-permute-start(bf16[640,128]{1,0:T(8,128)(2,1)S(1)} %dynamic-slice_bitcast_fusion.1), channel_id=1, source_target_pairs={{0,4},{4,0},{8,12},{12,8},{16,20},{20,16},{24,28},{28,24},{32,36},... | collective-permute-start | bytes 491528 | tf_op jit(solution)/shard_map/ppermute | solution.py:272
  118.6 11.7 %collective-permute-start.8 = (bf16[640,128]{1,0:T(8,128)(2,1)}, bf16[640,128]{1,0:T(8,128)(2,1)}, u32[]{:S(2)}, u32[]{:S(2)}) collective-permute-start(bf16[640,128]{1,0:T(8,128)(2,1)} %dynamic-slice_bitcast_fusion.2), channel_id=1, source_target_pairs={{0,4},{4,0},{8,12},{12,8},{16,20},{20,16},{24,28},{28,24},{32,36},... | collective-permute-start | bytes 491528 | tf_op jit(solution)/shard_map/ppermute | solution.py:272
  125.2 16.6 %collective-permute-start.12 = (bf16[640,128]{1,0:T(8,128)(2,1)}, bf16[640,128]{1,0:T(8,128)(2,1)}, u32[]{:S(2)}, u32[]{:S(2)}) collective-permute-start(bf16[640,128]{1,0:T(8,128)(2,1)} %dynamic-slice_bitcast_fusion), channel_id=1, source_target_pairs={{0,4},{4,0},{8,12},{12,8},{16,20},{20,16},{24,28},{28,24},{32,36},... | collective-permute-start | bytes 491528 | tf_op jit(solution)/shard_map/ppermute | solution.py:272
  126.1 11.5 %all-to-all-start.8 = ((bf16[16,40,128]{2,1,0:T(8,128)(2,1)}), bf16[16,40,128]{2,1,0:T(8,128)(2,1)}, u32[]{:S(2)}, u32[]{:S(2)}) async-start(bf16[16,40,128]{2,1,0:T(8,128)(2,1)} %bitcast.137), calls=%async_computation.8 | async-start | bytes 327680 | tf_op jit(solution)/shard_map/all_to_all | solution.py:278
  137.6 11.2 %all-to-all-start.6 = ((bf16[16,40,128]{2,1,0:T(8,128)(2,1)}), bf16[16,40,128]{2,1,0:T(8,128)(2,1)}, u32[]{:S(2)}, u32[]{:S(2)}) async-start(bf16[16,40,128]{2,1,0:T(8,128)(2,1)} %bitcast.135), calls=%async_computation.6 | async-start | bytes 327680 | tf_op jit(solution)/shard_map/all_to_all | solution.py:278
  148.8 11.3 %all-to-all-start.10 = ((bf16[16,40,128]{2,1,0:T(8,128)(2,1)}), bf16[16,40,128]{2,1,0:T(8,128)(2,1)}, u32[]{:S(2)}, u32[]{:S(2)}) async-start(bf16[16,40,128]{2,1,0:T(8,128)(2,1)} %bitcast.136), calls=%async_computation.10 | async-start | bytes 327680 | tf_op jit(solution)/shard_map/all_to_all | solution.py:278
  160.1 24.3 %all-to-all-start.9 = ((bf16[16,40,128]{2,1,0:T(8,128)(2,1)}), bf16[16,40,128]{2,1,0:T(8,128)(2,1)}, u32[]{:S(2)}, u32[]{:S(2)}) async-start(bf16[16,40,128]{2,1,0:T(8,128)(2,1)} %copy-done.43), calls=%async_computation.9 | async-start | bytes 327680 | tf_op jit(solution)/shard_map/all_to_all | solution.py:278
  167.2 102.7 %collective-permute-start.7 = (bf16[256,3072]{1,0:T(8,128)(2,1)}, bf16[256,3072]{1,0:T(8,128)(2,1)}, u32[]{:S(2)}, u32[]{:S(2)}) collective-permute-start(bf16[256,3072]{1,0:T(8,128)(2,1)} %pad_maximum_fusion), channel_id=1, source_target_pairs={{3,0},{0,1},{1,2},{2,3},{7,4},{4,5},{5,6},{6,7},{11,8},{8,9},{9,10... | collective-permute-start | bytes 4718600 | tf_op jit(solution)/shard_map/ppermute | solution.py:311
  184.4 13.8 %all-to-all-start.7 = ((bf16[16,40,128]{2,1,0:T(8,128)(2,1)}), bf16[16,40,128]{2,1,0:T(8,128)(2,1)}, u32[]{:S(2)}, u32[]{:S(2)}) async-start(bf16[16,40,128]{2,1,0:T(8,128)(2,1)} %copy-done.50), calls=%async_computation.7 | async-start | bytes 327680 | tf_op jit(solution)/shard_map/all_to_all | solution.py:278
  192.9 24.6 %collective-permute-start.11 = (bf16[640,128]{1,0:T(8,128)(2,1)}, bf16[640,128]{1,0:T(8,128)(2,1)}, u32[]{:S(2)}, u32[]{:S(2)}) collective-permute-start(bf16[640,128]{1,0:T(8,128)(2,1)} %fusion.19), channel_id=1, source_target_pairs={{0,4},{4,0},{8,12},{12,8},{16,20},{20,16},{24,28},{28,24},{32,36},... | collective-permute-start | bytes 491528 | tf_op jit(solution)/shard_map/ppermute | solution.py:272
  198.2 13.0 %all-to-all-start.11 = ((bf16[16,40,128]{2,1,0:T(8,128)(2,1)}), bf16[16,40,128]{2,1,0:T(8,128)(2,1)}, u32[]{:S(2)}, u32[]{:S(2)}) async-start(bf16[16,40,128]{2,1,0:T(8,128)(2,1)} %copy-done.47), calls=%async_computation.11 | async-start | bytes 327680 | tf_op jit(solution)/shard_map/all_to_all | solution.py:278
  205.8 12.9 %collective-permute-start.9 = (bf16[640,128]{1,0:T(8,128)(2,1)}, bf16[640,128]{1,0:T(8,128)(2,1)}, u32[]{:S(2)}, u32[]{:S(2)}) collective-permute-start(bf16[640,128]{1,0:T(8,128)(2,1)} %fusion.20), channel_id=1, source_target_pairs={{0,4},{4,0},{8,12},{12,8},{16,20},{20,16},{24,28},{28,24},{32,36},... | collective-permute-start | bytes 491528 | tf_op jit(solution)/shard_map/ppermute | solution.py:272
  234.0 11.3 %collective-permute-start.15 = (bf16[64,3072]{1,0:T(8,128)(2,1)S(1)}, bf16[64,3072]{1,0:T(8,128)(2,1)S(1)}, u32[]{:S(2)}, u32[]{:S(2)}) collective-permute-start(bf16[64,3072]{1,0:T(8,128)(2,1)S(1)} %get-tuple-element.68), channel_id=1, source_target_pairs={{1,0},{2,1},{3,2},{0,3},{5,4},{6,5},{7,6},{4,7},{9,8},{10,9},{11,1... | collective-permute-start | bytes 1179656 | tf_op jit(solution)/shard_map/ppermute | solution.py:311
  235.4 18.2 %collective-permute-start.18 = (bf16[64,3072]{1,0:T(8,128)(2,1)S(1)}, bf16[64,3072]{1,0:T(8,128)(2,1)S(1)}, u32[]{:S(2)}, u32[]{:S(2)}) collective-permute-start(bf16[64,3072]{1,0:T(8,128)(2,1)S(1)} %get-tuple-element.69), channel_id=1, source_target_pairs={{1,0},{2,1},{3,2},{0,3},{5,4},{6,5},{7,6},{4,7},{9,8},{10,9},{11,1... | collective-permute-start | bytes 1179656 | tf_op jit(solution)/shard_map/ppermute | solution.py:311
  236.9 25.1 %collective-permute-start.17 = (bf16[64,3072]{1,0:T(8,128)(2,1)S(1)}, bf16[64,3072]{1,0:T(8,128)(2,1)S(1)}, u32[]{:S(2)}, u32[]{:S(2)}) collective-permute-start(bf16[64,3072]{1,0:T(8,128)(2,1)S(1)} %get-tuple-element.70), channel_id=1, source_target_pairs={{1,0},{2,1},{3,2},{0,3},{5,4},{6,5},{7,6},{4,7},{9,8},{10,9},{11,1... | collective-permute-start | bytes 1179656 | tf_op jit(solution)/shard_map/ppermute | solution.py:311
  237.4 31.2 %collective-permute-start.16 = (bf16[64,3072]{1,0:T(8,128)(2,1)S(1)}, bf16[64,3072]{1,0:T(8,128)(2,1)S(1)}, u32[]{:S(2)}, u32[]{:S(2)}) collective-permute-start(bf16[64,3072]{1,0:T(8,128)(2,1)S(1)} %get-tuple-element.71), channel_id=1, source_target_pairs={{1,0},{2,1},{3,2},{0,3},{5,4},{6,5},{7,6},{4,7},{9,8},{10,9},{11,1... | collective-permute-start | bytes 1179656 | tf_op jit(solution)/shard_map/ppermute | solution.py:311
  (88 other events, 652.2 us)

commit v2 on v1

v2 whole, which is shorter than its diff:
```python
import functools
import math

import jax
import jax.numpy as jnp
from jax import lax
from jax.experimental import pallas as pl
from jax.experimental.pallas import tpu as pltpu
from jax.sharding import PartitionSpec as P

HEADS = 24
FEAT = 16
VDIM = 128
PACKED = 160
HALF = HEADS // 2
STEP_HEADS = 4
STEPS = HEADS // STEP_HEADS
STEP_LANES = STEP_HEADS * VDIM
HALF_STATE = HALF * PACKED
CHIPS = 16
PIECES = 4

EPSILON = 1e-06
SCORE_SCALE = 1.0 / math.sqrt(FEAT)
LINEAR_SCALE = FEAT ** (-0.25)
PAIR_SCALE = 1.0 / math.sqrt(2.0 * FEAT)

f32 = jnp.float32
bf16 = jnp.bfloat16


def dot(a, b, contract):
    return lax.dot_general(a, b, (contract, ((), ())), preferred_element_type=f32)


IN_HBM = pl.BlockSpec(memory_space=pltpu.HBM)
IN_SMEM = pl.BlockSpec(memory_space=pltpu.SMEM)


def params(micros, limit_mib=16):
    return dict(
        compiler_params=pltpu.CompilerParams(vmem_limit_bytes=limit_mib << 20),
        cost_estimate=pl.CostEstimate(flops=int(micros * 1.1e9), bytes_accessed=1 << 16, transcendentals=0),
    )


def shaped(*shapes):
    return [jax.ShapeDtypeStruct(dims, dtype) for dims, dtype in shapes]


def streamed(kernel, operands, out_shape, name, micros, scratch, copies, in_specs=None, limit_mib=62):
    return pl.pallas_call(
        kernel,
        in_specs=in_specs or [IN_HBM] * len(operands),
        out_specs=[IN_HBM] * len(out_shape),
        out_shape=shaped(*out_shape),
        scratch_shapes=[pltpu.VMEM(dims, dtype) for dims, dtype in scratch] + [pltpu.SemaphoreType.DMA((copies,))],
        name=name,
        **params(micros, limit_mib),
    )(*operands)


class Copies:
    def __init__(self, sems):
        self.sems, self.used = sems, 0

    def start(self, source, target):
        copy = pltpu.make_async_copy(source, target, self.sems.at[self.used])
        self.used += 1
        copy.start()
        return copy


def wait_all(copies):
    for copy in copies:
        copy.wait()


def rolled(block, distance):
    return pltpu.roll(block, distance % block.shape[0], 0)


def taylor_rows(cols, pair_weight):
    pieces = []
    for distance in range(FEAT // 2 + 1):
        if distance == 0:
            product = cols * cols * PAIR_SCALE
        else:
            product = cols * rolled(cols, -distance) * (PAIR_SCALE * pair_weight)
        pieces.append(product if distance < FEAT // 2 else product[: FEAT // 2])
    row = lax.broadcasted_iota(jnp.int32, (FEAT // 2, cols.shape[1]), 0)
    pieces.append(jnp.where(row == 0, 1.0, 0.0).astype(f32))
    pieces.append(cols * LINEAR_SCALE)
    return jnp.concatenate(pieces, axis=0).astype(bf16)


def taylor_back(cols, grad_rows, pair_weight):
    mixed = 2.0 * grad_rows[:FEAT] * cols
    for distance in range(1, FEAT // 2):
        part = grad_rows[FEAT * distance : FEAT * (distance + 1)]
        term = part * rolled(cols, -distance) + rolled(part * cols, distance)
        mixed = mixed + (term if pair_weight == 1.0 else pair_weight * term)
    half = FEAT // 2
    last = grad_rows[FEAT * half : FEAT * half + half]
    term = jnp.concatenate([last * cols[half:], last * cols[:half]], axis=0)
    mixed = mixed + (term if pair_weight == 1.0 else pair_weight * term)
    return grad_rows[PACKED - FEAT :] * LINEAR_SCALE + mixed * PAIR_SCALE


def head_of(index, size):
    return slice(index * size, (index + 1) * size)


def lanes_of(step):
    return slice(step * STEP_LANES, (step + 1) * STEP_LANES)


def half_rows(half):
    return pl.ds(pl.multiple_of(half * HALF_STATE, HALF_STATE), HALF_STATE)


def by_lanes(copies, source, target, steps=range(STEPS)):
    return [copies.start(source.at[:, lanes_of(step)], target.at[:, lanes_of(step)]) for step in steps]


def edge_kernel(x_hbm, gain_hbm, out_hbm, x_ref, gain_ref, out_ref, sems):
    copies = Copies(sems)
    rows = x_hbm.shape[0]
    wait_all([copies.start(x_hbm.at[rows - 16 : rows], x_ref), copies.start(gain_hbm, gain_ref)])
    x = x_ref[...].astype(f32)
    inv_rms = lax.rsqrt(jnp.mean(x * x, axis=1, keepdims=True) + EPSILON)
    out_ref[...] = (x * inv_rms * gain_ref[...]).astype(bf16)
    copies.start(out_ref, out_hbm).wait()


def edge_rows(x, gain):
    width = x.shape[1]
    edge = ((16, width), bf16)
    return streamed(edge_kernel, [x, gain], [edge], "edge", 1, [edge, ((1, width), f32), edge], 3)[0]


def state_kernel(
    core_ref,
    x_hbm,
    gain_hbm,
    query_hbm,
    key_hbm,
    before_hbm,
    taps_hbm,
    values_hbm,
    cols_hbm,
    own_hbm,
    away_hbm,
    x_ref,
    gain_ref,
    weight_ref,
    before_ref,
    taps_ref,
    normed_ref,
    values_ref,
    cols_ref,
    state_ref,
    sems,
):
    copies = Copies(sems)
    middle = query_hbm.shape[1]
    rows = x_ref.shape[0]
    first = [copies.start(x_hbm, x_ref), copies.start(gain_hbm, gain_ref)]
    weights = [
        copies.start(query_hbm, weight_ref.at[:, :middle]),
        copies.start(key_hbm, weight_ref.at[:, middle:]),
        copies.start(before_hbm, before_ref),
        copies.start(taps_hbm, taps_ref),
    ]
    wait_all(first)

    @pl.loop(0, rows // 16)
    def _(step):
        here = pl.ds(pl.multiple_of(step * 16, 16), 16)
        x = x_ref[here].astype(f32)
        inv_rms = lax.rsqrt(jnp.mean(x * x, axis=1, keepdims=True) + EPSILON)
        normed_ref[here] = (x * inv_rms * gain_ref[...]).astype(bf16)

    wait_all(weights)
    cols_ref[...] = dot(normed_ref[...], weight_ref[...], ((1,), (0,))).T.astype(bf16)
    out = [copies.start(cols_ref, cols_hbm)]
    edge = before_ref.shape[0]
    for step in range(STEPS):
        lanes = lanes_of(step)
        normed = normed_ref[:, lanes].astype(f32)
        before = before_ref[:, lanes].astype(f32)[edge - 8 :]
        row = lax.broadcasted_iota(jnp.int32, normed.shape, 0)
        one_back = jnp.where(row == 0, before[7:8], rolled(normed, 1))
        two_back = jnp.where(row == 0, before[6:7], rolled(one_back, 1))
        taps = taps_ref[:, lanes]
        values = (taps[0:1] * two_back + taps[1:2] * one_back + taps[2:3] * normed).astype(bf16)
        values_ref[:, lanes] = values
        out += by_lanes(copies, values_ref, values_hbm, [step])
        for head in range(STEP_HEADS):
            place = step * STEP_HEADS + head
            keys = cols_ref[middle + place * FEAT : middle + (place + 1) * FEAT].astype(f32)
            state = dot(taylor_rows(keys, 1.0), values[:, head_of(head, VDIM)], ((1,), (0,)))
            state_ref[head_of(place, PACKED)] = state.astype(bf16)
    core = core_ref[0]
    out.append(copies.start(state_ref.at[half_rows(1 - core)], away_hbm))
    out.append(copies.start(state_ref.at[half_rows(core)], own_hbm))
    wait_all(out)


def causal(rows):
    token = lax.broadcasted_iota(jnp.int32, (rows, rows), 0)
    other = lax.broadcasted_iota(jnp.int32, (rows, rows), 1)
    return token >= other, other >= token


def half_lanes(half):
    return slice(half * HALF * VDIM, (half + 1) * HALF * VDIM)


def inside_kernel(half, cols_hbm, values_hbm, inside_hbm, cols_ref, values_ref, inside_ref, sems):
    copies = Copies(sems)
    first = copies.start(cols_hbm, cols_ref)
    here = half_lanes(half)
    blocks = by_lanes(copies, values_hbm.at[:, here], values_ref, range(STEPS // 2))
    first.wait()
    middle, rows = cols_ref.shape[0] // 2, cols_ref.shape[1]
    mask, _ = causal(rows)
    out = []
    for step in range(STEPS // 2):
        blocks[step].wait()
        for head in range(STEP_HEADS):
            place = half * HALF + step * STEP_HEADS + head
            query = cols_ref[head_of(place, FEAT)]
            key = cols_ref[middle + place * FEAT : middle + (place + 1) * FEAT]
            scores = dot(query, key, ((0,), (0,))) * SCORE_SCALE
            weights = jnp.where(mask, 1.0 + scores + 0.5 * scores * scores, 0.0).astype(bf16)
            lanes = head_of(step * STEP_HEADS + head, VDIM)
            inside_ref[:, lanes] = dot(weights, values_ref[:, lanes], ((1,), (0,))).astype(bf16)
        out += by_lanes(copies, inside_ref, inside_hbm, [step])
    wait_all(out)


def states_in(copies, core, before_hbm, other_hbm, theirs_hbm, state_ref, other_ref):
    return [
        copies.start(before_hbm, state_ref.at[half_rows(core)]),
        copies.start(other_hbm, other_ref),
        copies.start(theirs_hbm, state_ref.at[half_rows(1 - core)]),
    ]


def state_of(place, adds_other, state_ref, other_ref):
    half, within = place // HALF, place % HALF
    state = state_ref[head_of(place, PACKED)]
    both = add_states(state, other_ref[head_of(within, PACKED)])
    return jnp.where(adds_other[half], both, state)


def head_mean(terms, ones):
    return dot(terms.astype(bf16), ones, ((1,), (0,))) * (1.0 / VDIM)


def output_kernel(
    core_ref,
    cols_hbm,
    inside_low_hbm,
    inside_high_hbm,
    before_hbm,
    other_hbm,
    theirs_hbm,
    x_hbm,
    grad_hbm,
    scale_hbm,
    out_hbm,
    numer_hbm,
    prefix_hbm,
    grad_own_hbm,
    grad_away_hbm,
    cols_ref,
    inside_ref,
    prefix_ref,
    other_ref,
    x_ref,
    grad_ref,
    scale_ref,
    out_ref,
    numer_ref,
    state_ref,
    sems,
):
    copies = Copies(sems)
    core = core_ref[0]
    middle = cols_ref.shape[0] // 2
    first = states_in(copies, core, before_hbm, other_hbm, theirs_hbm, prefix_ref, other_ref)
    first += [copies.start(cols_hbm.at[:middle], cols_ref.at[:middle]), copies.start(scale_hbm, scale_ref)]
    blocks = []
    for step in range(STEPS):
        source = inside_low_hbm if step < STEPS // 2 else inside_high_hbm
        blocks.append(
            [copies.start(source.at[:, lanes_of(step % (STEPS // 2))], inside_ref.at[:, lanes_of(step)])]
            + by_lanes(copies, x_hbm, x_ref, [step])
            + by_lanes(copies, grad_hbm, grad_ref, [step])
        )
    wait_all(first)
    adds_other = (False, core == 1)
    ones = jnp.ones((VDIM, VDIM), bf16)
    out = []
    for step in range(STEPS):
        wait_all(blocks[step])
        for head in range(STEP_HEADS):
            place = step * STEP_HEADS + head
            lanes = head_of(place, VDIM)
            feat = taylor_rows(cols_ref[head_of(place, FEAT)].astype(f32), 2.0)
            prefix = state_of(place, adds_other, prefix_ref, other_ref)
            prefix_ref[head_of(place, PACKED)] = prefix
            numer = inside_ref[:, lanes].astype(f32) + dot(feat, prefix, ((0,), (0,)))
            scale = scale_ref[:, lanes]
            grad = grad_ref[:, lanes].astype(f32) * scale
            inv = lax.rsqrt(head_mean(numer * numer, ones) + EPSILON)
            mean = head_mean(grad * numer, ones)
            out_ref[:, lanes] = (x_ref[:, lanes].astype(f32) + scale * (numer * inv)).astype(bf16)
            grad_numer = (inv * grad - numer * (inv * inv * inv * mean)).astype(bf16)
            numer_ref[:, lanes] = grad_numer
            state_ref[head_of(place, PACKED)] = dot(feat, grad_numer, ((1,), (0,))).astype(bf16)
        out += by_lanes(copies, out_ref, out_hbm, [step]) + by_lanes(copies, numer_ref, numer_hbm, [step])
    out.append(copies.start(state_ref.at[half_rows(1 - core)], grad_away_hbm))
    out.append(copies.start(state_ref.at[half_rows(core)], grad_own_hbm))
    out.append(copies.start(prefix_ref, prefix_hbm))
    wait_all(out)


def inside_back_kernel(
    half,
    cols_hbm,
    values_hbm,
    numer_hbm,
    prefix_hbm,
    grad_cols_hbm,
    grad_values_hbm,
    cols_ref,
    values_ref,
    numer_ref,
    prefix_ref,
    grad_cols_ref,
    grad_values_ref,
    sems,
):
    copies = Copies(sems)
    here = half_lanes(half)
    steps = range(STEPS // 2)
    first = [copies.start(cols_hbm, cols_ref)]
    state_rows = slice(half * HALF_STATE, (half + 1) * HALF_STATE)
    blocks = [
        by_lanes(copies, numer_hbm.at[:, here], numer_ref, [step])
        + by_lanes(copies, values_hbm.at[:, here], values_ref, [step])
        for step in steps
    ]
    first.append(copies.start(prefix_hbm.at[state_rows], prefix_ref))
    wait_all(first)
    middle, rows = cols_ref.shape[0] // 2, cols_ref.shape[1]
    mask, turned_mask = causal(rows)
    out = []
    for step in steps:
        wait_all(blocks[step])
        for head in range(STEP_HEADS):
            within = step * STEP_HEADS + head
            place = half * HALF + within
            lanes = head_of(within, VDIM)
            query = cols_ref[head_of(place, FEAT)]
            key = cols_ref[middle + place * FEAT : middle + (place + 1) * FEAT]
            grad_numer, values = numer_ref[:, lanes], values_ref[:, lanes]
            scores = dot(query, key, ((0,), (0,))) * SCORE_SCALE
            turned = dot(key, query, ((0,), (0,))) * SCORE_SCALE
            weights = jnp.where(turned_mask, 1.0 + turned + 0.5 * turned * turned, 0.0).astype(bf16)
            grad_values_ref[:, lanes] = dot(weights, grad_numer, ((1,), (0,))).astype(bf16)
            grad_weights = dot(grad_numer, values, ((1,), (1,)))
            grad_scores = jnp.where(mask, grad_weights * (1.0 + scores), 0.0).astype(bf16)
            grad_query = dot(key, grad_scores, ((1,), (1,))) * SCORE_SCALE
            grad_key = dot(query, grad_scores, ((1,), (0,))) * SCORE_SCALE
            grad_feat = dot(prefix_ref[head_of(within, PACKED)], grad_numer, ((1,), (1,)))
            grad_cols_ref[head_of(within, FEAT)] = grad_query + taylor_back(query.astype(f32), grad_feat, 2.0)
            grad_cols_ref[head_of(HALF + within, FEAT)] = grad_key
        out += by_lanes(copies, grad_values_ref, grad_values_hbm, [step])
    out.append(copies.start(grad_cols_ref, grad_cols_hbm))
    wait_all(out)


def late_kernel(
    core_ref,
    cols_hbm,
    values_hbm,
    before_hbm,
    other_hbm,
    theirs_hbm,
    cols_low_hbm,
    cols_high_hbm,
    values_low_hbm,
    values_high_hbm,
    query_hbm,
    key_hbm,
    taps_hbm,
    gain_hbm,
    x_hbm,
    grad_hbm,
    forward_hbm,
    *rest,
):
    edge_hbm, scaled_hbm, sums_hbm, forward_out_hbm = rest[:4]
    piece_hbms, rest = rest[4 : 3 + PIECES], rest[3 + PIECES :]
    (
        cols_ref,
        values_ref,
        state_ref,
        other_ref,
        grads_ref,
        early_ref,
        query_ref,
        key_ref,
        taps_ref,
        gain_ref,
        x_ref,
        grad_ref,
        grad_values_ref,
        turned_ref,
        scaled_ref,
        sums_ref,
        out_ref,
        edge_ref,
        forward_ref,
        sems,
    ) = rest
    copies = Copies(sems)
    core = core_ref[0]
    middle, rows = cols_ref.shape[0], cols_ref.shape[1]
    half_cols = middle // 2
    first = states_in(copies, core, before_hbm, other_hbm, theirs_hbm, state_ref, other_ref)
    first.append(copies.start(cols_hbm.at[middle:], cols_ref))
    for half, source in enumerate((cols_low_hbm, cols_high_hbm)):
        for kind in range(2):
            start = kind * middle + half * half_cols
            first.append(
                copies.start(
                    source.at[kind * half_cols : (kind + 1) * half_cols], grads_ref.at[start : start + half_cols]
                )
            )
    blocks = []
    for step in range(STEPS):
        source = values_low_hbm if step < STEPS // 2 else values_high_hbm
        blocks.append(
            by_lanes(copies, values_hbm, values_ref, [step])
            + [copies.start(source.at[:, lanes_of(step % (STEPS // 2))], early_ref.at[:, lanes_of(step)])]
        )
    weights = [copies.start(taps_hbm, taps_ref), copies.start(gain_hbm, gain_ref)]
    for step in range(STEPS):
        lanes = lanes_of(step)
        weights.append(copies.start(query_hbm.at[lanes], query_ref.at[lanes]))
        weights.append(copies.start(key_hbm.at[lanes], key_ref.at[lanes]))
    weights += [copies.start(x_hbm, x_ref), copies.start(grad_hbm, grad_ref)]
    forward_in = copies.start(forward_hbm, forward_ref)
    wait_all(first)
    adds_other = (core == 0, False)
    for step in range(STEPS):
        wait_all(blocks[step])
        for head in range(STEP_HEADS):
            place = step * STEP_HEADS + head
            lanes = head_of(place, VDIM)
            key = cols_ref[head_of(place, FEAT)].astype(f32)
            state = state_of(place, adds_other, state_ref, other_ref)
            grad_feat = dot(state, values_ref[:, lanes], ((1,), (1,)))
            key_rows = slice(middle + place * FEAT, middle + (place + 1) * FEAT)
            grads_ref[key_rows] = grads_ref[key_rows] + taylor_back(key, grad_feat, 1.0)
            late = dot(taylor_rows(key, 1.0), state, ((0,), (0,)))
            grad_values_ref[:, lanes] = early_ref[:, lanes].astype(f32) + late
    edge_ref[...] = grad_values_ref[:8]
    forward_in.wait()
    out = [copies.start(forward_ref, forward_out_hbm), copies.start(edge_ref, edge_hbm)]
    turned_ref[...] = grads_ref[...].T.astype(bf16)
    wait_all(weights)
    total = jnp.zeros((rows, VDIM), f32)
    squares = jnp.zeros((rows, VDIM), f32)
    for step in range(STEPS):
        lanes = lanes_of(step)
        grad_values = grad_values_ref[:, lanes]
        row = lax.broadcasted_iota(jnp.int32, grad_values.shape, 0)
        one_on = jnp.where(row == rows - 1, 0.0, rolled(grad_values, -1))
        two_on = jnp.where(row == rows - 1, 0.0, rolled(one_on, -1))
        grad_normed = dot(turned_ref[:, :middle], query_ref[lanes], ((1,), (1,)))
        grad_normed = grad_normed + dot(turned_ref[:, middle:], key_ref[lanes], ((1,), (1,)))
        taps = taps_ref[:, lanes]
        grad_normed = grad_normed + (taps[2:3] * grad_values + taps[1:2] * one_on + taps[0:1] * two_on)
        scaled = grad_normed * gain_ref[:, lanes]
        scaled_ref[:, lanes] = scaled
        x = x_ref[:, lanes].astype(f32)
        for head in range(STEP_HEADS):
            x_part, scaled_part = x[:, head_of(head, VDIM)], scaled[:, head_of(head, VDIM)]
            total = total + x_part * scaled_part
            squares = squares + x_part * x_part
    total = jnp.sum(total, axis=1, keepdims=True)
    squares = jnp.sum(squares, axis=1, keepdims=True)
    lane = lax.broadcasted_iota(jnp.int32, (rows, VDIM), 1)
    sums_ref[...] = jnp.where(lane == 0, total, jnp.where(lane == 1, squares, 0.0))
    cut = rows // PIECES
    tail = slice(rows - cut, rows)
    out += [copies.start(scaled_ref.at[tail], scaled_hbm), copies.start(sums_ref.at[tail], sums_hbm)]
    for piece in range(PIECES - 1):
        here = slice(piece * cut, (piece + 1) * cut)
        out_ref[here] = input_grad(scaled_ref[here], sums_ref[here], x_ref[here], grad_ref[here])
        out.append(copies.start(out_ref.at[here], piece_hbms[piece]))
    wait_all(out)


def input_grad(scaled, sums, x, grad):
    width = x.shape[1]
    inv = lax.rsqrt(sums[:, 1:2] / width + EPSILON)
    pull = inv * inv * inv * (sums[:, 0:1] / width)
    return (grad.astype(f32) + inv * scaled - x.astype(f32) * pull).astype(bf16)


def last_kernel(scaled_ref, sums_ref, x_ref, grad_ref, after_ref, taps_ref, gain_ref, out_ref):
    rows, width = x_ref.shape
    after = after_ref[...]
    row = lax.broadcasted_iota(jnp.int32, (rows, width), 0)
    upper = taps_ref[0:1] * after[0:1]
    lower = taps_ref[1:2] * after[0:1] + taps_ref[0:1] * after[1:2]
    extra = jnp.where(row == rows - 2, upper, jnp.where(row == rows - 1, lower, 0.0)) * gain_ref[...]
    with_x = jnp.sum(x_ref[...].astype(f32) * extra, axis=1, keepdims=True)
    lane = lax.broadcasted_iota(jnp.int32, sums_ref.shape, 1)
    sums = sums_ref[...] + jnp.where(lane == 0, with_x, 0.0)
    out_ref[...] = input_grad(scaled_ref[...] + extra, sums, x_ref[...], grad_ref[...])


def chip_sums_kernel(reverse, got_ref, out_ref):
    total = jnp.zeros(got_ref.shape[1:], f32)
    order = range(CHIPS - 1, -1, -1) if reverse else range(CHIPS)
    for chip in order:
        out_ref[chip] = total.astype(bf16)
        total = total + got_ref[chip].astype(f32)


def chip_sums(got, reverse):
    return pl.pallas_call(
        functools.partial(chip_sums_kernel, reverse),
        out_shape=jax.ShapeDtypeStruct(got.shape, bf16),
        name="chip_sums",
        **params(0.8),
    )(got)


def pair_sum_kernel(own_ref, other_ref, out_ref):
    rows = out_ref.shape[1]
    for chip in range(CHIPS):
        here = head_of(chip, rows)
        out_ref[chip] = add_states(own_ref[here], other_ref[here])


def pair_sum(own, other):
    return pl.pallas_call(
        pair_sum_kernel,
        out_shape=jax.ShapeDtypeStruct((CHIPS, own.shape[0] // CHIPS, VDIM), bf16),
        name="pair_sum",
        **params(0.5),
    )(own, other)


def join_kernel(*refs):
    *pieces, out_hbm, sems = refs
    copies = Copies(sems)
    rows = pieces[0].shape[0]
    wait_all([copies.start(piece, out_hbm.at[head_of(k, rows)]) for k, piece in enumerate(pieces)])


def joined(pieces):
    rows, width = pieces[0].shape
    anywhere = pl.BlockSpec(memory_space=pl.ANY)
    return pl.pallas_call(
        join_kernel,
        in_specs=[anywhere] * len(pieces),
        out_specs=anywhere,
        out_shape=jax.ShapeDtypeStruct((rows * len(pieces), width), bf16),
        scratch_shapes=[pltpu.SemaphoreType.DMA((len(pieces),))],
        name="join",
        **params(1),
    )(*pieces)


def core_swap(block):
    count = lax.axis_size("seq")
    return lax.ppermute(block, "seq", [(i, i ^ 1) for i in range(count)])


def over_chips(block):
    count = lax.axis_size("seq")
    groups = [list(range(core, count, 2)) for core in range(2)]
    return lax.all_to_all(block, "seq", 0, 0, tiled=True, axis_index_groups=groups)


def add_states(one, other):
    return (one.astype(f32) + other.astype(f32)).astype(bf16)


def scan_first(away, own):
    other = core_swap(away)
    return over_chips(pair_sum(own, other)), other


def scan_second(before, own, counts_own):
    before = before.reshape(own.shape)
    theirs = core_swap(jnp.where(counts_own, add_states(before, own), before))
    return before, theirs


def neighbour_rows(edge, distance):
    devices = range(lax.axis_size("seq"))
    route = [(i - distance, i) for i in devices if i - distance in devices]
    return lax.ppermute(edge, "seq", route)


def section_pass(block, distance):
    count = lax.axis_size("section")
    return lax.ppermute(block, "section", [((i - distance) % count, i) for i in range(count)])


def local(layer_in, norm_gain, conv_weight, query_weight, key_weight, out_gain, layer_grad):
    x, grad = layer_in[0], layer_grad[0]
    taps, query_proj, key_proj = conv_weight[0], query_weight[0], key_weight[0]
    rows, width = x.shape
    both = 2 * query_proj.shape[1]
    half_width = width // 2
    cut = rows // PIECES
    parity = lax.axis_index("seq") % 2
    core = parity.reshape(1).astype(jnp.int32)
    half_state = ((HALF_STATE, VDIM), bf16)
    all_state = ((2 * HALF_STATE, VDIM), bf16)
    tokens, tokens_wide = ((rows, width), bf16), ((rows, width), f32)
    cols_shape = ((both, rows), bf16)

    before_edge = neighbour_rows(edge_rows(x, norm_gain), 1)
    values, cols, own, away = streamed(
        state_kernel,
        [core, x, norm_gain, query_proj, key_proj, before_edge, taps],
        [tokens, cols_shape, half_state, half_state],
        "state",
        8,
        [tokens, ((1, width), f32), ((width, both), bf16), ((16, width), bf16), ((3, width), f32)]
        + [tokens, tokens, cols_shape, all_state],
        6 + 3 + STEPS,
        in_specs=[IN_SMEM] + [IN_HBM] * 6,
    )

    def inside(half, cols, values):
        shape = ((rows, half_width), bf16)
        return streamed(
            functools.partial(inside_kernel, half),
            [cols, values],
            [shape],
            "inside",
            3,
            [cols_shape, shape, shape],
            1 + STEPS,
        )[0]

    got, other = scan_first(away, own)
    got, inside_low = lax.optimization_barrier((got, inside(0, cols, values)))
    _, values_then = lax.optimization_barrier((got, values))
    before, inside_high = lax.optimization_barrier((over_chips(chip_sums(got, False)), inside(1, cols, values_then)))
    before, theirs = scan_second(before, own, parity == 0)
    output, numer, prefix, grad_own, grad_away = streamed(
        output_kernel,
        [core, cols, inside_low, inside_high, before, other, theirs, x, grad, out_gain],
        [tokens, tokens, all_state, half_state, half_state],
        "output",
        8,
        [cols_shape, tokens, all_state, half_state, tokens, tokens, ((1, width), f32), tokens, tokens, all_state],
        5 + 3 * STEPS + 2 * STEPS + 3,
        in_specs=[IN_SMEM] + [IN_HBM] * 9,
    )
    sent_forward = section_pass(output, 1)

    def inside_back(half, numer):
        shape = ((rows, half_width), bf16)
        grads = ((both // 2, rows), f32)
        return streamed(
            functools.partial(inside_back_kernel, half),
            [cols, values, numer, prefix],
            [grads, shape],
            "inside_back",
            5,
            [cols_shape, shape, shape, half_state, grads, shape],
            2 + 3 * (STEPS // 2) + 1,
        )

    got, grad_other = scan_first(grad_away, grad_own)
    got, low = lax.optimization_barrier((got, inside_back(0, numer)))
    _, numer_then = lax.optimization_barrier((got, numer))
    grad_before, high = lax.optimization_barrier((over_chips(chip_sums(got, True)), inside_back(1, numer_then)))
    grad_before, grad_theirs = scan_second(grad_before, grad_own, parity == 1)
    edge, scaled, sums, sent_forward, *pieces = streamed(
        late_kernel,
        [core, cols, values, grad_before, grad_other, grad_theirs, low[0], high[0], low[1], high[1]]
        + [query_proj, key_proj, taps, norm_gain, x, grad, sent_forward],
        [((8, width), f32), ((cut, width), f32), ((cut, VDIM), f32), tokens] + [((cut, width), bf16)] * (PIECES - 1),
        "late",
        9,
        [((both // 2, rows), bf16), tokens, all_state, half_state, ((both, rows), f32), tokens]
        + [((width, both // 2), bf16)] * 2
        + [((3, width), f32), ((1, width), f32), tokens, tokens, tokens_wide, ((rows, both), bf16), tokens_wide]
        + [((rows, VDIM), f32), tokens, ((8, width), f32), tokens],
        3 + 1 + 4 + 2 * STEPS + 2 + 2 * STEPS + 2 + 3 + 2 + PIECES - 1,
        in_specs=[IN_SMEM] + [IN_HBM] * 16,
    )
    after_edge = neighbour_rows(edge, -1)
    at_last = lambda: pl.BlockSpec((cut, width), lambda i: (PIECES - 1, 0))
    whole = lambda n, cols=width: pl.BlockSpec((n, cols), lambda i: (0, 0))
    pieces.append(
        pl.pallas_call(
            last_kernel,
            grid=(1,),
            in_specs=[whole(cut), whole(cut, VDIM), at_last(), at_last(), whole(8), whole(3), whole(1)],
            out_specs=whole(cut),
            out_shape=jax.ShapeDtypeStruct((cut, width), bf16),
            name="last",
            **params(1),
        )(scaled, sums, x, grad, after_edge, taps, norm_gain)
    )
    sent_backward = joined([section_pass(piece, -1) for piece in pieces])
    return (sent_forward[None], sent_backward[None])


def solution(mesh):
    return jax.shard_map(
        local,
        mesh=mesh,
        in_specs=(
            P("section", "seq", None),
            P("section", None),
            P("section", None, None),
            P("section", None, None),
            P("section", None, None),
            P("section", None),
            P("section", "seq", None),
        ),
        out_specs=(P("section", "seq", None), P("section", "seq", None)),
        check_vma=False,
    )
```

time: 274 us -> 162 us (0.59)
  starting transfers between devices: 100 us -> 37.2 us
  other arithmetic: 27.7 us -> 0.39 us
  waiting for transfers between devices: 75 us -> 54.9 us
  local copies, waits for them, and re-layouts: 27.6 us -> 8.56 us
  Pallas kernels: 39.9 us -> 58.6 us
    all_to_all x12 -> x4, starting transfers between devices: 61.4 us -> 19.3 us  [over_chips(): lax.all_to_all(block, 'seq', 0, 0, tiled=True, axis_index_groups=groups)]
    all_to_all x12 -> x4, waiting for transfers between devices: 40.1 us -> 17.9 us  [over_chips(): lax.all_to_all(block, 'seq', 0, 0, tiled=True, axis_index_groups=groups)]
    ppermute x12 -> x4, starting transfers between devices: 27.4 us -> 5.81 us  [core_swap(): return lax.ppermute(block, 'seq', [(i, i ^ 1) for i in range(count)])]
    pallas_call x17 -> x12, Pallas kernels: 36.2 us -> 56.9 us  [the longest x8 53.4 us: streamed(): pl.pallas_call(kernel, in_specs=in_specs or [IN_HBM] * len(operands), out...]
    unnamed x166 -> x37, local copies, waits for them, and re-layouts: 25.2 us -> 8.56 us
    select_n x12 -> x2, other arithmetic: 16.1 us -> 0.39 us  [scan_second(): theirs = core_swap(jnp.where(counts_own, add_states(before, own), before))]
    convert_element_type x6 -> x0, other arithmetic: 7.44 us -> none  [add_states(): return (one.astype(f32) + other.astype(f32)).astype(bf16)]
    ppermute x12 -> x4, waiting for transfers between devices: 0.03 us -> 3.96 us  [core_swap(): return lax.ppermute(block, 'seq', [(i, i ^ 1) for i in range(count)])]
  transfers between devices with their start and end apart: 31 -> 15, of which waited for: 16 -> 14; matrix products, arithmetic and copies ran while one was open for 11% -> 1% of each run, Pallas kernels for 13% -> 15%
where the time goes in v2:
time: 162 us; the launch traced here: 161 us
  Pallas kernels  58.6 us (36%)
  waiting for transfers between devices  54.9 us (34%)
  starting transfers between devices  37.2 us (23%)
  local copies, waits for them, and re-layouts  8.56 us (5%)
    pallas_call x8, Pallas kernels, streamed(): pl.pallas_call(kernel, in_specs=in_specs or [IN_HBM] * len(operands), out...  53.4 us
    ppermute x5, waiting for transfers between devices, section_pass(): lax.ppermute(block, 'section', [((i - distance) % count, i) for i in rang...  30.3 us
    all_to_all x4, starting transfers between devices, over_chips(): lax.all_to_all(block, 'seq', 0, 0, tiled=True, axis_index_groups=groups)  19.3 us
    all_to_all x4, waiting for transfers between devices, over_chips(): lax.all_to_all(block, 'seq', 0, 0, tiled=True, axis_index_groups=groups)  17.9 us
    unnamed x37, local copies, waits for them, and re-layouts  8.56 us
    ppermute x2, starting transfers between devices, neighbour_rows(): return lax.ppermute(edge, 'seq', route)  7.29 us
    ppermute x4, starting transfers between devices, core_swap(): return lax.ppermute(block, 'seq', [(i, i ^ 1) for i in range(count)])  5.81 us
    ppermute x5, starting transfers between devices, section_pass(): lax.ppermute(block, 'section', [((i - distance) % count, i) for i in rang...  4.79 us
  transfers between devices with their start and end apart: 15, of which 14 were waited for; matrix products, arithmetic and copies ran while one was open for 1% of the time, Pallas kernels for 15%

profile of v2, /device:TPU:1, one launch (start us, length us, event | category | flops | bytes accessed | tf_op | source)
XLA Modules:
  0.0 160.7 jit_solution(1051667485359825573)
XLA Ops:
  2.3 4.5 %collective-permute-start = (bf16[16,3072]{1,0:T(8,128)(2,1)}, bf16[16,3072]{1,0:T(8,128)(2,1)S(1)}, u32[]{:S(2)}, u32[]{:S(2)}) collective-permute-start(bf16[16,3072]{1,0:T(8,128)(2,1)} %edge.1), channel_id=1, source_target_pairs={{0,4},{4,8},{8,12},{12,16},{16,20},{20,24},{24,28},{28,32},{32,36}... | collective-permute-start | bytes 294920 | tf_op jit(solution)/shard_map/ppermute | solution.py:614
  9.4 8.6 %state.1 = (bf16[256,3072]{1,0:T(8,128)(2,1)}, bf16[768,256]{1,0:T(8,128)(2,1)}, bf16[1920,128]{1,0:T(8,128)(2,1)}, bf16[1920,128]{1,0:T(8,128)(2,1)}) custom-call(s32[1]{0:T(128)} %bitcast.core_ref, bf16[256,3072]{1,0:T(8,128)(2,1)} %bitcast.15, f32[1,3072]{1,0:T(1,128)} %gain_ref.1, bf16[3072,384]{1,0:T(8,128)(2,1)} %bitcast.27, ...), custom_call_target="tpu_custom_call" | custom-call | flops 8800000000 | bytes 65536 | tf_op jit(solution)/shard_map/state/pallas_call | solution.py:52
  22.3 8.4 %all-to-all-start = ((bf16[16,120,128]{2,1,0:T(8,128)(2,1)}), bf16[16,120,128]{2,1,0:T(8,128)(2,1)S(1)}, u32[]{:S(2)}, u32[]{:S(2)}) async-start(bf16[16,120,128]{2,1,0:T(8,128)(2,1)} %pair_sum.2), calls=%async_computation | async-start | bytes 983040 | tf_op jit(solution)/shard_map/all_to_all | solution.py:593
  30.7 3.7 %inside.2.inside_low_hbm = bf16[256,1536]{1,0:T(8,128)(2,1)} custom-call(bf16[768,256]{1,0:T(8,128)(2,1)} %get-tuple-element.34.cols_hbm, bf16[256,3072]{1,0:T(8,128)(2,1)} %get-tuple-element.40.values_hbm), custom_call_target="tpu_custom_call" | custom-call | flops 3300000000 | bytes 65536 | tf_op jit(solution)/shard_map/inside/pallas_call | solution.py:52
  34.4 6.7 %all-to-all-done.got_ref = bf16[16,120,128]{2,1,0:T(8,128)(2,1)S(1)} async-done(((bf16[16,120,128]{2,1,0:T(8,128)(2,1)}), bf16[16,120,128]{2,1,0:T(8,128)(2,1)S(1)}, u32[]{:S(2)}, u32[]{:S(2)}) %all-to-all-start) | async-done | bytes 491552 | tf_op jit(solution)/shard_map/all_to_all | solution.py:593
  41.9 3.6 %all-to-all-start.1 = ((bf16[16,120,128]{2,1,0:T(8,128)(2,1)}), bf16[16,120,128]{2,1,0:T(8,128)(2,1)S(1)}, u32[]{:S(2)}, u32[]{:S(2)}) async-start(bf16[16,120,128]{2,1,0:T(8,128)(2,1)} %chip_sums.2), calls=%async_computation.1 | async-start | bytes 983040 | tf_op jit(solution)/shard_map/all_to_all | solution.py:593
  45.5 3.7 %inside.3.inside_high_hbm = bf16[256,1536]{1,0:T(8,128)(2,1)} custom-call(bf16[768,256]{1,0:T(8,128)(2,1)} %get-tuple-element.34.cols_hbm, bf16[256,3072]{1,0:T(8,128)(2,1)} %get-tuple-element.40.values_hbm), custom_call_target="tpu_custom_call" | custom-call | flops 3300000000 | bytes 65536 | tf_op jit(solution)/shard_map/inside/pallas_call | solution.py:52
  49.2 5.7 %all-to-all-done.1 = bf16[16,120,128]{2,1,0:T(8,128)(2,1)S(1)} async-done(((bf16[16,120,128]{2,1,0:T(8,128)(2,1)}), bf16[16,120,128]{2,1,0:T(8,128)(2,1)S(1)}, u32[]{:S(2)}, u32[]{:S(2)}) %all-to-all-start.1) | async-done | bytes 491552 | tf_op jit(solution)/shard_map/all_to_all | solution.py:593
  55.2 2.9 %collective-permute-start.2 = (bf16[1920,128]{1,0:T(8,128)(2,1)S(1)}, bf16[1920,128]{1,0:T(8,128)(2,1)S(1)}, u32[]{:S(2)}, u32[]{:S(2)}) collective-permute-start(bf16[1920,128]{1,0:T(8,128)(2,1)S(1)} %fusion), channel_id=1, source_target_pairs={{0,4},{4,0},{8,12},{12,8},{16,20},{20,16},{24,28},{28,24},{32,36},... | collective-permute-start | bytes 1474568 | tf_op jit(solution)/shard_map/ppermute | solution.py:587
  60.4 11.0 %output.1 = (bf16[256,3072]{1,0:T(8,128)(2,1)}, bf16[256,3072]{1,0:T(8,128)(2,1)}, bf16[3840,128]{1,0:T(8,128)(2,1)}, bf16[1920,128]{1,0:T(8,128)(2,1)}, bf16[1920,128]{1,0:T(8,128)(2,1)}) custom-call(s32[1]{0:T(128)} %bitcast.core_ref, bf16[768,256]{1,0:T(8,128)(2,1)} %get-tuple-element.34.cols_hbm, bf16[256,1536]{1,0:T(8,128)(2,1)} %inside.2.inside_low_hbm, ...), custom_call_target="tpu_custom_call" | custom-call | flops 8800000000 | bytes 65536 | tf_op jit(solution)/shard_map/output/pallas_call | solution.py:52
  75.6 3.6 %all-to-all-start.2 = ((bf16[16,120,128]{2,1,0:T(8,128)(2,1)}), bf16[16,120,128]{2,1,0:T(8,128)(2,1)S(1)}, u32[]{:S(2)}, u32[]{:S(2)}) async-start(bf16[16,120,128]{2,1,0:T(8,128)(2,1)} %pair_sum.3), calls=%async_computation.2 | async-start | bytes 983040 | tf_op jit(solution)/shard_map/all_to_all | solution.py:593
  79.2 7.4 %inside_back.2 = (f32[384,256]{1,0:T(8,128)}, bf16[256,1536]{1,0:T(8,128)(2,1)}) custom-call(bf16[768,256]{1,0:T(8,128)(2,1)} %get-tuple-element.34.cols_hbm, bf16[256,3072]{1,0:T(8,128)(2,1)} %get-tuple-element.40.values_hbm, bf16[256,3072]{1,0:T(8,128)(2,1)} %get-tuple-element.50.numer_hbm, bf16[3840,128]{1,0:T(8,128)(2,1)} %get-tuple-element.46.prefix_hbm), custom_call_target="tpu_custom_call" | custom-call | flops 5500000256 | bytes 65536 | tf_op jit(solution)/shard_map/inside_back/pallas_call | solution.py:52
  86.6 3.2 %all-to-all-done.2.got_ref = bf16[16,120,128]{2,1,0:T(8,128)(2,1)S(1)} async-done(((bf16[16,120,128]{2,1,0:T(8,128)(2,1)}), bf16[16,120,128]{2,1,0:T(8,128)(2,1)S(1)}, u32[]{:S(2)}, u32[]{:S(2)}) %all-to-all-start.2) | async-done | bytes 491552 | tf_op jit(solution)/shard_map/all_to_all | solution.py:593
  90.7 3.8 %all-to-all-start.3 = ((bf16[16,120,128]{2,1,0:T(8,128)(2,1)}), bf16[16,120,128]{2,1,0:T(8,128)(2,1)S(1)}, u32[]{:S(2)}, u32[]{:S(2)}) async-start(bf16[16,120,128]{2,1,0:T(8,128)(2,1)} %chip_sums.3), calls=%async_computation.3 | async-start | bytes 983040 | tf_op jit(solution)/shard_map/all_to_all | solution.py:593
  94.5 7.4 %inside_back.3 = (f32[384,256]{1,0:T(8,128)}, bf16[256,1536]{1,0:T(8,128)(2,1)}) custom-call(bf16[768,256]{1,0:T(8,128)(2,1)} %get-tuple-element.34.cols_hbm, bf16[256,3072]{1,0:T(8,128)(2,1)} %get-tuple-element.40.values_hbm, bf16[256,3072]{1,0:T(8,128)(2,1)} %get-tuple-element.50.numer_hbm, bf16[3840,128]{1,0:T(8,128)(2,1)} %get-tuple-element.46.prefix_hbm), custom_call_target="tpu_custom_call" | custom-call | flops 5500000256 | bytes 65536 | tf_op jit(solution)/shard_map/inside_back/pallas_call | solution.py:52
  101.9 2.2 %all-to-all-done.3 = bf16[16,120,128]{2,1,0:T(8,128)(2,1)S(1)} async-done(((bf16[16,120,128]{2,1,0:T(8,128)(2,1)}), bf16[16,120,128]{2,1,0:T(8,128)(2,1)S(1)}, u32[]{:S(2)}, u32[]{:S(2)}) %all-to-all-start.3) | async-done | bytes 491552 | tf_op jit(solution)/shard_map/all_to_all | solution.py:593
  104.3 2.4 %collective-permute-start.4 = (bf16[1920,128]{1,0:T(8,128)(2,1)S(1)}, bf16[1920,128]{1,0:T(8,128)(2,1)S(1)}, u32[]{:S(2)}, u32[]{:S(2)}) collective-permute-start(bf16[1920,128]{1,0:T(8,128)(2,1)S(1)} %fusion.1), channel_id=1, source_target_pairs={{0,4},{4,0},{8,12},{12,8},{16,20},{20,16},{24,28},{28,24},{32,36},... | collective-permute-start | bytes 1474568 | tf_op jit(solution)/shard_map/ppermute | solution.py:587
  106.6 2.7 %collective-permute-done.5.forward_hbm = bf16[256,3072]{1,0:T(8,128)(2,1)} collective-permute-done((bf16[256,3072]{1,0:T(8,128)(2,1)}, bf16[256,3072]{1,0:T(8,128)(2,1)}, u32[]{:S(2)}, u32[]{:S(2)}) %collective-permute-start.5) | collective-permute-done | bytes 1572896 | tf_op jit(solution)/shard_map/ppermute | solution.py:619
  110.1 10.1 %late.1 = (f32[8,3072]{1,0:T(8,128)}, f32[64,3072]{1,0:T(8,128)}, f32[64,128]{1,0:T(8,128)}, bf16[256,3072]{1,0:T(8,128)(2,1)}, bf16[64,3072]{1,0:T(8,128)(2,1)}...) custom-call(s32[1]{0:T(128)} %bitcast.core_ref, bf16[768,256]{1,0:T(8,128)(2,1)} %get-tuple-element.34.cols_hbm, ...), custom_call_target="tpu_custom_call" | custom-call | flops 9900000256 | bytes 65536 | tf_op jit(solution)/shard_map/late/pallas_call | solution.py:52
  120.2 2.8 %collective-permute-start.9 = (f32[8,3072]{1,0:T(8,128)}, f32[8,3072]{1,0:T(8,128)S(1)}, u32[]{:S(2)}, u32[]{:S(2)}) collective-permute-start(f32[8,3072]{1,0:T(8,128)} %get-tuple-element.65), channel_id=1, source_target_pairs={{4,0},{8,4},{12,8},{16,12},{20,16},{24,20},{28,24},{32,28},{36,32}... | collective-permute-start | bytes 294920 | tf_op jit(solution)/shard_map/ppermute | solution.py:614
  131.8 2.6 %collective-permute-done.6.refs_0_ = bf16[64,3072]{1,0:T(8,128)(2,1)S(1)} collective-permute-done((bf16[64,3072]{1,0:T(8,128)(2,1)}, bf16[64,3072]{1,0:T(8,128)(2,1)S(1)}, u32[]{:S(2)}, u32[]{:S(2)}) %collective-permute-start.6) | collective-permute-done | bytes 393248 | tf_op jit(solution)/shard_map/ppermute | solution.py:619
  134.4 8.4 %collective-permute-done.7.refs_1_ = bf16[64,3072]{1,0:T(8,128)(2,1)S(1)} collective-permute-done((bf16[64,3072]{1,0:T(8,128)(2,1)}, bf16[64,3072]{1,0:T(8,128)(2,1)S(1)}, u32[]{:S(2)}, u32[]{:S(2)}) %collective-permute-start.7) | collective-permute-done | bytes 393248 | tf_op jit(solution)/shard_map/ppermute | solution.py:619
  142.8 8.4 %collective-permute-done.8.refs_2_ = bf16[64,3072]{1,0:T(8,128)(2,1)S(1)} collective-permute-done((bf16[64,3072]{1,0:T(8,128)(2,1)}, bf16[64,3072]{1,0:T(8,128)(2,1)S(1)}, u32[]{:S(2)}, u32[]{:S(2)}) %collective-permute-start.8) | collective-permute-done | bytes 393248 | tf_op jit(solution)/shard_map/ppermute | solution.py:619
  151.3 8.1 %collective-permute-done.10.refs_3_ = bf16[64,3072]{1,0:T(8,128)(2,1)S(1)} collective-permute-done((bf16[64,3072]{1,0:T(8,128)(2,1)S(1)}, bf16[64,3072]{1,0:T(8,128)(2,1)S(1)}, u32[]{:S(2)}, u32[]{:S(2)}) %collective-permute-start.10) | collective-permute-done | bytes 393248 | tf_op jit(solution)/shard_map/ppermute | solution.py:619
  (59 shorter events, 27.9 us)
Async XLA Ops:
  0.6 6.2 %copy-start.14 = (f32[1,3,3072]{2,0,1:T(1,128)S(1)}, f32[1,3,3072]{2,0,1:T(1,128)}, u32[]{:S(2)}) copy-start(f32[1,3,3072]{2,0,1:T(1,128)} %param.9) | copy-start | bytes 110596
  2.3 6.5 %collective-permute-start = (bf16[16,3072]{1,0:T(8,128)(2,1)}, bf16[16,3072]{1,0:T(8,128)(2,1)S(1)}, u32[]{:S(2)}, u32[]{:S(2)}) collective-permute-start(bf16[16,3072]{1,0:T(8,128)(2,1)} %edge.1), channel_id=1, source_target_pairs={{0,4},{4,8},{8,12},{12,16},{16,20},{20,24},{24,28},{28,32},{32,36}... | collective-permute-start | bytes 294920 | tf_op jit(solution)/shard_map/ppermute | solution.py:614
  18.0 2.2 %collective-permute-start.1 = (bf16[1920,128]{1,0:T(8,128)(2,1)}, bf16[1920,128]{1,0:T(8,128)(2,1)S(1)}, u32[]{:S(2)}, u32[]{:S(2)}) collective-permute-start(bf16[1920,128]{1,0:T(8,128)(2,1)} %get-tuple-element.37), channel_id=1, source_target_pairs={{0,4},{4,0},{8,12},{12,8},{16,20},{20,16},{24,28},{28,24},{32,36},... | collective-permute-start | bytes 1474568 | tf_op jit(solution)/shard_map/ppermute | solution.py:587
  20.1 14.2 %copy-start.11 = (bf16[1920,128]{1,0:T(8,128)(2,1)}, bf16[1920,128]{1,0:T(8,128)(2,1)S(1)}, u32[]{:S(2)}) copy-start(bf16[1920,128]{1,0:T(8,128)(2,1)S(1)} %collective-permute-done.1.other_ref.other_hbm) | copy-start | bytes 1474564
  22.3 18.8 %all-to-all-start = ((bf16[16,120,128]{2,1,0:T(8,128)(2,1)}), bf16[16,120,128]{2,1,0:T(8,128)(2,1)S(1)}, u32[]{:S(2)}, u32[]{:S(2)}) async-start(bf16[16,120,128]{2,1,0:T(8,128)(2,1)} %pair_sum.2), calls=%async_computation | async-start | bytes 983040 | tf_op jit(solution)/shard_map/all_to_all | solution.py:593
  41.9 13.1 %all-to-all-start.1 = ((bf16[16,120,128]{2,1,0:T(8,128)(2,1)}), bf16[16,120,128]{2,1,0:T(8,128)(2,1)S(1)}, u32[]{:S(2)}, u32[]{:S(2)}) async-start(bf16[16,120,128]{2,1,0:T(8,128)(2,1)} %chip_sums.2), calls=%async_computation.1 | async-start | bytes 983040 | tf_op jit(solution)/shard_map/all_to_all | solution.py:593
  45.5 9.5 %copy-start.6 = (bf16[1920,128]{1,0:T(8,128)(2,1)S(1)}, bf16[1920,128]{1,0:T(8,128)(2,1)}, u32[]{:S(2)}) copy-start(bf16[1920,128]{1,0:T(8,128)(2,1)} %get-tuple-element.36.own_ref) | copy-start | bytes 1474564
  55.0 4.6 %copy-start.13 = (bf16[16,120,128]{2,1,0:T(8,128)(2,1)}, bf16[16,120,128]{2,1,0:T(8,128)(2,1)S(1)}, u32[]{:S(2)}) copy-start(bf16[16,120,128]{2,1,0:T(8,128)(2,1)S(1)} %all-to-all-done.1) | copy-start | bytes 1474564
  55.2 4.4 %collective-permute-start.2 = (bf16[1920,128]{1,0:T(8,128)(2,1)S(1)}, bf16[1920,128]{1,0:T(8,128)(2,1)S(1)}, u32[]{:S(2)}, u32[]{:S(2)}) collective-permute-start(bf16[1920,128]{1,0:T(8,128)(2,1)S(1)} %fusion), channel_id=1, source_target_pairs={{0,4},{4,0},{8,12},{12,8},{16,20},{20,16},{24,28},{28,24},{32,36},... | collective-permute-start | bytes 1474568 | tf_op jit(solution)/shard_map/ppermute | solution.py:587
  71.4 2.2 %collective-permute-start.3 = (bf16[1920,128]{1,0:T(8,128)(2,1)}, bf16[1920,128]{1,0:T(8,128)(2,1)S(1)}, u32[]{:S(2)}, u32[]{:S(2)}) collective-permute-start(bf16[1920,128]{1,0:T(8,128)(2,1)} %get-tuple-element.44), channel_id=1, source_target_pairs={{0,4},{4,0},{8,12},{12,8},{16,20},{20,16},{24,28},{28,24},{32,36},... | collective-permute-start | bytes 1474568 | tf_op jit(solution)/shard_map/ppermute | solution.py:587
  71.8 37.5 %collective-permute-start.5 = (bf16[256,3072]{1,0:T(8,128)(2,1)}, bf16[256,3072]{1,0:T(8,128)(2,1)}, u32[]{:S(2)}, u32[]{:S(2)}) collective-permute-start(bf16[256,3072]{1,0:T(8,128)(2,1)} %get-tuple-element.58), channel_id=1, source_target_pairs={{3,0},{0,1},{1,2},{2,3},{7,4},{4,5},{5,6},{6,7},{11,8},{8,9},{9,10... | collective-permute-start | bytes 4718600 | tf_op jit(solution)/shard_map/ppermute | solution.py:619
  75.6 14.2 %all-to-all-start.2 = ((bf16[16,120,128]{2,1,0:T(8,128)(2,1)}), bf16[16,120,128]{2,1,0:T(8,128)(2,1)S(1)}, u32[]{:S(2)}, u32[]{:S(2)}) async-start(bf16[16,120,128]{2,1,0:T(8,128)(2,1)} %pair_sum.3), calls=%async_computation.2 | async-start | bytes 983040 | tf_op jit(solution)/shard_map/all_to_all | solution.py:593
  90.7 13.4 %all-to-all-start.3 = ((bf16[16,120,128]{2,1,0:T(8,128)(2,1)}), bf16[16,120,128]{2,1,0:T(8,128)(2,1)S(1)}, u32[]{:S(2)}, u32[]{:S(2)}) async-start(bf16[16,120,128]{2,1,0:T(8,128)(2,1)} %chip_sums.3), calls=%async_computation.3 | async-start | bytes 983040 | tf_op jit(solution)/shard_map/all_to_all | solution.py:593
  94.5 9.6 %copy-start.4 = (bf16[1920,128]{1,0:T(8,128)(2,1)S(1)}, bf16[1920,128]{1,0:T(8,128)(2,1)}, u32[]{:S(2)}) copy-start(bf16[1920,128]{1,0:T(8,128)(2,1)} %get-tuple-element.43.own_ref) | copy-start | bytes 1474564
  104.1 5.2 %copy-start.12 = (bf16[16,120,128]{2,1,0:T(8,128)(2,1)}, bf16[16,120,128]{2,1,0:T(8,128)(2,1)S(1)}, u32[]{:S(2)}) copy-start(bf16[16,120,128]{2,1,0:T(8,128)(2,1)S(1)} %all-to-all-done.3) | copy-start | bytes 1474564
  104.3 5.0 %collective-permute-start.4 = (bf16[1920,128]{1,0:T(8,128)(2,1)S(1)}, bf16[1920,128]{1,0:T(8,128)(2,1)S(1)}, u32[]{:S(2)}, u32[]{:S(2)}) collective-permute-start(bf16[1920,128]{1,0:T(8,128)(2,1)S(1)} %fusion.1), channel_id=1, source_target_pairs={{0,4},{4,0},{8,12},{12,8},{16,20},{20,16},{24,28},{28,24},{32,36},... | collective-permute-start | bytes 1474568 | tf_op jit(solution)/shard_map/ppermute | solution.py:587
  110.1 16.6 %copy-start = (bf16[1,256,3072]{2,1,0:T(8,128)(2,1)S(1)}, bf16[1,256,3072]{2,1,0:T(8,128)(2,1)}, u32[]{:S(2)}) copy-start(bf16[1,256,3072]{2,1,0:T(8,128)(2,1)} %param.7) | copy-start | bytes 4718596
  110.1 16.6 %copy-start.7 = (f32[1,3,3072]{2,1,0:T(4,128)S(1)}, f32[1,3,3072]{2,1,0:T(4,128)}, u32[]{:S(2)}) copy-start(f32[1,3,3072]{2,1,0:T(4,128)} %copy.11) | copy-start | bytes 110596
  110.1 16.6 %copy-start.9 = (f32[1,3072]{1,0:T(1,128)S(1)}, f32[1,3072]{1,0:T(1,128)}, u32[]{:S(2)}) copy-start(f32[1,3072]{1,0:T(1,128)} %gain_ref.1) | copy-start | bytes 36868
  120.2 6.4 %collective-permute-start.9 = (f32[8,3072]{1,0:T(8,128)}, f32[8,3072]{1,0:T(8,128)S(1)}, u32[]{:S(2)}, u32[]{:S(2)}) collective-permute-start(f32[8,3072]{1,0:T(8,128)} %get-tuple-element.65), channel_id=1, source_target_pairs={{4,0},{8,4},{12,8},{16,12},{20,16},{24,20},{28,24},{32,28},{36,32}... | collective-permute-start | bytes 294920 | tf_op jit(solution)/shard_map/ppermute | solution.py:614
  123.0 11.4 %collective-permute-start.6 = (bf16[64,3072]{1,0:T(8,128)(2,1)}, bf16[64,3072]{1,0:T(8,128)(2,1)S(1)}, u32[]{:S(2)}, u32[]{:S(2)}) collective-permute-start(bf16[64,3072]{1,0:T(8,128)(2,1)} %get-tuple-element.60), channel_id=1, source_target_pairs={{1,0},{2,1},{3,2},{0,3},{5,4},{6,5},{7,6},{4,7},{9,8},{10,9},{11,1... | collective-permute-start | bytes 1179656 | tf_op jit(solution)/shard_map/ppermute | solution.py:619
  124.6 18.3 %collective-permute-start.7 = (bf16[64,3072]{1,0:T(8,128)(2,1)}, bf16[64,3072]{1,0:T(8,128)(2,1)S(1)}, u32[]{:S(2)}, u32[]{:S(2)}) collective-permute-start(bf16[64,3072]{1,0:T(8,128)(2,1)} %get-tuple-element.61), channel_id=1, source_target_pairs={{1,0},{2,1},{3,2},{0,3},{5,4},{6,5},{7,6},{4,7},{9,8},{10,9},{11,1... | collective-permute-start | bytes 1179656 | tf_op jit(solution)/shard_map/ppermute | solution.py:619
  125.0 26.2 %collective-permute-start.8 = (bf16[64,3072]{1,0:T(8,128)(2,1)}, bf16[64,3072]{1,0:T(8,128)(2,1)S(1)}, u32[]{:S(2)}, u32[]{:S(2)}) collective-permute-start(bf16[64,3072]{1,0:T(8,128)(2,1)} %get-tuple-element.62), channel_id=1, source_target_pairs={{1,0},{2,1},{3,2},{0,3},{5,4},{6,5},{7,6},{4,7},{9,8},{10,9},{11,1... | collective-permute-start | bytes 1179656 | tf_op jit(solution)/shard_map/ppermute | solution.py:619
  130.4 28.9 %collective-permute-start.10 = (bf16[64,3072]{1,0:T(8,128)(2,1)S(1)}, bf16[64,3072]{1,0:T(8,128)(2,1)S(1)}, u32[]{:S(2)}, u32[]{:S(2)}) collective-permute-start(bf16[64,3072]{1,0:T(8,128)(2,1)S(1)} %last.1), channel_id=1, source_target_pairs={{1,0},{2,1},{3,2},{0,3},{5,4},{6,5},{7,6},{4,7},{9,8},{10,9},{11,1... | collective-permute-start | bytes 1179656 | tf_op jit(solution)/shard_map/ppermute | solution.py:619
  (9 other events, 10.1 us)

commit v3 on v2

--- a/solution.py
+++ b/solution.py
@@ -34,7 +34,6 @@
 
 
 IN_HBM = pl.BlockSpec(memory_space=pltpu.HBM)
-IN_SMEM = pl.BlockSpec(memory_space=pltpu.SMEM)
 
 
 def params(micros, limit_mib=16):
@@ -48,10 +47,10 @@
     return [jax.ShapeDtypeStruct(dims, dtype) for dims, dtype in shapes]
 
 
-def streamed(kernel, operands, out_shape, name, micros, scratch, copies, in_specs=None, limit_mib=62):
+def streamed(kernel, operands, out_shape, name, micros, scratch, copies, limit_mib=62):
     return pl.pallas_call(
         kernel,
-        in_specs=in_specs or [IN_HBM] * len(operands),
+        in_specs=[IN_HBM] * len(operands),
         out_specs=[IN_HBM] * len(out_shape),
         out_shape=shaped(*out_shape),
         scratch_shapes=[pltpu.VMEM(dims, dtype) for dims, dtype in scratch] + [pltpu.SemaphoreType.DMA((copies,))],
@@ -64,9 +63,15 @@
     def __init__(self, sems):
         self.sems, self.used = sems, 0
 
+    def make(self, source, target):
+        self.used += 1
+        return pltpu.make_async_copy(source, target, self.last())
+
+    def last(self):
+        return self.sems.at[self.used - 1]
+
     def start(self, source, target):
-        copy = pltpu.make_async_copy(source, target, self.sems.at[self.used])
-        self.used += 1
+        copy = self.make(source, target)
         copy.start()
         return copy
 
@@ -111,6 +116,10 @@
     return slice(index * size, (index + 1) * size)
 
 
+def core_here():
+    return lax.rem(lax.axis_index("seq"), 2)
+
+
 def lanes_of(step):
     return slice(step * STEP_LANES, (step + 1) * STEP_LANES)
 
@@ -123,24 +132,19 @@
     return [copies.start(source.at[:, lanes_of(step)], target.at[:, lanes_of(step)]) for step in steps]
 
 
-def edge_kernel(x_hbm, gain_hbm, out_hbm, x_ref, gain_ref, out_ref, sems):
-    copies = Copies(sems)
-    rows = x_hbm.shape[0]
-    wait_all([copies.start(x_hbm.at[rows - 16 : rows], x_ref), copies.start(gain_hbm, gain_ref)])
-    x = x_ref[...].astype(f32)
-    inv_rms = lax.rsqrt(jnp.mean(x * x, axis=1, keepdims=True) + EPSILON)
-    out_ref[...] = (x * inv_rms * gain_ref[...]).astype(bf16)
-    copies.start(out_ref, out_hbm).wait()
-
-
-def edge_rows(x, gain):
-    width = x.shape[1]
-    edge = ((16, width), bf16)
-    return streamed(edge_kernel, [x, gain], [edge], "edge", 1, [edge, ((1, width), f32), edge], 3)[0]
+def state_out(copies, core, step, state_ref, own_hbm, away_hbm):
+    rows = STEP_HEADS * PACKED
+    source = state_ref.at[head_of(step, rows)]
+    here = head_of(step % (STEPS // 2), rows)
+    is_own = core == step // (STEPS // 2)
+    to_own = copies.make(source, own_hbm.at[here])
+    to_away = pltpu.make_async_copy(source, away_hbm.at[here], copies.last())
+    pl.when(is_own)(to_own.start)
+    pl.when(jnp.logical_not(is_own))(to_away.start)
+    return to_own
 
 
 def state_kernel(
-    core_ref,
     x_hbm,
     gain_hbm,
     query_hbm,
@@ -166,25 +170,29 @@
     middle = query_hbm.shape[1]
     rows = x_ref.shape[0]
     first = [copies.start(x_hbm, x_ref), copies.start(gain_hbm, gain_ref)]
-    weights = [
-        copies.start(query_hbm, weight_ref.at[:, :middle]),
-        copies.start(key_hbm, weight_ref.at[:, middle:]),
-        copies.start(before_hbm, before_ref),
-        copies.start(taps_hbm, taps_ref),
-    ]
+    small = [copies.start(before_hbm, before_ref), copies.start(taps_hbm, taps_ref)]
+    weights = []
+    for step in range(STEPS):
+        here = lanes_of(step)
+        to_query = copies.start(query_hbm.at[here], weight_ref.at[here, :middle])
+        weights.append([to_query, copies.start(key_hbm.at[here], weight_ref.at[here, middle:])])
     wait_all(first)
 
-    @pl.loop(0, rows // 16)
+    def normed_rows(x):
+        x = x.astype(f32)
+        inv_rms = lax.rsqrt(jnp.mean(x * x, axis=1, keepdims=True) + EPSILON)
+        return (x * inv_rms * gain_ref[...]).astype(bf16)
+
+    @pl.loop(0, rows // 16, unroll=4)
     def _(step):
         here = pl.ds(pl.multiple_of(step * 16, 16), 16)
-        x = x_ref[here].astype(f32)
-        inv_rms = lax.rsqrt(jnp.mean(x * x, axis=1, keepdims=True) + EPSILON)
-        normed_ref[here] = (x * inv_rms * gain_ref[...]).astype(bf16)
-
-    wait_all(weights)
-    cols_ref[...] = dot(normed_ref[...], weight_ref[...], ((1,), (0,))).T.astype(bf16)
-    out = [copies.start(cols_ref, cols_hbm)]
+        normed_ref[here] = normed_rows(x_ref[here])
+
+    core = core_here()
+    wait_all(small)
     edge = before_ref.shape[0]
+    before_ref[...] = normed_rows(before_ref[...])
+    out = []
     for step in range(STEPS):
         lanes = lanes_of(step)
         normed = normed_ref[:, lanes].astype(f32)
@@ -192,18 +200,21 @@
         row = lax.broadcasted_iota(jnp.int32, normed.shape, 0)
         one_back = jnp.where(row == 0, before[7:8], rolled(normed, 1))
         two_back = jnp.where(row == 0, before[6:7], rolled(one_back, 1))
-        taps = taps_ref[:, lanes]
-        values = (taps[0:1] * two_back + taps[1:2] * one_back + taps[2:3] * normed).astype(bf16)
+        taps = [taps_ref[tap, :, lanes] for tap in range(3)]
+        values = (taps[0] * two_back + taps[1] * one_back + taps[2] * normed).astype(bf16)
         values_ref[:, lanes] = values
         out += by_lanes(copies, values_ref, values_hbm, [step])
-        for head in range(STEP_HEADS):
-            place = step * STEP_HEADS + head
+        wait_all(weights[step])
+        product = dot(normed_ref[:, lanes], weight_ref[lanes], ((1,), (0,)))
+        total = product if step == 0 else total + product
+    cols_ref[...] = total.T.astype(bf16)
+    out.append(copies.start(cols_ref, cols_hbm))
+    for step in range(STEPS):
+        for place in range(step * STEP_HEADS, (step + 1) * STEP_HEADS):
             keys = cols_ref[middle + place * FEAT : middle + (place + 1) * FEAT].astype(f32)
-            state = dot(taylor_rows(keys, 1.0), values[:, head_of(head, VDIM)], ((1,), (0,)))
+            state = dot(taylor_rows(keys, 1.0), values_ref[:, head_of(place, VDIM)], ((1,), (0,)))
             state_ref[head_of(place, PACKED)] = state.astype(bf16)
-    core = core_ref[0]
-    out.append(copies.start(state_ref.at[half_rows(1 - core)], away_hbm))
-    out.append(copies.start(state_ref.at[half_rows(core)], own_hbm))
+        out.append(state_out(copies, core, step, state_ref, own_hbm, away_hbm))
     wait_all(out)
 
 
@@ -255,12 +266,12 @@
     return jnp.where(adds_other[half], both, state)
 
 
-def head_mean(terms, ones):
-    return dot(terms.astype(bf16), ones, ((1,), (0,))) * (1.0 / VDIM)
+def head_means(terms, other_terms, ones):
+    both = jnp.concatenate([terms.astype(bf16), other_terms.astype(bf16)], axis=1)
+    return dot(both, ones, ((1,), (0,))) * (1.0 / VDIM)
 
 
 def output_kernel(
-    core_ref,
     cols_hbm,
     inside_low_hbm,
     inside_high_hbm,
@@ -288,7 +299,7 @@
     sems,
 ):
     copies = Copies(sems)
-    core = core_ref[0]
+    core = core_here()
     middle = cols_ref.shape[0] // 2
     first = states_in(copies, core, before_hbm, other_hbm, theirs_hbm, prefix_ref, other_ref)
     first += [copies.start(cols_hbm.at[:middle], cols_ref.at[:middle]), copies.start(scale_hbm, scale_ref)]
@@ -302,7 +313,9 @@
         )
     wait_all(first)
     adds_other = (False, core == 1)
-    ones = jnp.ones((VDIM, VDIM), bf16)
+    side = lax.broadcasted_iota(jnp.int32, (2 * VDIM, 2 * VDIM), 0) < VDIM
+    other_side = lax.broadcasted_iota(jnp.int32, (2 * VDIM, 2 * VDIM), 1) < VDIM
+    ones = jnp.where(side == other_side, 1.0, 0.0).astype(bf16)
     out = []
     for step in range(STEPS):
         wait_all(blocks[step])
@@ -315,16 +328,17 @@
             numer = inside_ref[:, lanes].astype(f32) + dot(feat, prefix, ((0,), (0,)))
             scale = scale_ref[:, lanes]
             grad = grad_ref[:, lanes].astype(f32) * scale
-            inv = lax.rsqrt(head_mean(numer * numer, ones) + EPSILON)
-            mean = head_mean(grad * numer, ones)
+            means = head_means(numer * numer, grad * numer, ones)
+            inv = lax.rsqrt(means[:, :VDIM] + EPSILON)
+            mean = means[:, VDIM:]
             out_ref[:, lanes] = (x_ref[:, lanes].astype(f32) + scale * (numer * inv)).astype(bf16)
             grad_numer = (inv * grad - numer * (inv * inv * inv * mean)).astype(bf16)
             numer_ref[:, lanes] = grad_numer
             state_ref[head_of(place, PACKED)] = dot(feat, grad_numer, ((1,), (0,))).astype(bf16)
+        state_rows = head_of(step, STEP_HEADS * PACKED)
+        out.append(state_out(copies, core, step, state_ref, grad_own_hbm, grad_away_hbm))
         out += by_lanes(copies, out_ref, out_hbm, [step]) + by_lanes(copies, numer_ref, numer_hbm, [step])
-    out.append(copies.start(state_ref.at[half_rows(1 - core)], grad_away_hbm))
-    out.append(copies.start(state_ref.at[half_rows(core)], grad_own_hbm))
-    out.append(copies.start(prefix_ref, prefix_hbm))
+        out.append(copies.start(prefix_ref.at[state_rows], prefix_hbm.at[state_rows]))
     wait_all(out)
 
 
@@ -385,7 +399,6 @@
 
 
 def late_kernel(
-    core_ref,
     cols_hbm,
     values_hbm,
     before_hbm,
@@ -401,11 +414,10 @@
     gain_hbm,
     x_hbm,
     grad_hbm,
-    forward_hbm,
     *rest,
 ):
-    edge_hbm, scaled_hbm, sums_hbm, forward_out_hbm = rest[:4]
-    piece_hbms, rest = rest[4 : 3 + PIECES], rest[3 + PIECES :]
+    edge_hbm, scaled_hbm, sums_hbm = rest[:3]
+    piece_hbms, rest = rest[3 : 2 + PIECES], rest[2 + PIECES :]
     (
         cols_ref,
         values_ref,
@@ -413,8 +425,7 @@
         other_ref,
         grads_ref,
         early_ref,
-        query_ref,
-        key_ref,
+        weight_ref,
         taps_ref,
         gain_ref,
         x_ref,
@@ -425,11 +436,10 @@
         sums_ref,
         out_ref,
         edge_ref,
-        forward_ref,
         sems,
     ) = rest
     copies = Copies(sems)
-    core = core_ref[0]
+    core = core_here()
     middle, rows = cols_ref.shape[0], cols_ref.shape[1]
     half_cols = middle // 2
     first = states_in(copies, core, before_hbm, other_hbm, theirs_hbm, state_ref, other_ref)
@@ -449,13 +459,14 @@
             by_lanes(copies, values_hbm, values_ref, [step])
             + [copies.start(source.at[:, lanes_of(step % (STEPS // 2))], early_ref.at[:, lanes_of(step)])]
         )
-    weights = [copies.start(taps_hbm, taps_ref), copies.start(gain_hbm, gain_ref)]
+    first += [copies.start(taps_hbm, taps_ref), copies.start(gain_hbm, gain_ref)]
+    weights = []
     for step in range(STEPS):
         lanes = lanes_of(step)
-        weights.append(copies.start(query_hbm.at[lanes], query_ref.at[lanes]))
-        weights.append(copies.start(key_hbm.at[lanes], key_ref.at[lanes]))
-    weights += [copies.start(x_hbm, x_ref), copies.start(grad_hbm, grad_ref)]
-    forward_in = copies.start(forward_hbm, forward_ref)
+        weights.append(copies.start(query_hbm.at[lanes], weight_ref.at[lanes, :middle]))
+        weights.append(copies.start(key_hbm.at[lanes], weight_ref.at[lanes, middle:]))
+    weights.append(copies.start(x_hbm, x_ref))
+    grad_in = copies.start(grad_hbm, grad_ref)
     wait_all(first)
     adds_other = (core == 0, False)
     for step in range(STEPS):
@@ -471,8 +482,7 @@
             late = dot(taylor_rows(key, 1.0), state, ((0,), (0,)))
             grad_values_ref[:, lanes] = early_ref[:, lanes].astype(f32) + late
     edge_ref[...] = grad_values_ref[:8]
-    forward_in.wait()
-    out = [copies.start(forward_ref, forward_out_hbm), copies.start(edge_ref, edge_hbm)]
+    out = [copies.start(edge_ref, edge_hbm)]
     turned_ref[...] = grads_ref[...].T.astype(bf16)
     wait_all(weights)
     total = jnp.zeros((rows, VDIM), f32)
@@ -483,10 +493,9 @@
         row = lax.broadcasted_iota(jnp.int32, grad_values.shape, 0)
         one_on = jnp.where(row == rows - 1, 0.0, rolled(grad_values, -1))
         two_on = jnp.where(row == rows - 1, 0.0, rolled(one_on, -1))
-        grad_normed = dot(turned_ref[:, :middle], query_ref[lanes], ((1,), (1,)))
-        grad_normed = grad_normed + dot(turned_ref[:, middle:], key_ref[lanes], ((1,), (1,)))
-        taps = taps_ref[:, lanes]
-        grad_normed = grad_normed + (taps[2:3] * grad_values + taps[1:2] * one_on + taps[0:1] * two_on)
+        grad_normed = dot(turned_ref[...], weight_ref[lanes], ((1,), (1,)))
+        taps = [taps_ref[tap, :, lanes] for tap in range(3)]
+        grad_normed = grad_normed + (taps[2] * grad_values + taps[1] * one_on + taps[0] * two_on)
         scaled = grad_normed * gain_ref[:, lanes]
         scaled_ref[:, lanes] = scaled
         x = x_ref[:, lanes].astype(f32)
@@ -501,6 +510,7 @@
     cut = rows // PIECES
     tail = slice(rows - cut, rows)
     out += [copies.start(scaled_ref.at[tail], scaled_hbm), copies.start(sums_ref.at[tail], sums_hbm)]
+    grad_in.wait()
     for piece in range(PIECES - 1):
         here = slice(piece * cut, (piece + 1) * cut)
         out_ref[here] = input_grad(scaled_ref[here], sums_ref[here], x_ref[here], grad_ref[here])
@@ -515,17 +525,28 @@
     return (grad.astype(f32) + inv * scaled - x.astype(f32) * pull).astype(bf16)
 
 
-def last_kernel(scaled_ref, sums_ref, x_ref, grad_ref, after_ref, taps_ref, gain_ref, out_ref):
+def last_kernel(*refs):
+    scaled_hbm, sums_hbm, x_hbm, grad_hbm, after_hbm, taps_hbm, gain_hbm, forward_hbm, out_hbm, forward_out_hbm = refs[:10]
+    scaled_ref, sums_ref, x_ref, grad_ref, after_ref, taps_ref, gain_ref, out_ref, forward_ref, sems = refs[10:]
+    copies = Copies(sems)
     rows, width = x_ref.shape
+    tail = slice(x_hbm.shape[0] - rows, x_hbm.shape[0])
+    sources = [scaled_hbm, sums_hbm, x_hbm.at[tail], grad_hbm.at[tail], after_hbm, taps_hbm, gain_hbm]
+    targets = [scaled_ref, sums_ref, x_ref, grad_ref, after_ref, taps_ref, gain_ref]
+    first = [copies.start(source, target) for source, target in zip(sources, targets)]
+    forward = copies.start(forward_hbm, forward_ref)
+    wait_all(first)
     after = after_ref[...]
     row = lax.broadcasted_iota(jnp.int32, (rows, width), 0)
-    upper = taps_ref[0:1] * after[0:1]
-    lower = taps_ref[1:2] * after[0:1] + taps_ref[0:1] * after[1:2]
+    upper = taps_ref[0] * after[0:1]
+    lower = taps_ref[1] * after[0:1] + taps_ref[0] * after[1:2]
     extra = jnp.where(row == rows - 2, upper, jnp.where(row == rows - 1, lower, 0.0)) * gain_ref[...]
     with_x = jnp.sum(x_ref[...].astype(f32) * extra, axis=1, keepdims=True)
     lane = lax.broadcasted_iota(jnp.int32, sums_ref.shape, 1)
     sums = sums_ref[...] + jnp.where(lane == 0, with_x, 0.0)
     out_ref[...] = input_grad(scaled_ref[...] + extra, sums, x_ref[...], grad_ref[...])
+    forward.wait()
+    wait_all([copies.start(out_ref, out_hbm), copies.start(forward_ref, forward_out_hbm)])
 
 
 def chip_sums_kernel(reverse, got_ref, out_ref):
@@ -561,27 +582,6 @@
     )(own, other)
 
 
-def join_kernel(*refs):
-    *pieces, out_hbm, sems = refs
-    copies = Copies(sems)
-    rows = pieces[0].shape[0]
-    wait_all([copies.start(piece, out_hbm.at[head_of(k, rows)]) for k, piece in enumerate(pieces)])
-
-
-def joined(pieces):
-    rows, width = pieces[0].shape
-    anywhere = pl.BlockSpec(memory_space=pl.ANY)
-    return pl.pallas_call(
-        join_kernel,
-        in_specs=[anywhere] * len(pieces),
-        out_specs=anywhere,
-        out_shape=jax.ShapeDtypeStruct((rows * len(pieces), width), bf16),
-        scratch_shapes=[pltpu.SemaphoreType.DMA((len(pieces),))],
-        name="join",
-        **params(1),
-    )(*pieces)
-
-
 def core_swap(block):
     count = lax.axis_size("seq")
     return lax.ppermute(block, "seq", [(i, i ^ 1) for i in range(count)])
@@ -621,29 +621,28 @@
 
 def local(layer_in, norm_gain, conv_weight, query_weight, key_weight, out_gain, layer_grad):
     x, grad = layer_in[0], layer_grad[0]
-    taps, query_proj, key_proj = conv_weight[0], query_weight[0], key_weight[0]
+    query_proj, key_proj = query_weight[0], key_weight[0]
+    taps = jnp.transpose(conv_weight, (1, 0, 2))
     rows, width = x.shape
     both = 2 * query_proj.shape[1]
     half_width = width // 2
     cut = rows // PIECES
-    parity = lax.axis_index("seq") % 2
-    core = parity.reshape(1).astype(jnp.int32)
+    parity = core_here()
     half_state = ((HALF_STATE, VDIM), bf16)
     all_state = ((2 * HALF_STATE, VDIM), bf16)
     tokens, tokens_wide = ((rows, width), bf16), ((rows, width), f32)
     cols_shape = ((both, rows), bf16)
 
-    before_edge = neighbour_rows(edge_rows(x, norm_gain), 1)
+    before_edge = neighbour_rows(x[rows - 16 :], 1)
     values, cols, own, away = streamed(
         state_kernel,
-        [core, x, norm_gain, query_proj, key_proj, before_edge, taps],
+        [x, norm_gain, query_proj, key_proj, before_edge, taps],
         [tokens, cols_shape, half_state, half_state],
         "state",
         8,
-        [tokens, ((1, width), f32), ((width, both), bf16), ((16, width), bf16), ((3, width), f32)]
+        [tokens, ((1, width), f32), ((width, both), bf16), ((16, width), bf16), ((3, 1, width), f32)]
         + [tokens, tokens, cols_shape, all_state],
-        6 + 3 + STEPS,
-        in_specs=[IN_SMEM] + [IN_HBM] * 6,
+        4 + 2 * STEPS + 1 + 2 * STEPS,
     )
 
     def inside(half, cols, values):
@@ -665,13 +664,12 @@
     before, theirs = scan_second(before, own, parity == 0)
     output, numer, prefix, grad_own, grad_away = streamed(
         output_kernel,
-        [core, cols, inside_low, inside_high, before, other, theirs, x, grad, out_gain],
+        [cols, inside_low, inside_high, before, other, theirs, x, grad, out_gain],
         [tokens, tokens, all_state, half_state, half_state],
         "output",
         8,
         [cols_shape, tokens, all_state, half_state, tokens, tokens, ((1, width), f32), tokens, tokens, all_state],
-        5 + 3 * STEPS + 2 * STEPS + 3,
-        in_specs=[IN_SMEM] + [IN_HBM] * 9,
+        5 + 3 * STEPS + 4 * STEPS,
     )
     sent_forward = section_pass(output, 1)
 
@@ -693,35 +691,33 @@
     _, numer_then = lax.optimization_barrier((got, numer))
     grad_before, high = lax.optimization_barrier((over_chips(chip_sums(got, True)), inside_back(1, numer_then)))
     grad_before, grad_theirs = scan_second(grad_before, grad_own, parity == 1)
-    edge, scaled, sums, sent_forward, *pieces = streamed(
+    edge, scaled, sums, *pieces = streamed(
         late_kernel,
-        [core, cols, values, grad_before, grad_other, grad_theirs, low[0], high[0], low[1], high[1]]
-        + [query_proj, key_proj, taps, norm_gain, x, grad, sent_forward],
-        [((8, width), f32), ((cut, width), f32), ((cut, VDIM), f32), tokens] + [((cut, width), bf16)] * (PIECES - 1),
+        [cols, values, grad_before, grad_other, grad_theirs, low[0], high[0], low[1], high[1]]
+        + [query_proj, key_proj, taps, norm_gain, x, grad],
+        [((8, width), f32), ((cut, width), f32), ((cut, VDIM), f32)] + [((cut, width), bf16)] * (PIECES - 1),
         "late",
         9,
         [((both // 2, rows), bf16), tokens, all_state, half_state, ((both, rows), f32), tokens]
-        + [((width, both // 2), bf16)] * 2
-        + [((3, width), f32), ((1, width), f32), tokens, tokens, tokens_wide, ((rows, both), bf16), tokens_wide]
-        + [((rows, VDIM), f32), tokens, ((8, width), f32), tokens],
-        3 + 1 + 4 + 2 * STEPS + 2 + 2 * STEPS + 2 + 3 + 2 + PIECES - 1,
-        in_specs=[IN_SMEM] + [IN_HBM] * 16,
+        + [((width, both), bf16)]
+        + [((3, 1, width), f32), ((1, width), f32), tokens, tokens, tokens_wide, ((rows, both), bf16), tokens_wide]
+        + [((rows, VDIM), f32), tokens, ((8, width), f32)],
+        3 + 1 + 4 + 2 * STEPS + 2 + 2 * STEPS + 2 + 1 + 2 + PIECES - 1,
     )
     after_edge = neighbour_rows(edge, -1)
-    at_last = lambda: pl.BlockSpec((cut, width), lambda i: (PIECES - 1, 0))
-    whole = lambda n, cols=width: pl.BlockSpec((n, cols), lambda i: (0, 0))
-    pieces.append(
-        pl.pallas_call(
-            last_kernel,
-            grid=(1,),
-            in_specs=[whole(cut), whole(cut, VDIM), at_last(), at_last(), whole(8), whole(3), whole(1)],
-            out_specs=whole(cut),
-            out_shape=jax.ShapeDtypeStruct((cut, width), bf16),
-            name="last",
-            **params(1),
-        )(scaled, sums, x, grad, after_edge, taps, norm_gain)
+    piece_wide, piece = ((cut, width), f32), ((cut, width), bf16)
+    last_piece, sent_forward = streamed(
+        last_kernel,
+        [scaled, sums, x, grad, after_edge, taps, norm_gain, sent_forward],
+        [piece, tokens],
+        "last",
+        2,
+        [piece_wide, ((cut, VDIM), f32), piece, piece, ((8, width), f32), ((3, 1, width), f32), ((1, width), f32)]
+        + [piece, tokens],
+        10,
     )
-    sent_backward = joined([section_pass(piece, -1) for piece in pieces])
+    pieces.append(last_piece)
+    sent_backward = jnp.concatenate([section_pass(piece, -1) for piece in pieces], axis=0)
     return (sent_forward[None], sent_backward[None])
 
 

time: 162 us -> 157 us (0.969)
  waiting for transfers between devices: 54.9 us -> 51.8 us
  starting transfers between devices: 37.2 us -> 39.6 us
  local copies, waits for them, and re-layouts: 8.56 us -> 6.2 us
  Pallas kernels: 58.6 us -> 56.6 us
    ppermute x5, waiting for transfers between devices: 30.3 us -> 26.3 us  [section_pass(): lax.ppermute(block, 'section', [((i - distance) % count, i) for i in rang...]
    unnamed x37 -> x24, local copies, waits for them, and re-layouts: 8.56 us -> 5.3 us
    ppermute x5, starting transfers between devices: 4.79 us -> 7.55 us  [section_pass(): lax.ppermute(block, 'section', [((i - distance) % count, i) for i in rang...]
    pallas_call x10 -> x8, Pallas kernels: 55.1 us -> 53 us  [streamed(): pl.pallas_call(kernel, in_specs=[IN_HBM] * len(operands), out_specs=[IN_H...]
  transfers between devices with their start and end apart: 15 -> 15, of which waited for: 14 -> 14; matrix products, arithmetic and copies ran while one was open for 1% -> 0% of each run, Pallas kernels for 15% -> 23%
where the time goes in v3:
time: 157 us
  Pallas kernels  56.6 us (36%)
  waiting for transfers between devices  51.8 us (33%)
  starting transfers between devices  39.6 us (25%)
  local copies, waits for them, and re-layouts  6.2 us (4%)
  other arithmetic  1.63 us (1%)
    pallas_call x8, Pallas kernels, streamed(): pl.pallas_call(kernel, in_specs=[IN_HBM] * len(operands), out_specs=[IN_H...  53 us
    ppermute x5, waiting for transfers between devices, section_pass(): lax.ppermute(block, 'section', [((i - distance) % count, i) for i in rang...  26.3 us
    all_to_all x4, starting transfers between devices, over_chips(): lax.all_to_all(block, 'seq', 0, 0, tiled=True, axis_index_groups=groups)  19.5 us
    all_to_all x4, waiting for transfers between devices, over_chips(): lax.all_to_all(block, 'seq', 0, 0, tiled=True, axis_index_groups=groups)  17.8 us
    ppermute x5, starting transfers between devices, section_pass(): lax.ppermute(block, 'section', [((i - distance) % count, i) for i in rang...  7.55 us
    ppermute x2, starting transfers between devices, neighbour_rows(): return lax.ppermute(edge, 'seq', route)  6.77 us
    ppermute x4, starting transfers between devices, core_swap(): return lax.ppermute(block, 'seq', [(i, i ^ 1) for i in range(count)])  5.81 us
    ppermute x4, waiting for transfers between devices, core_swap(): return lax.ppermute(block, 'seq', [(i, i ^ 1) for i in range(count)])  5.45 us
  transfers between devices with their start and end apart: 15, of which 14 were waited for; matrix products, arithmetic and copies ran while one was open for 0% of the time, Pallas kernels for 23%

profile of v3, /device:TPU:1, one launch (start us, length us, event | category | flops | bytes accessed | tf_op | source)
XLA Modules:
  0.0 156.7 jit_solution(8385719350786366143)
XLA Ops:
  1.5 4.5 %collective-permute-start = (bf16[16,3072]{1,0:T(8,128)(2,1)S(1)}, bf16[16,3072]{1,0:T(8,128)(2,1)S(1)}, u32[]{:S(2)}, u32[]{:S(2)}) collective-permute-start(bf16[16,3072]{1,0:T(8,128)(2,1)S(1)} %slice_bitcast_fusion), channel_id=1, source_target_pairs={{0,4},{4,8},{8,12},{12,16},{16,20},{20,24},{24,28},{28,32},{32,36}... | collective-permute-start | bytes 294920 | tf_op jit(solution)/shard_map/ppermute | solution.py:614
  8.3 7.8 %state.1 = (bf16[256,3072]{1,0:T(8,128)(2,1)}, bf16[768,256]{1,0:T(8,128)(2,1)}, bf16[1920,128]{1,0:T(8,128)(2,1)}, bf16[1920,128]{1,0:T(8,128)(2,1)}) custom-call(bf16[256,3072]{1,0:T(8,128)(2,1)} %bitcast.16, f32[1,3072]{1,0:T(1,128)} %refs_6_.1, bf16[3072,384]{1,0:T(8,128)(2,1)} %bitcast.20, bf16[3072,384]{1,0:T(8,128)(2,1)} %bitcast.22, ...), custom_call_target="tpu_custom_call" | custom-call | flops 8800000000 | bytes 65536 | tf_op jit(solution)/shard_map/state/pallas_call | solution.py:51
  20.4 8.5 %all-to-all-start = ((bf16[16,120,128]{2,1,0:T(8,128)(2,1)}), bf16[16,120,128]{2,1,0:T(8,128)(2,1)S(1)}, u32[]{:S(2)}, u32[]{:S(2)}) async-start(bf16[16,120,128]{2,1,0:T(8,128)(2,1)} %pair_sum.2), calls=%async_computation | async-start | bytes 983040 | tf_op jit(solution)/shard_map/all_to_all | solution.py:593
  28.9 3.7 %inside.2.inside_low_hbm = bf16[256,1536]{1,0:T(8,128)(2,1)} custom-call(bf16[768,256]{1,0:T(8,128)(2,1)} %get-tuple-element.35.cols_hbm, bf16[256,3072]{1,0:T(8,128)(2,1)} %get-tuple-element.41.values_hbm), custom_call_target="tpu_custom_call" | custom-call | flops 3300000000 | bytes 65536 | tf_op jit(solution)/shard_map/inside/pallas_call | solution.py:51
  32.6 6.7 %all-to-all-done.got_ref = bf16[16,120,128]{2,1,0:T(8,128)(2,1)S(1)} async-done(((bf16[16,120,128]{2,1,0:T(8,128)(2,1)}), bf16[16,120,128]{2,1,0:T(8,128)(2,1)S(1)}, u32[]{:S(2)}, u32[]{:S(2)}) %all-to-all-start) | async-done | bytes 491552 | tf_op jit(solution)/shard_map/all_to_all | solution.py:593
  40.1 3.6 %all-to-all-start.1 = ((bf16[16,120,128]{2,1,0:T(8,128)(2,1)}), bf16[16,120,128]{2,1,0:T(8,128)(2,1)S(1)}, u32[]{:S(2)}, u32[]{:S(2)}) async-start(bf16[16,120,128]{2,1,0:T(8,128)(2,1)} %chip_sums.2), calls=%async_computation.1 | async-start | bytes 983040 | tf_op jit(solution)/shard_map/all_to_all | solution.py:593
  43.7 3.7 %inside.3.inside_high_hbm = bf16[256,1536]{1,0:T(8,128)(2,1)} custom-call(bf16[768,256]{1,0:T(8,128)(2,1)} %get-tuple-element.35.cols_hbm, bf16[256,3072]{1,0:T(8,128)(2,1)} %get-tuple-element.41.values_hbm), custom_call_target="tpu_custom_call" | custom-call | flops 3300000000 | bytes 65536 | tf_op jit(solution)/shard_map/inside/pallas_call | solution.py:51
  47.4 5.8 %all-to-all-done.1 = bf16[16,120,128]{2,1,0:T(8,128)(2,1)S(1)} async-done(((bf16[16,120,128]{2,1,0:T(8,128)(2,1)}), bf16[16,120,128]{2,1,0:T(8,128)(2,1)S(1)}, u32[]{:S(2)}, u32[]{:S(2)}) %all-to-all-start.1) | async-done | bytes 491552 | tf_op jit(solution)/shard_map/all_to_all | solution.py:593
  53.4 2.9 %collective-permute-start.2 = (bf16[1920,128]{1,0:T(8,128)(2,1)S(1)}, bf16[1920,128]{1,0:T(8,128)(2,1)S(1)}, u32[]{:S(2)}, u32[]{:S(2)}) collective-permute-start(bf16[1920,128]{1,0:T(8,128)(2,1)S(1)} %fusion), channel_id=1, source_target_pairs={{0,4},{4,0},{8,12},{12,8},{16,20},{20,16},{24,28},{28,24},{32,36},... | collective-permute-start | bytes 1474568 | tf_op jit(solution)/shard_map/ppermute | solution.py:587
  58.6 10.5 %output.1 = (bf16[256,3072]{1,0:T(8,128)(2,1)}, bf16[256,3072]{1,0:T(8,128)(2,1)}, bf16[3840,128]{1,0:T(8,128)(2,1)}, bf16[1920,128]{1,0:T(8,128)(2,1)}, bf16[1920,128]{1,0:T(8,128)(2,1)}) custom-call(bf16[768,256]{1,0:T(8,128)(2,1)} %get-tuple-element.35.cols_hbm, bf16[256,1536]{1,0:T(8,128)(2,1)} %inside.2.inside_low_hbm, ...), custom_call_target="tpu_custom_call" | custom-call | flops 8800000000 | bytes 65536 | tf_op jit(solution)/shard_map/output/pallas_call | solution.py:51
  73.5 3.6 %all-to-all-start.2 = ((bf16[16,120,128]{2,1,0:T(8,128)(2,1)}), bf16[16,120,128]{2,1,0:T(8,128)(2,1)S(1)}, u32[]{:S(2)}, u32[]{:S(2)}) async-start(bf16[16,120,128]{2,1,0:T(8,128)(2,1)} %pair_sum.3), calls=%async_computation.2 | async-start | bytes 983040 | tf_op jit(solution)/shard_map/all_to_all | solution.py:593
  77.0 7.4 %inside_back.2 = (f32[384,256]{1,0:T(8,128)}, bf16[256,1536]{1,0:T(8,128)(2,1)}) custom-call(bf16[768,256]{1,0:T(8,128)(2,1)} %get-tuple-element.35.cols_hbm, bf16[256,3072]{1,0:T(8,128)(2,1)} %get-tuple-element.41.values_hbm, bf16[256,3072]{1,0:T(8,128)(2,1)} %get-tuple-element.51.numer_hbm, bf16[3840,128]{1,0:T(8,128)(2,1)} %get-tuple-element.47.prefix_hbm), custom_call_target="tpu_custom_call" | custom-call | flops 5500000256 | bytes 65536 | tf_op jit(solution)/shard_map/inside_back/pallas_call | solution.py:51
  84.4 3.2 %all-to-all-done.2.got_ref = bf16[16,120,128]{2,1,0:T(8,128)(2,1)S(1)} async-done(((bf16[16,120,128]{2,1,0:T(8,128)(2,1)}), bf16[16,120,128]{2,1,0:T(8,128)(2,1)S(1)}, u32[]{:S(2)}, u32[]{:S(2)}) %all-to-all-start.2) | async-done | bytes 491552 | tf_op jit(solution)/shard_map/all_to_all | solution.py:593
  88.5 3.8 %all-to-all-start.3 = ((bf16[16,120,128]{2,1,0:T(8,128)(2,1)}), bf16[16,120,128]{2,1,0:T(8,128)(2,1)S(1)}, u32[]{:S(2)}, u32[]{:S(2)}) async-start(bf16[16,120,128]{2,1,0:T(8,128)(2,1)} %chip_sums.3), calls=%async_computation.3 | async-start | bytes 983040 | tf_op jit(solution)/shard_map/all_to_all | solution.py:593
  92.3 7.5 %inside_back.3 = (f32[384,256]{1,0:T(8,128)}, bf16[256,1536]{1,0:T(8,128)(2,1)}) custom-call(bf16[768,256]{1,0:T(8,128)(2,1)} %get-tuple-element.35.cols_hbm, bf16[256,3072]{1,0:T(8,128)(2,1)} %get-tuple-element.41.values_hbm, bf16[256,3072]{1,0:T(8,128)(2,1)} %get-tuple-element.51.numer_hbm, bf16[3840,128]{1,0:T(8,128)(2,1)} %get-tuple-element.47.prefix_hbm), custom_call_target="tpu_custom_call" | custom-call | flops 5500000256 | bytes 65536 | tf_op jit(solution)/shard_map/inside_back/pallas_call | solution.py:51
  102.1 2.4 %collective-permute-start.4 = (bf16[1920,128]{1,0:T(8,128)(2,1)S(1)}, bf16[1920,128]{1,0:T(8,128)(2,1)S(1)}, u32[]{:S(2)}, u32[]{:S(2)}) collective-permute-start(bf16[1920,128]{1,0:T(8,128)(2,1)S(1)} %fusion.1), channel_id=1, source_target_pairs={{0,4},{4,0},{8,12},{12,8},{16,20},{20,16},{24,28},{28,24},{32,36},... | collective-permute-start | bytes 1474568 | tf_op jit(solution)/shard_map/ppermute | solution.py:587
  106.8 9.2 %late.1 = (f32[8,3072]{1,0:T(8,128)}, f32[64,3072]{1,0:T(8,128)}, f32[64,128]{1,0:T(8,128)}, bf16[64,3072]{1,0:T(8,128)(2,1)}, bf16[64,3072]{1,0:T(8,128)(2,1)}, /*index=5*/bf16[64,3072]{1,0:T(8,128)(2,1)}) custom-call(bf16[768,256]{1,0:T(8,128)(2,1)} %get-tuple-element.35.cols_hbm, bf16[256,3072]{1,0:T(8,128)(2,1)} %get-tuple-element.41.values_hbm, ...), custom_call_target="tpu_custom_call" | custom-call | flops 9900000256 | bytes 65536 | tf_op jit(solution)/shard_map/late/pallas_call | solution.py:51
  116.0 2.3 %collective-permute-start.5 = (f32[8,3072]{1,0:T(8,128)}, f32[8,3072]{1,0:T(8,128)S(1)}, u32[]{:S(2)}, u32[]{:S(2)}) collective-permute-start(f32[8,3072]{1,0:T(8,128)} %get-tuple-element.61), channel_id=1, source_target_pairs={{4,0},{8,4},{12,8},{16,12},{20,16},{24,20},{28,24},{32,28},{36,32}... | collective-permute-start | bytes 294920 | tf_op jit(solution)/shard_map/ppermute | solution.py:614
  118.2 2.8 %collective-permute-start.7 = (bf16[64,3072]{1,0:T(8,128)(2,1)}, bf16[64,3072]{1,0:T(8,128)(2,1)S(1)}, u32[]{:S(2)}, u32[]{:S(2)}) collective-permute-start(bf16[64,3072]{1,0:T(8,128)(2,1)} %get-tuple-element.64), channel_id=1, source_target_pairs={{1,0},{2,1},{3,2},{0,3},{5,4},{6,5},{7,6},{4,7},{9,8},{10,9},{11,1... | collective-permute-start | bytes 1179656 | tf_op jit(solution)/shard_map/ppermute | solution.py:619
  123.0 3.3 %last.1 = (bf16[64,3072]{1,0:T(8,128)(2,1)}, bf16[256,3072]{1,0:T(8,128)(2,1)}) custom-call(f32[64,3072]{1,0:T(8,128)} %get-tuple-element.59.refs_0_, f32[64,128]{1,0:T(8,128)} %get-tuple-element.60.refs_1_, bf16[256,3072]{1,0:T(8,128)(2,1)} %bitcast.19, bf16[256,3072]{1,0:T(8,128)(2,1)} %bitcast.26, f32[8,3072]{1,0:T(8,128)} %copy-done.10, ...), custom_call_target="tpu_custom_call" | custom-call | flops 2200000000 | bytes 65536 | tf_op jit(solution)/shard_map/last/pallas_call | solution.py:51
  126.4 2.8 %collective-permute-start.10 = (bf16[64,3072]{1,0:T(8,128)(2,1)}, bf16[64,3072]{1,0:T(8,128)(2,1)S(1)}, u32[]{:S(2)}, u32[]{:S(2)}) collective-permute-start(bf16[64,3072]{1,0:T(8,128)(2,1)} %get-tuple-element.67), channel_id=1, source_target_pairs={{1,0},{2,1},{3,2},{0,3},{5,4},{6,5},{7,6},{4,7},{9,8},{10,9},{11,1... | collective-permute-start | bytes 1179656 | tf_op jit(solution)/shard_map/ppermute | solution.py:619
  130.3 8.4 %collective-permute-done.8 = bf16[64,3072]{1,0:T(8,128)(2,1)S(1)} collective-permute-done((bf16[64,3072]{1,0:T(8,128)(2,1)}, bf16[64,3072]{1,0:T(8,128)(2,1)S(1)}, u32[]{:S(2)}, u32[]{:S(2)}) %collective-permute-start.8) | collective-permute-done | bytes 393248 | tf_op jit(solution)/shard_map/ppermute | solution.py:619
  138.7 8.4 %collective-permute-done.9 = bf16[64,3072]{1,0:T(8,128)(2,1)S(1)} collective-permute-done((bf16[64,3072]{1,0:T(8,128)(2,1)}, bf16[64,3072]{1,0:T(8,128)(2,1)S(1)}, u32[]{:S(2)}, u32[]{:S(2)}) %collective-permute-start.9) | collective-permute-done | bytes 393248 | tf_op jit(solution)/shard_map/ppermute | solution.py:619
  147.2 8.3 %collective-permute-done.10 = bf16[64,3072]{1,0:T(8,128)(2,1)S(1)} collective-permute-done((bf16[64,3072]{1,0:T(8,128)(2,1)}, bf16[64,3072]{1,0:T(8,128)(2,1)S(1)}, u32[]{:S(2)}, u32[]{:S(2)}) %collective-permute-start.10) | collective-permute-done | bytes 393248 | tf_op jit(solution)/shard_map/ppermute | solution.py:619
  (46 shorter events, 24.9 us)
Async XLA Ops:
  1.5 6.1 %collective-permute-start = (bf16[16,3072]{1,0:T(8,128)(2,1)S(1)}, bf16[16,3072]{1,0:T(8,128)(2,1)S(1)}, u32[]{:S(2)}, u32[]{:S(2)}) collective-permute-start(bf16[16,3072]{1,0:T(8,128)(2,1)S(1)} %slice_bitcast_fusion), channel_id=1, source_target_pairs={{0,4},{4,8},{8,12},{12,16},{16,20},{20,24},{24,28},{28,32},{32,36}... | collective-permute-start | bytes 294920 | tf_op jit(solution)/shard_map/ppermute | solution.py:614
  16.1 2.2 %collective-permute-start.1 = (bf16[1920,128]{1,0:T(8,128)(2,1)}, bf16[1920,128]{1,0:T(8,128)(2,1)S(1)}, u32[]{:S(2)}, u32[]{:S(2)}) collective-permute-start(bf16[1920,128]{1,0:T(8,128)(2,1)} %get-tuple-element.38), channel_id=1, source_target_pairs={{0,4},{4,0},{8,12},{12,8},{16,20},{20,16},{24,28},{28,24},{32,36},... | collective-permute-start | bytes 1474568 | tf_op jit(solution)/shard_map/ppermute | solution.py:587
  18.2 14.4 %copy-start.4 = (bf16[1920,128]{1,0:T(8,128)(2,1)}, bf16[1920,128]{1,0:T(8,128)(2,1)S(1)}, u32[]{:S(2)}) copy-start(bf16[1920,128]{1,0:T(8,128)(2,1)S(1)} %collective-permute-done.1.other_ref.other_hbm) | copy-start | bytes 1474564
  18.2 1.2 copy-start
  20.4 18.9 %all-to-all-start = ((bf16[16,120,128]{2,1,0:T(8,128)(2,1)}), bf16[16,120,128]{2,1,0:T(8,128)(2,1)S(1)}, u32[]{:S(2)}, u32[]{:S(2)}) async-start(bf16[16,120,128]{2,1,0:T(8,128)(2,1)} %pair_sum.2), calls=%async_computation | async-start | bytes 983040 | tf_op jit(solution)/shard_map/all_to_all | solution.py:593
  40.1 13.1 %all-to-all-start.1 = ((bf16[16,120,128]{2,1,0:T(8,128)(2,1)}), bf16[16,120,128]{2,1,0:T(8,128)(2,1)S(1)}, u32[]{:S(2)}, u32[]{:S(2)}) async-start(bf16[16,120,128]{2,1,0:T(8,128)(2,1)} %chip_sums.2), calls=%async_computation.1 | async-start | bytes 983040 | tf_op jit(solution)/shard_map/all_to_all | solution.py:593
  43.7 9.5 %copy-start.1 = (bf16[1920,128]{1,0:T(8,128)(2,1)S(1)}, bf16[1920,128]{1,0:T(8,128)(2,1)}, u32[]{:S(2)}) copy-start(bf16[1920,128]{1,0:T(8,128)(2,1)} %get-tuple-element.37.own_ref) | copy-start | bytes 1474564
  53.2 4.6 %copy-start.6 = (bf16[16,120,128]{2,1,0:T(8,128)(2,1)}, bf16[16,120,128]{2,1,0:T(8,128)(2,1)S(1)}, u32[]{:S(2)}) copy-start(bf16[16,120,128]{2,1,0:T(8,128)(2,1)S(1)} %all-to-all-done.1) | copy-start | bytes 1474564
  53.4 4.4 %collective-permute-start.2 = (bf16[1920,128]{1,0:T(8,128)(2,1)S(1)}, bf16[1920,128]{1,0:T(8,128)(2,1)S(1)}, u32[]{:S(2)}, u32[]{:S(2)}) collective-permute-start(bf16[1920,128]{1,0:T(8,128)(2,1)S(1)} %fusion), channel_id=1, source_target_pairs={{0,4},{4,0},{8,12},{12,8},{16,20},{20,16},{24,28},{28,24},{32,36},... | collective-permute-start | bytes 1474568 | tf_op jit(solution)/shard_map/ppermute | solution.py:587
  57.8 0.8 copy-start.9
  69.2 2.2 %collective-permute-start.3 = (bf16[1920,128]{1,0:T(8,128)(2,1)}, bf16[1920,128]{1,0:T(8,128)(2,1)S(1)}, u32[]{:S(2)}, u32[]{:S(2)}) collective-permute-start(bf16[1920,128]{1,0:T(8,128)(2,1)} %get-tuple-element.45), channel_id=1, source_target_pairs={{0,4},{4,0},{8,12},{12,8},{16,20},{20,16},{24,28},{28,24},{32,36},... | collective-permute-start | bytes 1474568 | tf_op jit(solution)/shard_map/ppermute | solution.py:587
  69.6 52.1 %collective-permute-start.6 = (bf16[256,3072]{1,0:T(8,128)(2,1)}, bf16[256,3072]{1,0:T(8,128)(2,1)}, u32[]{:S(2)}, u32[]{:S(2)}) collective-permute-start(bf16[256,3072]{1,0:T(8,128)(2,1)} %get-tuple-element.62), channel_id=1, source_target_pairs={{3,0},{0,1},{1,2},{2,3},{7,4},{4,5},{5,6},{6,7},{11,8},{8,9},{9,10... | collective-permute-start | bytes 4718600 | tf_op jit(solution)/shard_map/ppermute | solution.py:619
  71.3 13.1 %copy-start.5 = (bf16[1920,128]{1,0:T(8,128)(2,1)}, bf16[1920,128]{1,0:T(8,128)(2,1)S(1)}, u32[]{:S(2)}) copy-start(bf16[1920,128]{1,0:T(8,128)(2,1)S(1)} %collective-permute-done.3.other_ref.other_hbm) | copy-start | bytes 1474564
  71.3 1.2 copy-start.2
  73.5 14.2 %all-to-all-start.2 = ((bf16[16,120,128]{2,1,0:T(8,128)(2,1)}), bf16[16,120,128]{2,1,0:T(8,128)(2,1)S(1)}, u32[]{:S(2)}, u32[]{:S(2)}) async-start(bf16[16,120,128]{2,1,0:T(8,128)(2,1)} %pair_sum.3), calls=%async_computation.2 | async-start | bytes 983040 | tf_op jit(solution)/shard_map/all_to_all | solution.py:593
  88.5 13.4 %all-to-all-start.3 = ((bf16[16,120,128]{2,1,0:T(8,128)(2,1)}), bf16[16,120,128]{2,1,0:T(8,128)(2,1)S(1)}, u32[]{:S(2)}, u32[]{:S(2)}) async-start(bf16[16,120,128]{2,1,0:T(8,128)(2,1)} %chip_sums.3), calls=%async_computation.3 | async-start | bytes 983040 | tf_op jit(solution)/shard_map/all_to_all | solution.py:593
  92.3 9.6 %copy-start.3 = (bf16[1920,128]{1,0:T(8,128)(2,1)S(1)}, bf16[1920,128]{1,0:T(8,128)(2,1)}, u32[]{:S(2)}) copy-start(bf16[1920,128]{1,0:T(8,128)(2,1)} %get-tuple-element.44.own_ref) | copy-start | bytes 1474564
  101.9 4.1 %copy-start.7 = (bf16[16,120,128]{2,1,0:T(8,128)(2,1)}, bf16[16,120,128]{2,1,0:T(8,128)(2,1)S(1)}, u32[]{:S(2)}) copy-start(bf16[16,120,128]{2,1,0:T(8,128)(2,1)S(1)} %all-to-all-done.3) | copy-start | bytes 1474564
  102.1 3.8 %collective-permute-start.4 = (bf16[1920,128]{1,0:T(8,128)(2,1)S(1)}, bf16[1920,128]{1,0:T(8,128)(2,1)S(1)}, u32[]{:S(2)}, u32[]{:S(2)}) collective-permute-start(bf16[1920,128]{1,0:T(8,128)(2,1)S(1)} %fusion.1), channel_id=1, source_target_pairs={{0,4},{4,0},{8,12},{12,8},{16,20},{20,16},{24,28},{28,24},{32,36},... | collective-permute-start | bytes 1474568 | tf_op jit(solution)/shard_map/ppermute | solution.py:587
  116.0 6.4 %collective-permute-start.5 = (f32[8,3072]{1,0:T(8,128)}, f32[8,3072]{1,0:T(8,128)S(1)}, u32[]{:S(2)}, u32[]{:S(2)}) collective-permute-start(f32[8,3072]{1,0:T(8,128)} %get-tuple-element.61), channel_id=1, source_target_pairs={{4,0},{8,4},{12,8},{16,12},{20,16},{24,20},{28,24},{32,28},{36,32}... | collective-permute-start | bytes 294920 | tf_op jit(solution)/shard_map/ppermute | solution.py:614
  118.2 12.1 %collective-permute-start.7 = (bf16[64,3072]{1,0:T(8,128)(2,1)}, bf16[64,3072]{1,0:T(8,128)(2,1)S(1)}, u32[]{:S(2)}, u32[]{:S(2)}) collective-permute-start(bf16[64,3072]{1,0:T(8,128)(2,1)} %get-tuple-element.64), channel_id=1, source_target_pairs={{1,0},{2,1},{3,2},{0,3},{5,4},{6,5},{7,6},{4,7},{9,8},{10,9},{11,1... | collective-permute-start | bytes 1179656 | tf_op jit(solution)/shard_map/ppermute | solution.py:619
  121.1 17.7 %collective-permute-start.8 = (bf16[64,3072]{1,0:T(8,128)(2,1)}, bf16[64,3072]{1,0:T(8,128)(2,1)S(1)}, u32[]{:S(2)}, u32[]{:S(2)}) collective-permute-start(bf16[64,3072]{1,0:T(8,128)(2,1)} %get-tuple-element.65), channel_id=1, source_target_pairs={{1,0},{2,1},{3,2},{0,3},{5,4},{6,5},{7,6},{4,7},{9,8},{10,9},{11,1... | collective-permute-start | bytes 1179656 | tf_op jit(solution)/shard_map/ppermute | solution.py:619
  121.5 25.6 %collective-permute-start.9 = (bf16[64,3072]{1,0:T(8,128)(2,1)}, bf16[64,3072]{1,0:T(8,128)(2,1)S(1)}, u32[]{:S(2)}, u32[]{:S(2)}) collective-permute-start(bf16[64,3072]{1,0:T(8,128)(2,1)} %get-tuple-element.66), channel_id=1, source_target_pairs={{1,0},{2,1},{3,2},{0,3},{5,4},{6,5},{7,6},{4,7},{9,8},{10,9},{11,1... | collective-permute-start | bytes 1179656 | tf_op jit(solution)/shard_map/ppermute | solution.py:619
  126.4 29.1 %collective-permute-start.10 = (bf16[64,3072]{1,0:T(8,128)(2,1)}, bf16[64,3072]{1,0:T(8,128)(2,1)S(1)}, u32[]{:S(2)}, u32[]{:S(2)}) collective-permute-start(bf16[64,3072]{1,0:T(8,128)(2,1)} %get-tuple-element.67), channel_id=1, source_target_pairs={{1,0},{2,1},{3,2},{0,3},{5,4},{6,5},{7,6},{4,7},{9,8},{10,9},{11,1... | collective-permute-start | bytes 1179656 | tf_op jit(solution)/shard_map/ppermute | solution.py:619
  (3 other events, 2.1 us)

commit v4 on v3

--- a/solution.py
+++ b/solution.py
@@ -47,13 +47,14 @@
     return [jax.ShapeDtypeStruct(dims, dtype) for dims, dtype in shapes]
 
 
-def streamed(kernel, operands, out_shape, name, micros, scratch, copies, limit_mib=62):
+def streamed(kernel, operands, out_shape, name, micros, scratch, copies, aliases=None, limit_mib=62):
     return pl.pallas_call(
         kernel,
         in_specs=[IN_HBM] * len(operands),
         out_specs=[IN_HBM] * len(out_shape),
         out_shape=shaped(*out_shape),
         scratch_shapes=[pltpu.VMEM(dims, dtype) for dims, dtype in scratch] + [pltpu.SemaphoreType.DMA((copies,))],
+        input_output_aliases=aliases or {},
         name=name,
         **params(micros, limit_mib),
     )(*operands)
@@ -251,11 +252,11 @@
     wait_all(out)
 
 
-def states_in(copies, core, before_hbm, other_hbm, theirs_hbm, state_ref, other_ref):
+def states_in(copies, own_half, before_hbm, other_hbm, theirs_hbm, state_ref, other_ref):
     return [
-        copies.start(before_hbm, state_ref.at[half_rows(core)]),
+        copies.start(before_hbm, state_ref.at[half_rows(own_half)]),
         copies.start(other_hbm, other_ref),
-        copies.start(theirs_hbm, state_ref.at[half_rows(1 - core)]),
+        copies.start(theirs_hbm, state_ref.at[half_rows(1 - own_half)]),
     ]
 
 
@@ -271,60 +272,53 @@
     return dot(both, ones, ((1,), (0,))) * (1.0 / VDIM)
 
 
-def output_kernel(
-    cols_hbm,
-    inside_low_hbm,
-    inside_high_hbm,
-    before_hbm,
-    other_hbm,
-    theirs_hbm,
-    x_hbm,
-    grad_hbm,
-    scale_hbm,
-    out_hbm,
-    numer_hbm,
-    prefix_hbm,
-    grad_own_hbm,
-    grad_away_hbm,
-    cols_ref,
-    inside_ref,
-    prefix_ref,
-    other_ref,
-    x_ref,
-    grad_ref,
-    scale_ref,
-    out_ref,
-    numer_ref,
-    state_ref,
-    sems,
-):
+def output_kernel(turn, cols_hbm, inside_low_hbm, inside_high_hbm, *refs):
+    count = 2 if turn == 0 else 1
+    state_hbms, refs = refs[:count], refs[count:]
+    x_hbm, grad_hbm, scale_hbm = refs[:3]
+    refs = refs[3 + 3 * turn :]
+    out_hbm, numer_hbm, prefix_hbm, grads_hbm = refs[:4]
+    cols_ref, inside_ref, prefix_ref, other_ref, x_ref, grad_ref, scale_ref, out_ref, numer_ref, state_ref, sems = refs[4:]
     copies = Copies(sems)
     core = core_here()
-    middle = cols_ref.shape[0] // 2
-    first = states_in(copies, core, before_hbm, other_hbm, theirs_hbm, prefix_ref, other_ref)
-    first += [copies.start(cols_hbm.at[:middle], cols_ref.at[:middle]), copies.start(scale_hbm, scale_ref)]
+    half = core if turn == 0 else 1 - core
+    half_lane, half_cols = HALF * VDIM, HALF * FEAT
+
+    def at(step):
+        return pl.ds(pl.multiple_of(half * half_lane + step * STEP_LANES, STEP_LANES), STEP_LANES)
+
+    def rows_at(step):
+        size = STEP_HEADS * PACKED
+        return pl.ds(pl.multiple_of(half * HALF_STATE + step * size, size), size)
+
+    first = [copies.start(state_hbms[0], prefix_ref)]
+    if turn == 0:
+        first.append(copies.start(state_hbms[1], other_ref))
+    first.append(copies.start(cols_hbm.at[pl.ds(pl.multiple_of(half * half_cols, half_cols), half_cols)], cols_ref))
+    first.append(copies.start(scale_hbm.at[:, pl.ds(pl.multiple_of(half * half_lane, half_lane), half_lane)], scale_ref))
     blocks = []
-    for step in range(STEPS):
-        source = inside_low_hbm if step < STEPS // 2 else inside_high_hbm
-        blocks.append(
-            [copies.start(source.at[:, lanes_of(step % (STEPS // 2))], inside_ref.at[:, lanes_of(step)])]
-            + by_lanes(copies, x_hbm, x_ref, [step])
-            + by_lanes(copies, grad_hbm, grad_ref, [step])
-        )
+    for step in range(STEPS // 2):
+        lanes = lanes_of(step)
+        low = copies.make(inside_low_hbm.at[:, lanes], inside_ref.at[:, lanes])
+        high = pltpu.make_async_copy(inside_high_hbm.at[:, lanes], inside_ref.at[:, lanes], copies.last())
+        pl.when(half == 0)(low.start)
+        pl.when(half != 0)(high.start)
+        x_in = copies.start(x_hbm.at[:, at(step)], x_ref.at[:, lanes])
+        blocks.append([low, x_in, copies.start(grad_hbm.at[:, at(step)], grad_ref.at[:, lanes])])
     wait_all(first)
-    adds_other = (False, core == 1)
     side = lax.broadcasted_iota(jnp.int32, (2 * VDIM, 2 * VDIM), 0) < VDIM
     other_side = lax.broadcasted_iota(jnp.int32, (2 * VDIM, 2 * VDIM), 1) < VDIM
     ones = jnp.where(side == other_side, 1.0, 0.0).astype(bf16)
     out = []
-    for step in range(STEPS):
+    for step in range(STEPS // 2):
         wait_all(blocks[step])
-        for head in range(STEP_HEADS):
-            place = step * STEP_HEADS + head
-            lanes = head_of(place, VDIM)
+        for place in range(step * STEP_HEADS, (step + 1) * STEP_HEADS):
+            lanes, state_rows = head_of(place, VDIM), head_of(place, PACKED)
             feat = taylor_rows(cols_ref[head_of(place, FEAT)].astype(f32), 2.0)
-            prefix = state_of(place, adds_other, prefix_ref, other_ref)
-            prefix_ref[head_of(place, PACKED)] = prefix
+            prefix = prefix_ref[state_rows]
+            if turn == 0:
+                prefix = jnp.where(core == 1, add_states(prefix, other_ref[state_rows]), prefix)
+                prefix_ref[state_rows] = prefix
             numer = inside_ref[:, lanes].astype(f32) + dot(feat, prefix, ((0,), (0,)))
             scale = scale_ref[:, lanes]
             grad = grad_ref[:, lanes].astype(f32) * scale
@@ -334,11 +328,12 @@
             out_ref[:, lanes] = (x_ref[:, lanes].astype(f32) + scale * (numer * inv)).astype(bf16)
             grad_numer = (inv * grad - numer * (inv * inv * inv * mean)).astype(bf16)
             numer_ref[:, lanes] = grad_numer
-            state_ref[head_of(place, PACKED)] = dot(feat, grad_numer, ((1,), (0,))).astype(bf16)
-        state_rows = head_of(step, STEP_HEADS * PACKED)
-        out.append(state_out(copies, core, step, state_ref, grad_own_hbm, grad_away_hbm))
-        out += by_lanes(copies, out_ref, out_hbm, [step]) + by_lanes(copies, numer_ref, numer_hbm, [step])
-        out.append(copies.start(prefix_ref.at[state_rows], prefix_hbm.at[state_rows]))
+            state_ref[state_rows] = dot(feat, grad_numer, ((1,), (0,))).astype(bf16)
+        state_rows, lanes = head_of(step, STEP_HEADS * PACKED), lanes_of(step)
+        out.append(copies.start(state_ref.at[state_rows], grads_hbm.at[state_rows]))
+        out.append(copies.start(out_ref.at[:, lanes], out_hbm.at[:, at(step)]))
+        out.append(copies.start(numer_ref.at[:, lanes], numer_hbm.at[:, at(step)]))
+        out.append(copies.start(prefix_ref.at[state_rows], prefix_hbm.at[rows_at(step)]))
     wait_all(out)
 
 
@@ -442,7 +437,7 @@
     core = core_here()
     middle, rows = cols_ref.shape[0], cols_ref.shape[1]
     half_cols = middle // 2
-    first = states_in(copies, core, before_hbm, other_hbm, theirs_hbm, state_ref, other_ref)
+    first = states_in(copies, 1 - core, before_hbm, other_hbm, theirs_hbm, state_ref, other_ref)
     first.append(copies.start(cols_hbm.at[middle:], cols_ref))
     for half, source in enumerate((cols_low_hbm, cols_high_hbm)):
         for kind in range(2):
@@ -468,7 +463,7 @@
     weights.append(copies.start(x_hbm, x_ref))
     grad_in = copies.start(grad_hbm, grad_ref)
     wait_all(first)
-    adds_other = (core == 0, False)
+    adds_other = (False, core == 0)
     for step in range(STEPS):
         wait_all(blocks[step])
         for head in range(STEP_HEADS):
@@ -662,15 +657,24 @@
     _, values_then = lax.optimization_barrier((got, values))
     before, inside_high = lax.optimization_barrier((over_chips(chip_sums(got, False)), inside(1, cols, values_then)))
     before, theirs = scan_second(before, own, parity == 0)
-    output, numer, prefix, grad_own, grad_away = streamed(
-        output_kernel,
-        [cols, inside_low, inside_high, before, other, theirs, x, grad, out_gain],
-        [tokens, tokens, all_state, half_state, half_state],
-        "output",
-        8,
-        [cols_shape, tokens, all_state, half_state, tokens, tokens, ((1, width), f32), tokens, tokens, all_state],
-        5 + 3 * STEPS + 4 * STEPS,
-    )
+    half_tokens = ((rows, half_width), bf16)
+
+    def outputs(turn, states, filled):
+        operands = [cols, inside_low, inside_high, *states, x, grad, out_gain, *filled]
+        return streamed(
+            functools.partial(output_kernel, turn),
+            operands,
+            [tokens, tokens, all_state, half_state],
+            "output",
+            5,
+            [((both // 4, rows), bf16), half_tokens, half_state, half_state, half_tokens, half_tokens]
+            + [((1, half_width), f32), half_tokens, half_tokens, half_state],
+            4 + 3 * (STEPS // 2) + 4 * (STEPS // 2),
+            aliases={len(operands) - len(filled) + k: k for k in range(len(filled))},
+        )
+
+    *filled, grad_away = outputs(0, [before, other], [])
+    output, numer, prefix, grad_own = outputs(1, [theirs], filled)
     sent_forward = section_pass(output, 1)
 
     def inside_back(half, numer):

time: 157 us -> 157 us (level)
  waiting for transfers between devices: 51.8 us -> 49.6 us
  Pallas kernels: 56.6 us -> 58.6 us
    pallas_call x8 -> x9, Pallas kernels: 53 us -> 55 us  [streamed(): pl.pallas_call(kernel, in_specs=[IN_HBM] * len(operands), out_specs=[IN_H...]
    ppermute x4, waiting for transfers between devices: 5.45 us -> 3.56 us  [core_swap(): return lax.ppermute(block, 'seq', [(i, i ^ 1) for i in range(count)])]
  transfers between devices with their start and end apart: 15 -> 15, of which waited for: 14 -> 12; matrix products, arithmetic and copies ran while one was open for 0% -> 0% of each run, Pallas kernels for 23% -> 31%
where the time goes in v4:
time: 157 us; the launch traced here: 156 us
  Pallas kernels  58.6 us (37%)
  waiting for transfers between devices  49.6 us (32%)
  starting transfers between devices  39 us (25%)
  local copies, waits for them, and re-layouts  6.16 us (4%)
  other arithmetic  1.63 us (1%)
    pallas_call x9, Pallas kernels, streamed(): pl.pallas_call(kernel, in_specs=[IN_HBM] * len(operands), out_specs=[IN_H...  55 us
    ppermute x5, waiting for transfers between devices, section_pass(): lax.ppermute(block, 'section', [((i - distance) % count, i) for i in rang...  26.5 us
    all_to_all x4, starting transfers between devices, over_chips(): lax.all_to_all(block, 'seq', 0, 0, tiled=True, axis_index_groups=groups)  20.2 us
    all_to_all x4, waiting for transfers between devices, over_chips(): lax.all_to_all(block, 'seq', 0, 0, tiled=True, axis_index_groups=groups)  17.2 us
    ppermute x2, starting transfers between devices, neighbour_rows(): return lax.ppermute(edge, 'seq', route)  6.78 us
    ppermute x5, starting transfers between devices, section_pass(): lax.ppermute(block, 'section', [((i - distance) % count, i) for i in rang...  6.58 us
    ppermute x4, starting transfers between devices, core_swap(): return lax.ppermute(block, 'seq', [(i, i ^ 1) for i in range(count)])  5.44 us
    unnamed x24, local copies, waits for them, and re-layouts  5.26 us
  transfers between devices with their start and end apart: 15, of which 12 were waited for; matrix products, arithmetic and copies ran while one was open for 0% of the time, Pallas kernels for 31%

profile of v4, /device:TPU:1, one launch (start us, length us, event | category | flops | bytes accessed | tf_op | source)
XLA Modules:
  0.0 155.8 jit_solution(1767590732938543806)
XLA Ops:
  1.5 4.5 %collective-permute-start = (bf16[16,3072]{1,0:T(8,128)(2,1)S(1)}, bf16[16,3072]{1,0:T(8,128)(2,1)S(1)}, u32[]{:S(2)}, u32[]{:S(2)}) collective-permute-start(bf16[16,3072]{1,0:T(8,128)(2,1)S(1)} %slice_bitcast_fusion), channel_id=1, source_target_pairs={{0,4},{4,8},{8,12},{12,16},{16,20},{20,24},{24,28},{28,32},{32,36}... | collective-permute-start | bytes 294920 | tf_op jit(solution)/shard_map/ppermute | solution.py:609
  8.3 7.8 %state.1 = (bf16[256,3072]{1,0:T(8,128)(2,1)}, bf16[768,256]{1,0:T(8,128)(2,1)}, bf16[1920,128]{1,0:T(8,128)(2,1)}, bf16[1920,128]{1,0:T(8,128)(2,1)}) custom-call(bf16[256,3072]{1,0:T(8,128)(2,1)} %bitcast.16, f32[1,3072]{1,0:T(1,128)} %refs_6_.1, bf16[3072,384]{1,0:T(8,128)(2,1)} %bitcast.21, bf16[3072,384]{1,0:T(8,128)(2,1)} %bitcast.23, ...), custom_call_target="tpu_custom_call" | custom-call | flops 8800000000 | bytes 65536 | tf_op jit(solution)/shard_map/state/pallas_call | solution.py:51
  16.2 2.1 %collective-permute-done.1.other_ref.refs_1_ = bf16[1920,128]{1,0:T(8,128)(2,1)S(1)} collective-permute-done((bf16[1920,128]{1,0:T(8,128)(2,1)}, bf16[1920,128]{1,0:T(8,128)(2,1)S(1)}, u32[]{:S(2)}, u32[]{:S(2)}) %collective-permute-start.1) | collective-permute-done | bytes 491552 | tf_op jit(solution)/shard_map/ppermute | solution.py:582
  20.4 8.5 %all-to-all-start = ((bf16[16,120,128]{2,1,0:T(8,128)(2,1)}), bf16[16,120,128]{2,1,0:T(8,128)(2,1)S(1)}, u32[]{:S(2)}, u32[]{:S(2)}) async-start(bf16[16,120,128]{2,1,0:T(8,128)(2,1)} %pair_sum.2), calls=%async_computation | async-start | bytes 983040 | tf_op jit(solution)/shard_map/all_to_all | solution.py:588
  28.9 3.6 %inside.2.inside_low_hbm = bf16[256,1536]{1,0:T(8,128)(2,1)} custom-call(bf16[768,256]{1,0:T(8,128)(2,1)} %get-tuple-element.38.cols_hbm, bf16[256,3072]{1,0:T(8,128)(2,1)} %get-tuple-element.44.values_hbm), custom_call_target="tpu_custom_call" | custom-call | flops 3300000000 | bytes 65536 | tf_op jit(solution)/shard_map/inside/pallas_call | solution.py:51
  32.5 6.7 %all-to-all-done.got_ref = bf16[16,120,128]{2,1,0:T(8,128)(2,1)S(1)} async-done(((bf16[16,120,128]{2,1,0:T(8,128)(2,1)}), bf16[16,120,128]{2,1,0:T(8,128)(2,1)S(1)}, u32[]{:S(2)}, u32[]{:S(2)}) %all-to-all-start) | async-done | bytes 491552 | tf_op jit(solution)/shard_map/all_to_all | solution.py:588
  40.1 3.6 %all-to-all-start.1 = ((bf16[16,120,128]{2,1,0:T(8,128)(2,1)}), bf16[16,120,128]{2,1,0:T(8,128)(2,1)S(1)}, u32[]{:S(2)}, u32[]{:S(2)}) async-start(bf16[16,120,128]{2,1,0:T(8,128)(2,1)} %chip_sums.2), calls=%async_computation.1 | async-start | bytes 983040 | tf_op jit(solution)/shard_map/all_to_all | solution.py:588
  43.7 3.7 %inside.3.inside_high_hbm = bf16[256,1536]{1,0:T(8,128)(2,1)} custom-call(bf16[768,256]{1,0:T(8,128)(2,1)} %get-tuple-element.38.cols_hbm, bf16[256,3072]{1,0:T(8,128)(2,1)} %get-tuple-element.44.values_hbm), custom_call_target="tpu_custom_call" | custom-call | flops 3300000000 | bytes 65536 | tf_op jit(solution)/shard_map/inside/pallas_call | solution.py:51
  47.4 5.8 %all-to-all-done.1 = bf16[16,120,128]{2,1,0:T(8,128)(2,1)S(1)} async-done(((bf16[16,120,128]{2,1,0:T(8,128)(2,1)}), bf16[16,120,128]{2,1,0:T(8,128)(2,1)S(1)}, u32[]{:S(2)}, u32[]{:S(2)}) %all-to-all-start.1) | async-done | bytes 491552 | tf_op jit(solution)/shard_map/all_to_all | solution.py:588
  53.4 2.9 %collective-permute-start.2 = (bf16[1920,128]{1,0:T(8,128)(2,1)S(1)}, bf16[1920,128]{1,0:T(8,128)(2,1)S(1)}, u32[]{:S(2)}, u32[]{:S(2)}) collective-permute-start(bf16[1920,128]{1,0:T(8,128)(2,1)S(1)} %fusion), channel_id=1, source_target_pairs={{0,4},{4,0},{8,12},{12,8},{16,20},{20,16},{24,28},{28,24},{32,36},... | collective-permute-start | bytes 1474568 | tf_op jit(solution)/shard_map/ppermute | solution.py:582
  56.3 6.4 %output.2 = (bf16[256,3072]{1,0:T(8,128)(2,1)}, bf16[256,3072]{1,0:T(8,128)(2,1)}, bf16[3840,128]{1,0:T(8,128)(2,1)}, bf16[1920,128]{1,0:T(8,128)(2,1)}) custom-call(bf16[768,256]{1,0:T(8,128)(2,1)} %get-tuple-element.38.cols_hbm, bf16[256,1536]{1,0:T(8,128)(2,1)} %inside.2.inside_low_hbm, bf16[256,1536]{1,0:T(8,128)(2,1)} %inside.3.inside_high_hbm, ...), custom_call_target="tpu_custom_call" | custom-call | flops 5500000256 | bytes 65536 | tf_op jit(solution)/shard_map/output/pallas_call | solution.py:51
  63.9 6.2 %output.3 = (bf16[256,3072]{1,0:T(8,128)(2,1)}, bf16[256,3072]{1,0:T(8,128)(2,1)}, bf16[3840,128]{1,0:T(8,128)(2,1)}, bf16[1920,128]{1,0:T(8,128)(2,1)}) custom-call(bf16[768,256]{1,0:T(8,128)(2,1)} %get-tuple-element.38.cols_hbm, bf16[256,1536]{1,0:T(8,128)(2,1)} %inside.2.inside_low_hbm, ...), custom_call_target="tpu_custom_call", output_to_operand_aliasing={{0}: (7, {}), {1}: (8, {}), {2}: (9, {})} | custom-call | flops 5500000256 | bytes 65536 | tf_op jit(solution)/shard_map/output/pallas_call | solution.py:51
  72.3 3.6 %all-to-all-start.2 = ((bf16[16,120,128]{2,1,0:T(8,128)(2,1)}), bf16[16,120,128]{2,1,0:T(8,128)(2,1)S(1)}, u32[]{:S(2)}, u32[]{:S(2)}) async-start(bf16[16,120,128]{2,1,0:T(8,128)(2,1)} %pair_sum.3), calls=%async_computation.2 | async-start | bytes 983040 | tf_op jit(solution)/shard_map/all_to_all | solution.py:588
  77.2 7.4 %inside_back.2 = (f32[384,256]{1,0:T(8,128)}, bf16[256,1536]{1,0:T(8,128)(2,1)}) custom-call(bf16[768,256]{1,0:T(8,128)(2,1)} %get-tuple-element.38.cols_hbm, bf16[256,3072]{1,0:T(8,128)(2,1)} %get-tuple-element.44.values_hbm, bf16[256,3072]{1,0:T(8,128)(2,1)} %get-tuple-element.57.numer_hbm, bf16[3840,128]{1,0:T(8,128)(2,1)} %get-tuple-element.53.prefix_hbm), custom_call_target="tpu_custom_call" | custom-call | flops 5500000256 | bytes 65536 | tf_op jit(solution)/shard_map/inside_back/pallas_call | solution.py:51
  87.4 4.6 %all-to-all-start.3 = ((bf16[16,120,128]{2,1,0:T(8,128)(2,1)}), bf16[16,120,128]{2,1,0:T(8,128)(2,1)S(1)}, u32[]{:S(2)}, u32[]{:S(2)}) async-start(bf16[16,120,128]{2,1,0:T(8,128)(2,1)} %chip_sums.3), calls=%async_computation.3 | async-start | bytes 983040 | tf_op jit(solution)/shard_map/all_to_all | solution.py:588
  92.0 7.4 %inside_back.3 = (f32[384,256]{1,0:T(8,128)}, bf16[256,1536]{1,0:T(8,128)(2,1)}) custom-call(bf16[768,256]{1,0:T(8,128)(2,1)} %get-tuple-element.38.cols_hbm, bf16[256,3072]{1,0:T(8,128)(2,1)} %get-tuple-element.44.values_hbm, bf16[256,3072]{1,0:T(8,128)(2,1)} %get-tuple-element.57.numer_hbm, bf16[3840,128]{1,0:T(8,128)(2,1)} %get-tuple-element.53.prefix_hbm), custom_call_target="tpu_custom_call" | custom-call | flops 5500000256 | bytes 65536 | tf_op jit(solution)/shard_map/inside_back/pallas_call | solution.py:51
  99.4 2.7 %all-to-all-done.3 = bf16[16,120,128]{2,1,0:T(8,128)(2,1)S(1)} async-done(((bf16[16,120,128]{2,1,0:T(8,128)(2,1)}), bf16[16,120,128]{2,1,0:T(8,128)(2,1)S(1)}, u32[]{:S(2)}, u32[]{:S(2)}) %all-to-all-start.3) | async-done | bytes 491552 | tf_op jit(solution)/shard_map/all_to_all | solution.py:588
  102.3 2.1 %collective-permute-start.4 = (bf16[1920,128]{1,0:T(8,128)(2,1)S(1)}, bf16[1920,128]{1,0:T(8,128)(2,1)S(1)}, u32[]{:S(2)}, u32[]{:S(2)}) collective-permute-start(bf16[1920,128]{1,0:T(8,128)(2,1)S(1)} %fusion.1), channel_id=1, source_target_pairs={{0,4},{4,0},{8,12},{12,8},{16,20},{20,16},{24,28},{28,24},{32,36},... | collective-permute-start | bytes 1474568 | tf_op jit(solution)/shard_map/ppermute | solution.py:582
  106.7 9.2 %late.1 = (f32[8,3072]{1,0:T(8,128)}, f32[64,3072]{1,0:T(8,128)}, f32[64,128]{1,0:T(8,128)}, bf16[64,3072]{1,0:T(8,128)(2,1)}, bf16[64,3072]{1,0:T(8,128)(2,1)}, /*index=5*/bf16[64,3072]{1,0:T(8,128)(2,1)}) custom-call(bf16[768,256]{1,0:T(8,128)(2,1)} %get-tuple-element.38.cols_hbm, bf16[256,3072]{1,0:T(8,128)(2,1)} %get-tuple-element.44.values_hbm, ...), custom_call_target="tpu_custom_call" | custom-call | flops 9900000256 | bytes 65536 | tf_op jit(solution)/shard_map/late/pallas_call | solution.py:51
  115.9 2.3 %collective-permute-start.5 = (f32[8,3072]{1,0:T(8,128)}, f32[8,3072]{1,0:T(8,128)S(1)}, u32[]{:S(2)}, u32[]{:S(2)}) collective-permute-start(f32[8,3072]{1,0:T(8,128)} %get-tuple-element.67), channel_id=1, source_target_pairs={{4,0},{8,4},{12,8},{16,12},{20,16},{24,20},{28,24},{32,28},{36,32}... | collective-permute-start | bytes 294920 | tf_op jit(solution)/shard_map/ppermute | solution.py:609
  123.0 3.3 %last.1 = (bf16[64,3072]{1,0:T(8,128)(2,1)}, bf16[256,3072]{1,0:T(8,128)(2,1)}) custom-call(f32[64,3072]{1,0:T(8,128)} %get-tuple-element.65.refs_0_, f32[64,128]{1,0:T(8,128)} %get-tuple-element.66.refs_1_, bf16[256,3072]{1,0:T(8,128)(2,1)} %bitcast.20, bf16[256,3072]{1,0:T(8,128)(2,1)} %bitcast.28, f32[8,3072]{1,0:T(8,128)} %copy-done.10, ...), custom_call_target="tpu_custom_call" | custom-call | flops 2200000000 | bytes 65536 | tf_op jit(solution)/shard_map/last/pallas_call | solution.py:51
  129.6 8.4 %collective-permute-done.8 = bf16[64,3072]{1,0:T(8,128)(2,1)S(1)} collective-permute-done((bf16[64,3072]{1,0:T(8,128)(2,1)}, bf16[64,3072]{1,0:T(8,128)(2,1)S(1)}, u32[]{:S(2)}, u32[]{:S(2)}) %collective-permute-start.8) | collective-permute-done | bytes 393248 | tf_op jit(solution)/shard_map/ppermute | solution.py:614
  138.0 8.4 %collective-permute-done.9 = bf16[64,3072]{1,0:T(8,128)(2,1)S(1)} collective-permute-done((bf16[64,3072]{1,0:T(8,128)(2,1)}, bf16[64,3072]{1,0:T(8,128)(2,1)S(1)}, u32[]{:S(2)}, u32[]{:S(2)}) %collective-permute-start.9) | collective-permute-done | bytes 393248 | tf_op jit(solution)/shard_map/ppermute | solution.py:614
  146.4 8.1 %collective-permute-done.10 = bf16[64,3072]{1,0:T(8,128)(2,1)S(1)} collective-permute-done((bf16[64,3072]{1,0:T(8,128)(2,1)}, bf16[64,3072]{1,0:T(8,128)(2,1)S(1)}, u32[]{:S(2)}, u32[]{:S(2)}) %collective-permute-start.10) | collective-permute-done | bytes 393248 | tf_op jit(solution)/shard_map/ppermute | solution.py:614
  (47 shorter events, 25.7 us)
Async XLA Ops:
  1.5 6.1 %collective-permute-start = (bf16[16,3072]{1,0:T(8,128)(2,1)S(1)}, bf16[16,3072]{1,0:T(8,128)(2,1)S(1)}, u32[]{:S(2)}, u32[]{:S(2)}) collective-permute-start(bf16[16,3072]{1,0:T(8,128)(2,1)S(1)} %slice_bitcast_fusion), channel_id=1, source_target_pairs={{0,4},{4,8},{8,12},{12,16},{16,20},{20,24},{24,28},{28,32},{32,36}... | collective-permute-start | bytes 294920 | tf_op jit(solution)/shard_map/ppermute | solution.py:609
  16.1 2.2 %collective-permute-start.1 = (bf16[1920,128]{1,0:T(8,128)(2,1)}, bf16[1920,128]{1,0:T(8,128)(2,1)S(1)}, u32[]{:S(2)}, u32[]{:S(2)}) collective-permute-start(bf16[1920,128]{1,0:T(8,128)(2,1)} %get-tuple-element.41), channel_id=1, source_target_pairs={{0,4},{4,0},{8,12},{12,8},{16,20},{20,16},{24,28},{28,24},{32,36},... | collective-permute-start | bytes 1474568 | tf_op jit(solution)/shard_map/ppermute | solution.py:582
  18.2 14.3 %copy-start.5 = (bf16[1920,128]{1,0:T(8,128)(2,1)}, bf16[1920,128]{1,0:T(8,128)(2,1)S(1)}, u32[]{:S(2)}) copy-start(bf16[1920,128]{1,0:T(8,128)(2,1)S(1)} %collective-permute-done.1.other_ref.refs_1_) | copy-start | bytes 1474564
  18.2 1.2 copy-start
  20.4 18.9 %all-to-all-start = ((bf16[16,120,128]{2,1,0:T(8,128)(2,1)}), bf16[16,120,128]{2,1,0:T(8,128)(2,1)S(1)}, u32[]{:S(2)}, u32[]{:S(2)}) async-start(bf16[16,120,128]{2,1,0:T(8,128)(2,1)} %pair_sum.2), calls=%async_computation | async-start | bytes 983040 | tf_op jit(solution)/shard_map/all_to_all | solution.py:588
  40.1 13.1 %all-to-all-start.1 = ((bf16[16,120,128]{2,1,0:T(8,128)(2,1)}), bf16[16,120,128]{2,1,0:T(8,128)(2,1)S(1)}, u32[]{:S(2)}, u32[]{:S(2)}) async-start(bf16[16,120,128]{2,1,0:T(8,128)(2,1)} %chip_sums.2), calls=%async_computation.1 | async-start | bytes 983040 | tf_op jit(solution)/shard_map/all_to_all | solution.py:588
  43.7 9.5 %copy-start.1 = (bf16[1920,128]{1,0:T(8,128)(2,1)S(1)}, bf16[1920,128]{1,0:T(8,128)(2,1)}, u32[]{:S(2)}) copy-start(bf16[1920,128]{1,0:T(8,128)(2,1)} %get-tuple-element.40.own_ref) | copy-start | bytes 1474564
  53.2 3.1 %copy-start.6 = (bf16[16,120,128]{2,1,0:T(8,128)(2,1)}, bf16[16,120,128]{2,1,0:T(8,128)(2,1)S(1)}, u32[]{:S(2)}) copy-start(bf16[16,120,128]{2,1,0:T(8,128)(2,1)S(1)} %all-to-all-done.1) | copy-start | bytes 1474564
  53.4 9.7 %collective-permute-start.2 = (bf16[1920,128]{1,0:T(8,128)(2,1)S(1)}, bf16[1920,128]{1,0:T(8,128)(2,1)S(1)}, u32[]{:S(2)}, u32[]{:S(2)}) collective-permute-start(bf16[1920,128]{1,0:T(8,128)(2,1)S(1)} %fusion), channel_id=1, source_target_pairs={{0,4},{4,0},{8,12},{12,8},{16,20},{20,16},{24,28},{28,24},{32,36},... | collective-permute-start | bytes 1474568 | tf_op jit(solution)/shard_map/ppermute | solution.py:582
  62.7 7.4 %collective-permute-start.3 = (bf16[1920,128]{1,0:T(8,128)(2,1)}, bf16[1920,128]{1,0:T(8,128)(2,1)S(1)}, u32[]{:S(2)}, u32[]{:S(2)}) collective-permute-start(bf16[1920,128]{1,0:T(8,128)(2,1)} %get-tuple-element.51), channel_id=1, source_target_pairs={{0,4},{4,0},{8,12},{12,8},{16,20},{20,16},{24,28},{28,24},{32,36},... | collective-permute-start | bytes 1474568 | tf_op jit(solution)/shard_map/ppermute | solution.py:582
  63.1 0.8 copy-start.8
  70.1 14.5 %copy-start.4 = (bf16[1920,128]{1,0:T(8,128)(2,1)}, bf16[1920,128]{1,0:T(8,128)(2,1)S(1)}, u32[]{:S(2)}) copy-start(bf16[1920,128]{1,0:T(8,128)(2,1)S(1)} %collective-permute-done.3.other_ref.other_hbm) | copy-start | bytes 1474564
  70.1 1.2 copy-start.2
  72.3 14.3 %all-to-all-start.2 = ((bf16[16,120,128]{2,1,0:T(8,128)(2,1)}), bf16[16,120,128]{2,1,0:T(8,128)(2,1)S(1)}, u32[]{:S(2)}, u32[]{:S(2)}) async-start(bf16[16,120,128]{2,1,0:T(8,128)(2,1)} %pair_sum.3), calls=%async_computation.2 | async-start | bytes 983040 | tf_op jit(solution)/shard_map/all_to_all | solution.py:588
  75.8 46.5 %collective-permute-start.6 = (bf16[256,3072]{1,0:T(8,128)(2,1)}, bf16[256,3072]{1,0:T(8,128)(2,1)}, u32[]{:S(2)}, u32[]{:S(2)}) collective-permute-start(bf16[256,3072]{1,0:T(8,128)(2,1)} %get-tuple-element.68), channel_id=1, source_target_pairs={{3,0},{0,1},{1,2},{2,3},{7,4},{4,5},{5,6},{6,7},{11,8},{8,9},{9,10... | collective-permute-start | bytes 4718600 | tf_op jit(solution)/shard_map/ppermute | solution.py:614
  87.4 14.7 %all-to-all-start.3 = ((bf16[16,120,128]{2,1,0:T(8,128)(2,1)}), bf16[16,120,128]{2,1,0:T(8,128)(2,1)S(1)}, u32[]{:S(2)}, u32[]{:S(2)}) async-start(bf16[16,120,128]{2,1,0:T(8,128)(2,1)} %chip_sums.3), calls=%async_computation.3 | async-start | bytes 983040 | tf_op jit(solution)/shard_map/all_to_all | solution.py:588
  92.0 10.1 %copy-start.3 = (bf16[1920,128]{1,0:T(8,128)(2,1)S(1)}, bf16[1920,128]{1,0:T(8,128)(2,1)}, u32[]{:S(2)}) copy-start(bf16[1920,128]{1,0:T(8,128)(2,1)} %get-tuple-element.50.own_ref) | copy-start | bytes 1474564
  102.1 3.8 %copy-start.7 = (bf16[16,120,128]{2,1,0:T(8,128)(2,1)}, bf16[16,120,128]{2,1,0:T(8,128)(2,1)S(1)}, u32[]{:S(2)}) copy-start(bf16[16,120,128]{2,1,0:T(8,128)(2,1)S(1)} %all-to-all-done.3) | copy-start | bytes 1474564
  102.3 3.6 %collective-permute-start.4 = (bf16[1920,128]{1,0:T(8,128)(2,1)S(1)}, bf16[1920,128]{1,0:T(8,128)(2,1)S(1)}, u32[]{:S(2)}, u32[]{:S(2)}) collective-permute-start(bf16[1920,128]{1,0:T(8,128)(2,1)S(1)} %fusion.1), channel_id=1, source_target_pairs={{0,4},{4,0},{8,12},{12,8},{16,20},{20,16},{24,28},{28,24},{32,36},... | collective-permute-start | bytes 1474568 | tf_op jit(solution)/shard_map/ppermute | solution.py:582
  115.9 6.4 %collective-permute-start.5 = (f32[8,3072]{1,0:T(8,128)}, f32[8,3072]{1,0:T(8,128)S(1)}, u32[]{:S(2)}, u32[]{:S(2)}) collective-permute-start(f32[8,3072]{1,0:T(8,128)} %get-tuple-element.67), channel_id=1, source_target_pairs={{4,0},{8,4},{12,8},{16,12},{20,16},{24,20},{28,24},{32,28},{36,32}... | collective-permute-start | bytes 294920 | tf_op jit(solution)/shard_map/ppermute | solution.py:609
  118.2 11.4 %collective-permute-start.7 = (bf16[64,3072]{1,0:T(8,128)(2,1)}, bf16[64,3072]{1,0:T(8,128)(2,1)S(1)}, u32[]{:S(2)}, u32[]{:S(2)}) collective-permute-start(bf16[64,3072]{1,0:T(8,128)(2,1)} %get-tuple-element.70), channel_id=1, source_target_pairs={{1,0},{2,1},{3,2},{0,3},{5,4},{6,5},{7,6},{4,7},{9,8},{10,9},{11,1... | collective-permute-start | bytes 1179656 | tf_op jit(solution)/shard_map/ppermute | solution.py:614
  119.9 18.1 %collective-permute-start.8 = (bf16[64,3072]{1,0:T(8,128)(2,1)}, bf16[64,3072]{1,0:T(8,128)(2,1)S(1)}, u32[]{:S(2)}, u32[]{:S(2)}) collective-permute-start(bf16[64,3072]{1,0:T(8,128)(2,1)} %get-tuple-element.71), channel_id=1, source_target_pairs={{1,0},{2,1},{3,2},{0,3},{5,4},{6,5},{7,6},{4,7},{9,8},{10,9},{11,1... | collective-permute-start | bytes 1179656 | tf_op jit(solution)/shard_map/ppermute | solution.py:614
  121.2 25.3 %collective-permute-start.9 = (bf16[64,3072]{1,0:T(8,128)(2,1)}, bf16[64,3072]{1,0:T(8,128)(2,1)S(1)}, u32[]{:S(2)}, u32[]{:S(2)}) collective-permute-start(bf16[64,3072]{1,0:T(8,128)(2,1)} %get-tuple-element.72), channel_id=1, source_target_pairs={{1,0},{2,1},{3,2},{0,3},{5,4},{6,5},{7,6},{4,7},{9,8},{10,9},{11,1... | collective-permute-start | bytes 1179656 | tf_op jit(solution)/shard_map/ppermute | solution.py:614
  126.3 28.3 %collective-permute-start.10 = (bf16[64,3072]{1,0:T(8,128)(2,1)}, bf16[64,3072]{1,0:T(8,128)(2,1)S(1)}, u32[]{:S(2)}, u32[]{:S(2)}) collective-permute-start(bf16[64,3072]{1,0:T(8,128)(2,1)} %get-tuple-element.73), channel_id=1, source_target_pairs={{1,0},{2,1},{3,2},{0,3},{5,4},{6,5},{7,6},{4,7},{9,8},{10,9},{11,1... | collective-permute-start | bytes 1179656 | tf_op jit(solution)/shard_map/ppermute | solution.py:614
  (3 other events, 2.0 us)
